TPU v7x, 512 devices: a whole 4x8x8 slice. The times are simulated.
512 devices in a mesh: cfg: 2 (over x_hi), seq: 16 (over y, core), req: 16 (over x_lo, z).
Axes of the slice: x: 4 (x_hi: 2, x_lo: 2; x = x_hi * 2 + x_lo), y: 8, z: 8, core: 2. Of those that a mesh axis runs over, the one named last changes fastest.
Arguments:
- qkv: bfloat16 [2, 3, 16, 1024, 2048], P('cfg', None, 'req', 'seq'), may hold values from -4.5 to 4.5
- residual: bfloat16 [2, 16, 1024, 3072], P('cfg', 'req', 'seq'), may hold values from -6 to 6
- out_weight: bfloat16 [2048, 3072], P('req', 'seq'), may hold values from -0.5 to 0.5
- final_weight: bfloat16 [3072, 64], replicated, may hold values from -0.109375 to 0.109375
- modulation: float32 [2, 3, 3072], P('cfg'), may hold values from -3 to 3
- frames: int32 [16, 8], P('req'), may hold values from 33 to 129, as said below
- timestep: int32 [1], replicated, may hold values from 0 to 49
- noisy: float32 [16, 1024, 64], P('req', 'seq', 'cfg'), may hold values from -6 to 6
Outputs:
- clean_estimate: float32 [16, 1024, 64], P('req', 'seq', 'cfg')
Inputs may be any that keep to these rules, and one draw needn't show every extreme that they name: Each value is 4 n + 1. In every group one request has 129 frames and, where a group holds three or more requests, another has 33.
All inputs are finite; a program needn't handle non-finite values.
Results may differ from a plain program's by a relative error of at most 0.008.
Values may be sent and summed in bfloat16 or wider, within the bound.
No kernel may reach another device: no remote copies, remote signals or barrier semaphores. Data moves between devices by JAX's collectives and lax.ppermute only.
A program may use at most 64 MiB of HBM per device.

v0:
```python
import jax
import jax.numpy as jnp
from jax import lax
from jax.sharding import PartitionSpec as P

HD = 128
STEPS = 50
FRAME_TOK = 2


negative_fill = -1e30
guide_scale = 6.0
shift_value = 7.0
norm_eps = 1e-06


def from_partner(array, axis, bit):
    return lax.ppermute(array, axis, [(i, i ^ 1 << bit) for i in range(lax.axis_size(axis))])


def shards(qkv, residual, out_weight, final_weight, modulation, frames, timestep, noisy):
    own_rows = qkv[0, :, 0]
    head_major = lax.all_to_all(own_rows, "seq", split_axis=2, concat_axis=1, tiled=True)
    group_rows = head_major.shape[1]
    width_dev = head_major.shape[2]
    count_heads = width_dev // HD
    block_rows = min(512, group_rows)
    scale_factor = HD ** (-0.5)
    query_all = head_major[0].reshape(group_rows, count_heads, HD)
    key_all = head_major[1].reshape(group_rows, count_heads, HD)
    value_all = head_major[2].reshape(group_rows, count_heads, HD)
    lengths = ((frames[0] - 1) // 4 + 1) * FRAME_TOK
    span_ends = jnp.cumsum(lengths)
    positions = jnp.arange(group_rows, dtype=jnp.int32)
    segment_of = jnp.sum((positions[:, None] >= span_ends[None, :]).astype(jnp.int32), axis=1)

    def query_block(block_index):
        first_row = block_index * block_rows
        query_block_rows = lax.dynamic_slice_in_dim(query_all, first_row, block_rows, 0)
        query_ids = lax.dynamic_slice_in_dim(segment_of, first_row, block_rows, 0)
        lower_block = jnp.int32(0)
        upper_block = jnp.int32(group_rows // block_rows)

        def key_step(key_index, state_now):
            running, denominator, numerator = state_now
            start_key = key_index * block_rows
            key_block_rows = lax.dynamic_slice_in_dim(key_all, start_key, block_rows, 0)
            value_block_rows = lax.dynamic_slice_in_dim(value_all, start_key, block_rows, 0)
            key_ids = lax.dynamic_slice_in_dim(segment_of, start_key, block_rows, 0)
            scores = (
                jnp.einsum(
                    "qhd,khd->hqk",
                    query_block_rows,
                    key_block_rows,
                    preferred_element_type=jnp.float32,
                )
                * scale_factor
            )
            visible = query_ids[None, :, None] == key_ids[None, None, :]
            scores = jnp.where(visible, scores, negative_fill)
            newest = jnp.maximum(running, jnp.max(scores, axis=2))
            factor = jnp.exp(running - newest)
            weights = jnp.exp(scores - newest[:, :, None])
            denominator = denominator * factor + jnp.sum(weights, axis=2)
            numerator = numerator * factor[:, :, None] + jnp.einsum(
                "hqk,khd->hqd",
                weights.astype(jnp.bfloat16),
                value_block_rows,
                preferred_element_type=jnp.float32,
            )
            return (newest, denominator, numerator)

        initial = (
            jnp.full((count_heads, block_rows), negative_fill, jnp.float32),
            jnp.zeros((count_heads, block_rows), jnp.float32),
            jnp.zeros((count_heads, block_rows, HD), jnp.float32),
        )
        running, denominator, numerator = lax.fori_loop(lower_block, upper_block, key_step, initial)
        result = numerator / denominator[:, :, None]
        return result.transpose(1, 0, 2).reshape(block_rows, width_dev).astype(jnp.bfloat16)

    block_results = lax.map(query_block, jnp.arange(group_rows // block_rows, dtype=jnp.int32))
    head_results = block_results.reshape(group_rows, width_dev)
    weight_full = lax.all_gather(out_weight, "req", axis=0, tiled=True)
    row_results = lax.all_to_all(head_results, "seq", split_axis=0, concat_axis=1, tiled=True)
    attn_out = jnp.dot(
        row_results,
        lax.all_gather(weight_full, "seq", axis=1, tiled=True),
        preferred_element_type=jnp.float32,
    ).astype(jnp.bfloat16)
    modulation_row = modulation[0]
    stream = residual[0, 0].astype(jnp.float32) + modulation_row[0] * attn_out.astype(jnp.float32)
    row_mean = jnp.mean(stream, axis=1, keepdims=True)
    centered = stream - row_mean
    row_var = jnp.mean(centered * centered, axis=1, keepdims=True)
    normed = (
        centered / jnp.sqrt(row_var + norm_eps) * (1.0 + modulation_row[2]) + modulation_row[1]
    ).astype(jnp.bfloat16)
    prediction = jnp.dot(normed, final_weight, preferred_element_type=jnp.float32)
    branch = lax.axis_index("cfg")
    partner_pred = from_partner(prediction, "cfg", 0)
    conditional = jnp.where(branch == 0, prediction, partner_pred)
    unconditional = jnp.where(branch == 0, partner_pred, prediction)
    guided = unconditional + guide_scale * (conditional - unconditional)
    half_width = noisy.shape[2]
    guided_half = lax.dynamic_slice_in_dim(guided, branch * half_width, half_width, 1)
    progress = 1.0 - timestep[0].astype(jnp.float32) / STEPS
    sigma_now = shift_value * progress / (1.0 + (shift_value - 1.0) * progress)
    clean_estimate = noisy[0] - sigma_now * guided_half
    return clean_estimate[None]


def solution(mesh):
    return jax.shard_map(
        shards,
        mesh=mesh,
        in_specs=(
            P("cfg", None, "req", "seq", None),
            P("cfg", "req", "seq", None),
            P("req", "seq"),
            P(),
            P("cfg", None, None),
            P("req", None),
            P(),
            P("req", "seq", "cfg"),
        ),
        out_specs=P("req", "seq", "cfg"),
        check_vma=False,
    )
```

profile of v0, /device:TPU:1, one launch (start us, length us, event | category | flops | bytes accessed | tf_op | source)
XLA Modules:
  0.0 174.1 jit_solution(8026918071041368157)
XLA Ops:
  6.5 40.4 %all_gather.6 = bf16[2048,192]{0,1:T(8,128)(2,1)} all-gather(bf16[128,192]{0,1:T(8,128)(2,1)} %param.14), channel_id=1, replica_groups=mesh['cfg'=2,'seq'=16,'req'=16] {'req'}, dimensions={0}, use_global_device_ids=true | all-gather | bytes 835584 | tf_op jit(solution)/shard_map/all_gather | solution.py:84
  47.0 4.0 %copy.21 = bf16[1,3,1,64,2048]{3,1,4,2,0:T(4,128)(2,1)} copy(bf16[1,3,1,64,2048]{4,3,2,1,0:T(8,128)(2,1)} %param.12) | data formatting | bytes 1572864 | tf_op args[0]
  51.0 2.0 %bitcast_bitcast_fusion = bf16[2048,3,64]{2,1,0:T(4,128)(2,1)S(1)} fusion(bf16[1,3,1,64,2048]{3,1,4,2,0:T(4,128)(2,1)} %copy.21), kind=kLoop, calls=%fused_computation.50 | loop fusion | bytes 1572864
  53.0 2.5 %reshape.137 = bf16[16,2,12288]{2,1,0:T(2,128)(2,1)} reshape(bf16[2048,3,64]{2,1,0:T(4,128)(2,1)S(1)} %bitcast_bitcast_fusion) | data formatting | bytes 1572864
  55.5 15.0 %all-to-all-start = ((bf16[16,2,12288]{2,1,0:T(2,128)(2,1)}), bf16[16,2,12288]{2,1,0:T(2,128)(2,1)S(1)}, u32[]{:S(2)}, u32[]{:S(2)}) async-start(bf16[16,2,12288]{2,1,0:T(2,128)(2,1)} %reshape.137), calls=%async_computation | async-start | bytes 1572864 | tf_op jit(solution)/shard_map/all_to_all | solution.py:23
  70.8 29.7 %all-to-all-done = bf16[16,2,12288]{2,1,0:T(2,128)(2,1)S(1)} async-done(((bf16[16,2,12288]{2,1,0:T(2,128)(2,1)}), bf16[16,2,12288]{2,1,0:T(2,128)(2,1)S(1)}, u32[]{:S(2)}, u32[]{:S(2)}) %all-to-all-start) | async-done | bytes 786464 | tf_op jit(solution)/shard_map/all_to_all | solution.py:23
  100.5 1.3 reshape.138
  101.8 1.2 copy.27
  103.4 8.8 %while.26 = (s32[]{:T(128)}, bf16[2,512,128]{2,1,0:T(8,128)(2,1)}, s32[2]{0:T(128)S(1)}, bf16[1024,1,128]{2,0,1:T(8,128)(2,1)S(1)}, s32[1024]{0:T(1024)S(1)}, /*...) while((s32[]{:T(128)}, bf16[2,512,128]{2,1,0:T(8,128)(2,1)}, ...), condition=%wide.region_7.8_spmd, body=%wide.region_2.7_spmd.sunk | while | flops 136645120 | bytes 4766722 | solution.py:82
  103.4 0.7 dynamic_slice.48
  104.9 2.1 %while.27 = (s32[]{:T(128)}, f32[1,512]{1,0:T(1,128)S(1)}, f32[1,512]{1,0:T(1,128)S(1)}, f32[1,512,128]{2,1,0:T(8,128)S(1)}, s32[512]{0:T(512)S(1)}, /*index=5*/...) while((s32[]{:T(128)}, f32[1,512]{1,0:T(1,128)S(1)}, ...), condition=%wide.region_6.6_spmd.clone, body=%wide.region_3.5_spmd.clone.sunk | while | flops 136514048 | bytes 4104387 | solution.py:78
  107.0 0.8 fusion.39
  107.8 0.7 dynamic_slice.48
  109.3 2.1 %while.27 = (s32[]{:T(128)}, f32[1,512]{1,0:T(1,128)S(1)}, f32[1,512]{1,0:T(1,128)S(1)}, f32[1,512,128]{2,1,0:T(8,128)S(1)}, s32[512]{0:T(512)S(1)}, /*index=5*/...) while((s32[]{:T(128)}, f32[1,512]{1,0:T(1,128)S(1)}, ...), condition=%wide.region_6.6_spmd.clone, body=%wide.region_3.5_spmd.clone.sunk | while | flops 136514048 | bytes 4104387 | solution.py:78
  109.9 0.4 fusion.46
  111.4 0.8 fusion.39
  112.2 4.7 %all-to-all-start.1 = ((bf16[16,64,128]{2,1,0:T(8,128)(2,1)}), bf16[16,64,128]{2,1,0:T(8,128)(2,1)S(1)}, u32[]{:S(2)}, u32[]{:S(2)}) async-start(bf16[16,64,128]{2,1,0:T(8,128)(2,1)} %bitcast.14), calls=%async_computation.1 | async-start | bytes 524288 | tf_op jit(solution)/shard_map/all_to_all | solution.py:85
  116.9 14.5 %all-to-all-done.1 = bf16[16,64,128]{2,1,0:T(8,128)(2,1)S(1)} async-done(((bf16[16,64,128]{2,1,0:T(8,128)(2,1)}), bf16[16,64,128]{2,1,0:T(8,128)(2,1)S(1)}, u32[]{:S(2)}, u32[]{:S(2)}) %all-to-all-start.1) | async-done | bytes 262176 | tf_op jit(solution)/shard_map/all_to_all | solution.py:85
  131.3 19.8 %all-gather.2.cloned.1.call-done = bf16[2048,3072]{0,1:T(8,128)(2,1)} async-done(((bf16[2048,192]{0,1:T(8,128)(2,1)}), bf16[2048,3072]{0,1:T(8,128)(2,1)}) %all-gather.2.cloned.1.call-update) | async-done | bytes 12582928 | tf_op jit(solution)/shard_map/all_gather | solution.py:88
  151.2 8.6 %fusion.27 = (f32[64]{0:T(128)S(1)}, f32[64,3072]{1,0:T(8,128)S(1)}) fusion(bf16[2048,3072]{0,1:T(8,128)(2,1)} %all-gather.2.cloned.1.call-done, f32[3072]{0:T(1024)S(1)} %bitcast.97, bf16[1,1,64,3072]{3,2,1,0:T(8,128)(2,1)S(1)} %copy-done.1, bf16[16,64,128]{2,1,0:T(8,128)(2,1)S(1)} %all-to-all-done.1), kind=kOutput, calls=%fused_computation.49 | convolution fusion | flops 806485952 | bytes 14037248 | tf_op jit(solution)/shard_map/dot_general | solution.py:86
  160.1 0.4 fusion.21
  160.4 4.6 %collective-permute-start = (f32[64,64]{0,1:T(8,128)S(1)}, f32[64,64]{0,1:T(8,128)S(1)}, u32[]{:S(2)}, u32[]{:S(2)}) collective-permute-start(f32[64,64]{0,1:T(8,128)S(1)} %fusion.21), channel_id=1, source_target_pairs={{0,256},{256,0},{1,257},{257,1},{2,258},{258,2},{3,259},{259,3},{4... | collective-permute-start | bytes 49160 | tf_op jit(solution)/shard_map/ppermute | solution.py:18
  165.8 0.8 collective-permute-done
  166.6 0.6 fusion.24
  (62 shorter events, 4.7 us)
Async XLA Ops:
  6.5 153.5 %copy-start = (bf16[3072,64]{0,1:T(8,128)(2,1)S(1)}, bf16[3072,64]{0,1:T(8,128)(2,1)}, u32[]{:S(2)}) copy-start(bf16[3072,64]{0,1:T(8,128)(2,1)} %param.15) | copy-start | bytes 1179652
  6.5 64.0 %copy-start.4 = (s32[1,8]{1,0:T(1,128)S(1)}, s32[1,8]{1,0:T(1,128)}, u32[]{:S(2)}) copy-start(s32[1,8]{1,0:T(1,128)} %param.17) | copy-start | bytes 100
  6.5 144.6 %all-gather.2.cloned.1.call-start = ((), (), s32[]{:S(2)}) async-start(), calls=%async_computation.2 | async-start | bytes 13369344 | tf_op jit(solution)/shard_map/all_gather | solution.py:88
  55.5 45.0 %all-to-all-start = ((bf16[16,2,12288]{2,1,0:T(2,128)(2,1)}), bf16[16,2,12288]{2,1,0:T(2,128)(2,1)S(1)}, u32[]{:S(2)}, u32[]{:S(2)}) async-start(bf16[16,2,12288]{2,1,0:T(2,128)(2,1)} %reshape.137), calls=%async_computation | async-start | bytes 1572864 | tf_op jit(solution)/shard_map/all_to_all | solution.py:23
  103.4 13.5 %copy-start.2 = (f32[1,3,3072]{2,0,1:T(1,128)S(1)}, f32[1,3,3072]{2,0,1:T(1,128)}, u32[]{:S(2)}) copy-start(f32[1,3,3072]{2,0,1:T(1,128)} %param.16) | copy-start | bytes 110596
  103.4 47.8 %copy-start.1 = (bf16[1,1,64,3072]{3,2,1,0:T(8,128)(2,1)S(1)}, bf16[1,1,64,3072]{3,2,1,0:T(8,128)(2,1)}, u32[]{:S(2)}) copy-start(bf16[1,1,64,3072]{3,2,1,0:T(8,128)(2,1)} %param.13) | copy-start | bytes 1179652
  112.2 54.4 %copy-start.3 = (f32[1,64,32]{1,2,0:T(8,128)S(1)}, f32[1,64,32]{1,2,0:T(8,128)}, u32[]{:S(2)}) copy-start(f32[1,64,32]{1,2,0:T(8,128)} %param.19) | copy-start | bytes 24580
  112.2 19.2 %all-to-all-start.1 = ((bf16[16,64,128]{2,1,0:T(8,128)(2,1)}), bf16[16,64,128]{2,1,0:T(8,128)(2,1)S(1)}, u32[]{:S(2)}, u32[]{:S(2)}) async-start(bf16[16,64,128]{2,1,0:T(8,128)(2,1)} %bitcast.14), calls=%async_computation.1 | async-start | bytes 524288 | tf_op jit(solution)/shard_map/all_to_all | solution.py:85
  160.4 6.2 %collective-permute-start = (f32[64,64]{0,1:T(8,128)S(1)}, f32[64,64]{0,1:T(8,128)S(1)}, u32[]{:S(2)}, u32[]{:S(2)}) collective-permute-start(f32[64,64]{0,1:T(8,128)S(1)} %fusion.21), channel_id=1, source_target_pairs={{0,256},{256,0},{1,257},{257,1},{2,258},{258,2},{3,259},{259,3},{4... | collective-permute-start | bytes 49160 | tf_op jit(solution)/shard_map/ppermute | solution.py:18
Sparse Core Ops, SparseCore 0:
  47.1 103.9 all-gather.1
where the time goes:
time: 175 us; the launch traced here: 174 us
  waiting for transfers between devices  64.8 us (37%)
  blocking collectives  40.4 us (23%)
  starting transfers between devices  24.3 us (14%)
  between operations  14.2 us (8%)
  local copies, waits for them, and re-layouts  13.1 us (7%)
  matrix products  11.7 us (7%)
  other arithmetic  3.69 us (2%)
    all_gather x1, blocking collectives, shards(): weight_full = lax.all_gather(out_weight, 'req', axis=0, tiled=True)  40.4 us
    all_to_all x1, waiting for transfers between devices, shards(): lax.all_to_all(own_rows, 'seq', split_axis=2, concat_axis=1, tiled=True)  29.7 us
    all_gather x1, waiting for transfers between devices, shards(): lax.all_gather(weight_full, 'seq', axis=1, tiled=True)  19.8 us
    all_to_all x1, starting transfers between devices, shards(): lax.all_to_all(own_rows, 'seq', split_axis=2, concat_axis=1, tiled=True)  15 us
    all_to_all x1, waiting for transfers between devices, shards(): lax.all_to_all(head_results, 'seq', split_axis=0, concat_axis=1, tiled=True)  14.5 us
    unnamed x14, local copies, waits for them, and re-layouts  9.78 us
    dot_general x1, matrix products, shards(): jnp.dot(row_results, lax.all_gather(weight_full, 'seq', axis=1, tiled=Tru...  8.61 us
    all_to_all x1, starting transfers between devices, shards(): lax.all_to_all(head_results, 'seq', split_axis=0, concat_axis=1, tiled=True)  4.66 us
  transfers between devices with their start and end apart: 4, of which 4 were waited for; matrix products, arithmetic and copies ran while one was open for 11% of the time, Pallas kernels for 0%

commit v1 on v0

v1 whole, which is shorter than its diff:
```python
import functools

import jax
import jax.numpy as jnp
import numpy as np
from jax import lax
from jax.experimental import pallas as pl
from jax.experimental.pallas import tpu as pltpu
from jax.sharding import Mesh, PartitionSpec as P

HD = 128
STEPS = 50
FRAME_TOK = 2
GUIDE = 6.0
SHIFT = 7.0
EPS = 1e-06
FILL = -1e30
ROWS = 1024
DEV_ROWS = 64
HALF = 1536
WIDTH = 3072
LOG2E = 1.4426950408889634

NT = (((1,), (1,)), ((), ()))
VMEM = pltpu.VMEM
SMEM = pltpu.SMEM


def spec(space):
    return pl.BlockSpec(memory_space=space)


def pack_kernel(in_ref, out_ref):
    for y in range(8):
        for k in range(2):
            head = 8 * k + y
            out_ref[2 * y + k] = in_ref[:, :, head * HD : (head + 1) * HD]


def pack(own):
    return pl.pallas_call(
        pack_kernel,
        out_shape=jax.ShapeDtypeStruct((16, 3, DEV_ROWS, HD), jnp.bfloat16),
        in_specs=[spec(VMEM)],
        out_specs=spec(VMEM),
        name="pack",
    )(own)


BLOCKS = ((0, 128, 0, 256), (128, 256, 0, 1024), (256, 512, 128, 1024), (512, 768, 128, 1024), (768, 1024, 128, 1024))


def attend_kernel(frames_ref, x_ref, out_ref):
    ends = []
    total = jnp.int32(0)
    for r in range(8):
        total = total + ((frames_ref[r] - 1) // 4 + 1) * FRAME_TOK
        ends.append(total)

    def ids(shape, dim, first):
        place = lax.broadcasted_iota(jnp.int32, shape, dim) + first
        found = jnp.zeros(shape, jnp.int32)
        for end in ends:
            found = found + (place >= end).astype(jnp.int32)
        return found

    scale = HD**-0.5 * LOG2E
    for first, last, low, high in BLOCKS:
        n, m = last - first, high - low
        q = x_ref[first // 64 : last // 64, 0].reshape(n, HD)
        k = x_ref[low // 64 : high // 64, 1].reshape(m, HD)
        v = x_ref[low // 64 : high // 64, 2].reshape(m, HD)
        scores = lax.dot_general(q, k, NT, preferred_element_type=jnp.float32)
        same = ids((n, 1), 0, first) == ids((1, m), 1, low)
        scores = jnp.where(same, scores, FILL)
        largest = jnp.max(scores, axis=1, keepdims=True)
        weights = jnp.exp2((scores - largest) * scale)
        denominator = jnp.sum(weights, axis=1, keepdims=True)
        mixed = jnp.dot(weights.astype(jnp.bfloat16), v, preferred_element_type=jnp.float32)
        result = (mixed / denominator).astype(jnp.bfloat16).reshape(n // 128, 128, HD)
        out_ref[0, first // 128 : last // 128] = result
        out_ref[1, first // 128 : last // 128] = result


def attend(frames, gathered):
    return pl.pallas_call(
        attend_kernel,
        out_shape=jax.ShapeDtypeStruct((2, 8, 128, HD), jnp.bfloat16),
        in_specs=[spec(SMEM), spec(VMEM)],
        out_specs=spec(VMEM),
        compiler_params=pltpu.CompilerParams(vmem_limit_bytes=48 * 2**20),
        cost_estimate=pl.CostEstimate(flops=540_000_000, bytes_accessed=2_000_000, transcendentals=1_000_000),
        name="attend",
    )(frames, gathered)


def project_kernel(where_ref, x_ref, w_ref, keep_ref, send_ref):
    core = where_ref[0]
    x = jnp.concatenate([x_ref[:, h].reshape(256, HD) for h in range(8)], axis=1)
    tile = 512
    for t in range(HALF // tile):
        cols = slice(t * tile, (t + 1) * tile)
        w = jnp.concatenate([w_ref[h, cols] for h in range(8)], axis=1)
        part = lax.dot_general(x, w, NT, preferred_element_type=jnp.float32)
        for b in range(2):
            low = part[b * 128 : b * 128 + 64]
            high = part[b * 128 + 64 : b * 128 + 128]
            keep_ref[b, :, cols] = jnp.where(core == 0, low, high)
            send_ref[b, :, cols] = jnp.where(core == 0, high, low).astype(jnp.bfloat16)


def project(where, x, w):
    return pl.pallas_call(
        project_kernel,
        out_shape=(
            jax.ShapeDtypeStruct((2, DEV_ROWS, HALF), jnp.float32),
            jax.ShapeDtypeStruct((2, DEV_ROWS, HALF), jnp.bfloat16),
        ),
        in_specs=[spec(SMEM), spec(VMEM), spec(VMEM)],
        out_specs=(spec(VMEM), spec(VMEM)),
        compiler_params=pltpu.CompilerParams(vmem_limit_bytes=48 * 2**20),
        cost_estimate=pl.CostEstimate(flops=810_000_000, bytes_accessed=5_000_000, transcendentals=0),
        name="project",
    )(where, x, w)


def norm_kernel(where_ref, keep_ref, came_ref, own_ref, other_ref, mod_ref, r_ref, out_ref, send_ref):
    me = where_ref[1]
    lane = lax.broadcasted_iota(jnp.int32, (DEV_ROWS, 128), 1)
    both = jnp.zeros((DEV_ROWS, 256), jnp.float32)
    extra = jnp.zeros((DEV_ROWS, 128), jnp.float32)
    for b in range(2):
        residual = jnp.where(me == b, own_ref[...].astype(jnp.float32), other_ref[...].astype(jnp.float32))
        attn_out = (keep_ref[b] + came_ref[b].astype(jnp.float32)).astype(jnp.bfloat16).astype(jnp.float32)
        stream = residual + mod_ref[b, 0:1] * attn_out
        mean = jnp.mean(stream, axis=1, keepdims=True)
        centered = stream - mean
        spread = jnp.sum(centered * centered, axis=1, keepdims=True)
        scaled = (centered * (1.0 + mod_ref[b, 2:3])).astype(jnp.bfloat16)
        both = both + lax.dot_general(scaled, r_ref[b], NT, preferred_element_type=jnp.float32)
        extra = jnp.where(lane == 64 + b, mean, extra)
        extra = jnp.where(lane == 66 + b, spread, extra)
    out_ref[...] = both[:, :128] + extra
    send_ref[...] = both[:, 128:] + extra


def norm(where, keep, came, own, other, mod, r):
    return pl.pallas_call(
        norm_kernel,
        out_shape=(
            jax.ShapeDtypeStruct((DEV_ROWS, 128), jnp.float32),
            jax.ShapeDtypeStruct((DEV_ROWS, 128), jnp.float32),
        ),
        in_specs=[spec(SMEM)] + [spec(VMEM)] * 6,
        out_specs=(spec(VMEM), spec(VMEM)),
        compiler_params=pltpu.CompilerParams(vmem_limit_bytes=48 * 2**20),
        name="norm",
    )(where, keep, came, own, other, mod, r)


def flip(array, axis):
    return lax.ppermute(array, axis, [(0, 1), (1, 0)])


def spread_pairs():
    pairs = []
    for c in range(2):
        for y in range(8):
            for k in range(2):
                for l in range(2):
                    source = ((c * 8 + y) * 2 + k) * 2 + l
                    target = (((y // 4) * 8 + (y % 4) * 2 + k) * 2 + l) * 2 + c
                    pairs.append((source, target))
    return pairs


def gather_weight(out_weight):
    block = lax.ppermute(out_weight.T, ("c", "y", "k", "l"), spread_pairs())
    unit = lax.all_gather(block, "y", axis=0, tiled=True)
    return lax.all_gather(unit, "z", axis=0, tiled=False)


def shards(qkv, residual, out_weight, final_weight, modulation, frames, timestep, noisy):
    branch = lax.axis_index("c")
    core = lax.axis_index("k")
    where = jnp.stack([core, branch]).astype(jnp.int32)

    packed = pack(qkv[0, :, 0])
    gathered = lax.all_to_all(packed, ("y", "k"), 0, 0, tiled=True)

    weight = gather_weight(out_weight)

    here = lax.dynamic_slice_in_dim(residual[0, 0], branch * HALF, HALF, 1)
    there = lax.dynamic_slice_in_dim(residual[0, 0], (1 - branch) * HALF, HALF, 1)
    other = flip(there, "c")
    mod_other = flip(modulation[0], "c")
    mod_all = jnp.where(branch == 0, jnp.stack([modulation[0], mod_other]), jnp.stack([mod_other, modulation[0]]))
    mod_half = lax.dynamic_slice_in_dim(mod_all, branch * HALF, HALF, 2)

    fw = final_weight.T
    fw_half = lax.dynamic_slice_in_dim(fw, branch * HALF, HALF, 1)
    fw_mine = lax.dynamic_slice_in_dim(fw_half, branch * 32, 32, 0)
    fw_partner = lax.dynamic_slice_in_dim(fw_half, (1 - branch) * 32, 32, 0)
    empty = jnp.zeros((32, HALF), jnp.bfloat16)
    r = jnp.stack(
        [
            jnp.concatenate([fw_mine, empty, empty, empty, fw_partner, empty, empty, empty]),
            jnp.concatenate([empty, fw_mine, empty, empty, empty, fw_partner, empty, empty]),
        ]
    )
    fw_channels = lax.dynamic_slice_in_dim(fw, branch * 32, 32, 0).astype(jnp.float32)
    scaled_sums = jnp.sum((1.0 + mod_all[:, 2])[:, None, :].reshape(2, 1, 2, HALF) * fw_channels.reshape(1, 32, 2, HALF), axis=3)
    tilt = scaled_sums[:, :, 0] - scaled_sums[:, :, 1]
    offset = jnp.sum(mod_all[:, 1][:, None, :] * fw_channels[None], axis=2)

    heads = attend(frames[0], gathered)
    rows = lax.all_to_all(heads.reshape(16, 128, HD), ("c", "y"), 0, 0, tiled=True)
    keep, send = project(where, rows.reshape(2, 8, 128, HD), weight)
    came = flip(send, "k")
    own_sums, partner_sums = norm(where, keep, came, here, other, mod_half, r)
    came_sums = flip(partner_sums, "c")

    prediction = []
    for b in range(2):
        first_mean = jnp.where(branch == 0, own_sums[:, 64 + b], came_sums[:, 64 + b])
        second_mean = jnp.where(branch == 0, came_sums[:, 64 + b], own_sums[:, 64 + b])
        gap = 0.5 * (first_mean - second_mean)
        var = (own_sums[:, 66 + b] + came_sums[:, 66 + b] + WIDTH * gap * gap) / WIDTH
        part = (own_sums + came_sums)[:, 32 * b : 32 * b + 32]
        prediction.append((part + gap[:, None] * tilt[b]) / jnp.sqrt(var + EPS)[:, None] + offset[b])
    guided = prediction[1] + GUIDE * (prediction[0] - prediction[1])
    progress = 1.0 - timestep[0].astype(jnp.float32) / STEPS
    sigma = SHIFT * progress / (1.0 + (SHIFT - 1.0) * progress)
    return noisy - sigma * guided[None]


def solution(mesh):
    fine = Mesh(mesh.devices.reshape(2, 8, 2, 2, 8), ("c", "y", "k", "l", "z"))
    seq, req = ("y", "k"), ("l", "z")
    return jax.shard_map(
        shards,
        mesh=fine,
        in_specs=(
            P("c", None, req, seq, None),
            P("c", req, seq, None),
            P(req, seq),
            P(),
            P("c", None, None),
            P(req, None),
            P(),
            P(req, seq, "c"),
        ),
        out_specs=P(req, seq, "c"),
        check_vma=False,
    )
```

time: 175 us -> 127 us (0.73)
  waiting for transfers between devices: 64.8 us -> 30.5 us
  blocking collectives: 40.4 us -> 27.1 us
  starting transfers between devices: 24.3 us -> 36.9 us
  matrix products: 11.7 us -> 0 us
  Pallas kernels: 0 us -> 8.73 us
  local copies, waits for them, and re-layouts: 13.1 us -> 5.43 us
    all_to_all x2, waiting for transfers between devices: 44.2 us -> 24 us  [the longest x1 12 us: shards(): lax.all_to_all(heads.reshape(16, 128, HD), ('c', 'y'), 0, 0, tiled=True)]
    all_gather x1, waiting for transfers between devices: 19.8 us -> 0.01 us  [gather_weight(): return lax.all_gather(unit, 'z', axis=0, tiled=False)]
    ppermute x1 -> x5, starting transfers between devices: 4.61 us -> 19.7 us  [the longest x4 15.2 us: flip(): return lax.ppermute(array, axis, [(0, 1), (1, 0)])]
    all_gather x1, blocking collectives: 40.4 us -> 27.1 us  [gather_weight(): unit = lax.all_gather(block, 'y', axis=0, tiled=True)]
    dot_general x10 -> x0, matrix products: 11.7 us -> none  [the longest x1 8.61 us: shards(): jnp.dot(row_results, lax.all_gather(weight_full, 'seq', axis=1, tiled=Tru...]
    pallas_call x0 -> x4, Pallas kernels: none -> 8.73 us  [the longest x1 3.62 us: attend(): pl.pallas_call(attend_kernel, out_shape=jax.ShapeDtypeStruct((2, 8, 128,...]
    unnamed x14 -> x19, local copies, waits for them, and re-layouts: 9.78 us -> 2.9 us
    ppermute x1 -> x5, waiting for transfers between devices: 0.84 us -> 6.52 us  [the longest x4 4.64 us: flip(): return lax.ppermute(array, axis, [(0, 1), (1, 0)])]
  transfers between devices with their start and end apart: 4 -> 8, of which waited for: 4 -> 5; matrix products, arithmetic and copies ran while one was open for 11% -> 4% of each run, Pallas kernels for 0% -> 6%
where the time goes in v1:
time: 127 us; the launch traced here: 126 us
  starting transfers between devices  36.9 us (29%)
  waiting for transfers between devices  30.5 us (24%)
  blocking collectives  27.1 us (21%)
  between operations  14.3 us (11%)
  Pallas kernels  8.73 us (7%)
  local copies, waits for them, and re-layouts  5.43 us (4%)
  other arithmetic  2.82 us (2%)
    all_gather x1, blocking collectives, gather_weight(): unit = lax.all_gather(block, 'y', axis=0, tiled=True)  27.1 us
    ppermute x4, starting transfers between devices, flip(): return lax.ppermute(array, axis, [(0, 1), (1, 0)])  15.2 us
    all_to_all x1, waiting for transfers between devices, shards(): lax.all_to_all(heads.reshape(16, 128, HD), ('c', 'y'), 0, 0, tiled=True)  12 us
    all_to_all x1, waiting for transfers between devices, shards(): gathered = lax.all_to_all(packed, ('y', 'k'), 0, 0, tiled=True)  12 us
    all_to_all x1, starting transfers between devices, shards(): gathered = lax.all_to_all(packed, ('y', 'k'), 0, 0, tiled=True)  10.6 us
    all_to_all x1, starting transfers between devices, shards(): lax.all_to_all(heads.reshape(16, 128, HD), ('c', 'y'), 0, 0, tiled=True)  6.53 us
    ppermute x4, waiting for transfers between devices, flip(): return lax.ppermute(array, axis, [(0, 1), (1, 0)])  4.64 us
    ppermute x1, starting transfers between devices, gather_weight(): block = lax.ppermute(out_weight.T, ('c', 'y', 'k', 'l'), spread_pairs())  4.58 us
  transfers between devices with their start and end apart: 8, of which 5 were waited for; matrix products, arithmetic and copies ran while one was open for 4% of the time, Pallas kernels for 6%

profile of v1, /device:TPU:1, one launch (start us, length us, event | category | flops | bytes accessed | tf_op | source)
XLA Modules:
  0.0 125.9 jit_solution(17795466482934780381)
XLA Ops:
  6.5 4.6 %collective-permute-start = (bf16[192,128]{1,0:T(8,128)(2,1)}, bf16[192,128]{1,0:T(8,128)(2,1)S(1)}, u32[]{:S(2)}, u32[]{:S(2)}) collective-permute-start(bf16[192,128]{1,0:T(8,128)(2,1)} %bitcast.52), channel_id=1, source_target_pairs={{0,0},{8,16},{16,32},{24,48},{32,64},{40,80},{48,96},{56,112},{64,... | collective-permute-start | bytes 147464 | tf_op jit(solution)/shard_map/ppermute | solution.py:178
  11.1 1.9 %collective-permute-done = bf16[192,128]{1,0:T(8,128)(2,1)S(1)} collective-permute-done((bf16[192,128]{1,0:T(8,128)(2,1)}, bf16[192,128]{1,0:T(8,128)(2,1)S(1)}, u32[]{:S(2)}, u32[]{:S(2)}) %collective-permute-start) | collective-permute-done | bytes 49184 | tf_op jit(solution)/shard_map/ppermute | solution.py:178
  13.0 27.1 %all_gather.9 = bf16[1536,128]{1,0:T(8,128)(2,1)} all-gather(bf16[192,128]{1,0:T(8,128)(2,1)S(1)} %collective-permute-done), channel_id=1, replica_groups=mesh['c'=2,'y'=8,'k'=2,'l'=2,'z'=8] {'y'}, dimensions={0}, use_global_device_ids=true | all-gather | bytes 442368 | tf_op jit(solution)/shard_map/all_gather | solution.py:179
  40.2 2.2 %pack.1 = bf16[16,3,64,128]{3,2,1,0:T(8,128)(2,1)} custom-call(bf16[3,64,2048]{2,1,0:T(8,128)(2,1)} %bitcast.50), custom_call_target="tpu_custom_call" | custom-call | tf_op jit(solution)/shard_map/pack/pallas_call | solution.py:41
  42.4 10.6 %all-to-all-start = ((bf16[16,3,64,128]{3,2,1,0:T(8,128)(2,1)}), bf16[16,3,64,128]{3,2,1,0:T(8,128)(2,1)S(1)}, u32[]{:S(2)}, u32[]{:S(2)}) async-start(bf16[16,3,64,128]{3,2,1,0:T(8,128)(2,1)} %pack.1), calls=%async_computation | async-start | bytes 1572864 | tf_op jit(solution)/shard_map/all_to_all | solution.py:189
  53.0 0.7 dynamic-slice_bitcast_fusion
  53.7 6.0 %collective-permute-start.2 = (bf16[64,1536]{1,0:T(8,128)(2,1)}, bf16[64,1536]{1,0:T(8,128)(2,1)S(1)}, u32[]{:S(2)}, u32[]{:S(2)}) collective-permute-start(bf16[64,1536]{1,0:T(8,128)(2,1)} %get-tuple-element.23), channel_id=1, source_target_pairs={{0,256},{256,0},{1,257},{257,1},{2,258},{258,2},{3,259},{259,3},{4... | collective-permute-start | bytes 589832 | tf_op jit(solution)/shard_map/ppermute | solution.py:162
  59.7 0.6 copy.36
  60.3 1.9 %collective-permute-start.3 = (f32[3,3072]{1,0:T(4,128)}, f32[3,3072]{1,0:T(4,128)}, u32[]{:S(2)}, u32[]{:S(2)}) collective-permute-start(f32[3,3072]{1,0:T(4,128)} %bitcast.39.clone.2), channel_id=1, source_target_pairs={{0,256},{256,0},{1,257},{257,1},{2,258},{258,2},{3,259},{259,3},{4... | collective-permute-start | bytes 110600 | tf_op jit(solution)/shard_map/ppermute | solution.py:162
  62.8 0.8 dynamic-slice_convert_fusion
  63.7 12.0 %all-to-all-done.x_ref = bf16[16,3,64,128]{3,2,1,0:T(8,128)(2,1)S(1)} async-done(((bf16[16,3,64,128]{3,2,1,0:T(8,128)(2,1)}), bf16[16,3,64,128]{3,2,1,0:T(8,128)(2,1)S(1)}, u32[]{:S(2)}, u32[]{:S(2)}) %all-to-all-start) | async-done | bytes 786464 | tf_op jit(solution)/shard_map/all_to_all | solution.py:189
  75.7 3.6 %attend.1 = bf16[2,8,128,128]{3,2,1,0:T(8,128)(2,1)} custom-call(s32[8]{0:T(128)S(1)} %bitcast.46, bf16[16,3,64,128]{3,2,1,0:T(8,128)(2,1)S(1)} %all-to-all-done.x_ref), custom_call_target="tpu_custom_call" | custom-call | flops 540000000 | bytes 2000000 | tf_op jit(solution)/shard_map/attend/pallas_call | solution.py:86
  79.3 6.5 %all-to-all-start.1 = ((bf16[16,128,128]{2,1,0:T(8,128)(2,1)}), bf16[16,128,128]{2,1,0:T(8,128)(2,1)S(1)}, u32[]{:S(2)}, u32[]{:S(2)}) async-start(bf16[16,128,128]{2,1,0:T(8,128)(2,1)} %bitcast.5), calls=%async_computation.1 | async-start | bytes 1048576 | tf_op jit(solution)/shard_map/all_to_all | solution.py:217
  86.0 1.0 copy.34
  87.7 0.9 maximum_select_fusion
  89.0 12.0 %all-to-all-done.1 = bf16[16,128,128]{2,1,0:T(8,128)(2,1)S(1)} async-done(((bf16[16,128,128]{2,1,0:T(8,128)(2,1)}), bf16[16,128,128]{2,1,0:T(8,128)(2,1)S(1)}, u32[]{:S(2)}, u32[]{:S(2)}) %all-to-all-start.1) | async-done | bytes 524320 | tf_op jit(solution)/shard_map/all_to_all | solution.py:217
  101.0 1.9 %copy-done = bf16[12288,128]{1,0:T(8,128)(2,1)S(1)} copy-done((bf16[12288,128]{1,0:T(8,128)(2,1)S(1)}, bf16[12288,128]{1,0:T(8,128)(2,1)}, u32[]{:S(2)}) %copy-start) | copy-done | bytes 3145752
  102.9 1.6 %project.1 = (f32[2,64,1536]{2,1,0:T(8,128)S(1)}, bf16[2,64,1536]{2,1,0:T(8,128)(2,1)S(1)}) custom-call(s32[2]{0:T(128)S(1)} %pad_add_fusion.where_ref, bf16[2,8,128,128]{3,2,1,0:T(8,128)(2,1)S(1)} %bitcast.45, bf16[8,1536,128]{2,1,0:T(8,128)(2,1)S(1)} %bitcast.44), custom_call_target="tpu_custom_call" | custom-call | flops 810000000 | bytes 5000000 | tf_op jit(solution)/shard_map/project/pallas_call | solution.py:113
  104.4 4.7 %collective-permute-start.1 = (bf16[2,64,1536]{2,1,0:T(8,128)(2,1)S(1)}, bf16[2,64,1536]{2,1,0:T(8,128)(2,1)S(1)}, u32[]{:S(2)}, u32[]{:S(2)}) collective-permute-start(bf16[2,64,1536]{2,1,0:T(8,128)(2,1)S(1)} %get-tuple-element.10), channel_id=1, source_target_pairs={{0,16},{16,0},{1,17},{17,1},{2,18},{18,2},{3,19},{19,3},{4,20},{20... | collective-permute-start | bytes 1179656 | tf_op jit(solution)/shard_map/ppermute | solution.py:162
  109.3 1.1 collective-permute-done.1.came_ref
  110.4 1.3 %norm.1 = (f32[64,128]{1,0:T(8,128)S(1)}, f32[64,128]{1,0:T(8,128)S(1)}) custom-call(s32[2]{0:T(128)S(1)} %pad_add_fusion.where_ref, f32[2,64,1536]{2,1,0:T(8,128)S(1)} %get-tuple-element.9.keep_ref, bf16[2,64,1536]{2,1,0:T(8,128)(2,1)S(1)} %collective-permute-done.1.came_ref, bf16[64,1536]{1,0:T(8,128)(2,1)S(1)} %get-tuple-element.24.own_ref, ...), custom_call_target="tpu_custom_call" | custom-call | tf_op jit(solution)/shard_map/norm/pallas_call | solution.py:148
  111.8 2.6 %collective-permute-start.4 = (f32[64,128]{1,0:T(8,128)S(1)}, f32[64,128]{1,0:T(8,128)S(1)}, u32[]{:S(2)}, u32[]{:S(2)}) collective-permute-start(f32[64,128]{1,0:T(8,128)S(1)} %get-tuple-element.12), channel_id=1, source_target_pairs={{0,256},{256,0},{1,257},{257,1},{2,258},{258,2},{3,259},{259,3},{4... | collective-permute-start | bytes 98312 | tf_op jit(solution)/shard_map/ppermute | solution.py:162
  114.4 3.5 %collective-permute-done.4 = f32[64,128]{1,0:T(8,128)S(1)} collective-permute-done((f32[64,128]{1,0:T(8,128)S(1)}, f32[64,128]{1,0:T(8,128)S(1)}, u32[]{:S(2)}, u32[]{:S(2)}) %collective-permute-start.4) | collective-permute-done | bytes 32800 | tf_op jit(solution)/shard_map/ppermute | solution.py:162
  118.4 0.7 copy.26
  (38 shorter events, 1.6 us)
Async XLA Ops:
  6.5 94.4 %all-gather.3.cloned.1.call-start = ((), (), s32[]{:S(2)}) async-start(), calls=%async_computation.2 | async-start | bytes 3538944 | tf_op jit(solution)/shard_map/all_gather | solution.py:180
  6.5 6.5 %collective-permute-start = (bf16[192,128]{1,0:T(8,128)(2,1)}, bf16[192,128]{1,0:T(8,128)(2,1)S(1)}, u32[]{:S(2)}, u32[]{:S(2)}) collective-permute-start(bf16[192,128]{1,0:T(8,128)(2,1)} %bitcast.52), channel_id=1, source_target_pairs={{0,0},{8,16},{16,32},{24,48},{32,64},{40,80},{48,96},{56,112},{64,... | collective-permute-start | bytes 147464 | tf_op jit(solution)/shard_map/ppermute | solution.py:178
  40.2 12.8 %copy-start.2 = (bf16[1,1,64,3072]{3,2,1,0:T(8,128)(2,1)S(1)}, bf16[1,1,64,3072]{3,2,1,0:T(8,128)(2,1)}, u32[]{:S(2)}) copy-start(bf16[1,1,64,3072]{3,2,1,0:T(8,128)(2,1)} %param.9) | copy-start | bytes 1179652
  42.4 17.3 %copy-start.4 = (f32[1,3,3072]{2,0,1:T(1,128)S(1)}, f32[1,3,3072]{2,0,1:T(1,128)}, u32[]{:S(2)}) copy-start(f32[1,3,3072]{2,0,1:T(1,128)} %param.12) | copy-start | bytes 110596
  42.4 19.9 %copy-start.3 = (bf16[3072,64]{0,1:T(8,128)(2,1)S(1)}, bf16[3072,64]{0,1:T(8,128)(2,1)}, u32[]{:S(2)}) copy-start(bf16[3072,64]{0,1:T(8,128)(2,1)} %param.11) | copy-start | bytes 1179652
  42.4 33.3 %all-to-all-start = ((bf16[16,3,64,128]{3,2,1,0:T(8,128)(2,1)}), bf16[16,3,64,128]{3,2,1,0:T(8,128)(2,1)S(1)}, u32[]{:S(2)}, u32[]{:S(2)}) async-start(bf16[16,3,64,128]{3,2,1,0:T(8,128)(2,1)} %pack.1), calls=%async_computation | async-start | bytes 1572864 | tf_op jit(solution)/shard_map/all_to_all | solution.py:189
  53.7 55.6 %collective-permute-start.2 = (bf16[64,1536]{1,0:T(8,128)(2,1)}, bf16[64,1536]{1,0:T(8,128)(2,1)S(1)}, u32[]{:S(2)}, u32[]{:S(2)}) collective-permute-start(bf16[64,1536]{1,0:T(8,128)(2,1)} %get-tuple-element.23), channel_id=1, source_target_pairs={{0,256},{256,0},{1,257},{257,1},{2,258},{258,2},{3,259},{259,3},{4... | collective-permute-start | bytes 589832 | tf_op jit(solution)/shard_map/ppermute | solution.py:162
  60.3 27.4 %collective-permute-start.3 = (f32[3,3072]{1,0:T(4,128)}, f32[3,3072]{1,0:T(4,128)}, u32[]{:S(2)}, u32[]{:S(2)}) collective-permute-start(f32[3,3072]{1,0:T(4,128)} %bitcast.39.clone.2), channel_id=1, source_target_pairs={{0,256},{256,0},{1,257},{257,1},{2,258},{258,2},{3,259},{259,3},{4... | collective-permute-start | bytes 110600 | tf_op jit(solution)/shard_map/ppermute | solution.py:162
  62.7 13.0 %copy-start.1 = (s32[1,8]{1,0:T(1,128)S(1)}, s32[1,8]{1,0:T(1,128)}, u32[]{:S(2)}) copy-start(s32[1,8]{1,0:T(1,128)} %param.13) | copy-start | bytes 100
  63.7 22.2 %copy-start.5 = (f32[1,64,32]{1,2,0:T(8,128)S(1)}, f32[1,64,32]{1,2,0:T(8,128)}, u32[]{:S(2)}) copy-start(f32[1,64,32]{1,2,0:T(8,128)} %param.15) | copy-start | bytes 24580
  79.3 21.7 %all-to-all-start.1 = ((bf16[16,128,128]{2,1,0:T(8,128)(2,1)}), bf16[16,128,128]{2,1,0:T(8,128)(2,1)S(1)}, u32[]{:S(2)}, u32[]{:S(2)}) async-start(bf16[16,128,128]{2,1,0:T(8,128)(2,1)} %bitcast.5), calls=%async_computation.1 | async-start | bytes 1048576 | tf_op jit(solution)/shard_map/all_to_all | solution.py:217
  101.0 1.9 %copy-start = (bf16[12288,128]{1,0:T(8,128)(2,1)S(1)}, bf16[12288,128]{1,0:T(8,128)(2,1)}, u32[]{:S(2)}) copy-start(bf16[12288,128]{1,0:T(8,128)(2,1)} %all-gather.3.cloned.1.call-done) | copy-start | bytes 9437188
  104.4 6.0 %collective-permute-start.1 = (bf16[2,64,1536]{2,1,0:T(8,128)(2,1)S(1)}, bf16[2,64,1536]{2,1,0:T(8,128)(2,1)S(1)}, u32[]{:S(2)}, u32[]{:S(2)}) collective-permute-start(bf16[2,64,1536]{2,1,0:T(8,128)(2,1)S(1)} %get-tuple-element.10), channel_id=1, source_target_pairs={{0,16},{16,0},{1,17},{17,1},{2,18},{18,2},{3,19},{19,3},{4,20},{20... | collective-permute-start | bytes 1179656 | tf_op jit(solution)/shard_map/ppermute | solution.py:162
  111.8 6.2 %collective-permute-start.4 = (f32[64,128]{1,0:T(8,128)S(1)}, f32[64,128]{1,0:T(8,128)S(1)}, u32[]{:S(2)}, u32[]{:S(2)}) collective-permute-start(f32[64,128]{1,0:T(8,128)S(1)} %get-tuple-element.12), channel_id=1, source_target_pairs={{0,256},{256,0},{1,257},{257,1},{2,258},{258,2},{3,259},{259,3},{4... | collective-permute-start | bytes 98312 | tf_op jit(solution)/shard_map/ppermute | solution.py:162
Sparse Core Ops, SparseCore 0:
  40.3 56.9 all-gather.2

commit v2 on v1

--- a/solution.py
+++ b/solution.py
@@ -94,14 +94,25 @@
     )(frames, gathered)
 
 
-def project_kernel(where_ref, x_ref, w_ref, keep_ref, send_ref):
-    core = where_ref[0]
-    x = jnp.concatenate([x_ref[:, h].reshape(256, HD) for h in range(8)], axis=1)
-    tile = 512
-    for t in range(HALF // tile):
-        cols = slice(t * tile, (t + 1) * tile)
-        w = jnp.concatenate([w_ref[h, cols] for h in range(8)], axis=1)
+def project_kernel(where_ref, x_ref, *refs):
+    units, (keep_ref, send_ref) = refs[:9], refs[9:]
+    core, y, z = where_ref[0], where_ref[2], where_ref[3]
+    heads = [lax.rem(z + d + 8, 8) for d in (0, -1, 1, -2, 2, -3, 3, 4)]
+    x = jnp.concatenate([x_ref[:, h].reshape(256, HD) for h in heads], axis=1)
+    for t in range(4):
+        steps = [lax.bitwise_xor(jnp.int32(2 * t + i), y) for i in range(2)]
+        slots = [4 * lax.rem(step, 2) + lax.bitwise_and(step, 2) + step // 4 for step in steps]
+        tiles = [
+            jnp.concatenate([unit[pl.ds(pl.multiple_of(slot * 192, 64), 192)] for slot in slots], axis=0) for unit in units[:7]
+        ]
+        last = []
+        for slot in slots:
+            place = pl.ds(pl.multiple_of(lax.rem(slot, 4) * 192, 64), 192)
+            last.append(jnp.where(slot >= 4, units[8][place], units[7][place]))
+        tiles.append(jnp.concatenate(last, axis=0))
+        w = jnp.concatenate(tiles, axis=1)
         part = lax.dot_general(x, w, NT, preferred_element_type=jnp.float32)
+        cols = slice(t * 384, (t + 1) * 384)
         for b in range(2):
             low = part[b * 128 : b * 128 + 64]
             high = part[b * 128 + 64 : b * 128 + 128]
@@ -109,19 +120,19 @@
             send_ref[b, :, cols] = jnp.where(core == 0, high, low).astype(jnp.bfloat16)
 
 
-def project(where, x, w):
+def project(where, x, units):
     return pl.pallas_call(
         project_kernel,
         out_shape=(
             jax.ShapeDtypeStruct((2, DEV_ROWS, HALF), jnp.float32),
             jax.ShapeDtypeStruct((2, DEV_ROWS, HALF), jnp.bfloat16),
         ),
-        in_specs=[spec(SMEM), spec(VMEM), spec(VMEM)],
+        in_specs=[spec(SMEM)] + [spec(VMEM)] * 10,
         out_specs=(spec(VMEM), spec(VMEM)),
         compiler_params=pltpu.CompilerParams(vmem_limit_bytes=48 * 2**20),
         cost_estimate=pl.CostEstimate(flops=810_000_000, bytes_accessed=5_000_000, transcendentals=0),
         name="project",
-    )(where, x, w)
+    )(where, x, *units)
 
 
 def norm_kernel(where_ref, keep_ref, came_ref, own_ref, other_ref, mod_ref, r_ref, out_ref, send_ref):
@@ -175,15 +186,27 @@
 
 
 def gather_weight(out_weight):
-    block = lax.ppermute(out_weight.T, ("c", "y", "k", "l"), spread_pairs())
-    unit = lax.all_gather(block, "y", axis=0, tiled=True)
-    return lax.all_gather(unit, "z", axis=0, tiled=False)
+    unit = lax.ppermute(out_weight.T, ("c", "y", "k", "l"), spread_pairs())
+    for bit in (4, 2, 1):
+        unit = jnp.concatenate([unit, lax.ppermute(unit, "y", [(i, i ^ bit) for i in range(8)])])
+    up = [(i, (i + 1) % 8) for i in range(8)]
+    down = [(i, (i + 7) % 8) for i in range(8)]
+    units = [unit]
+    from_below = from_above = unit
+    for _ in range(3):
+        from_below = lax.ppermute(from_below, "z", up)
+        from_above = lax.ppermute(from_above, "z", down)
+        units += [from_below, from_above]
+    half = HALF // 2
+    units.append(lax.ppermute(from_below[:half], "z", up))
+    units.append(lax.ppermute(from_above[half:], "z", down))
+    return units
 
 
 def shards(qkv, residual, out_weight, final_weight, modulation, frames, timestep, noisy):
     branch = lax.axis_index("c")
     core = lax.axis_index("k")
-    where = jnp.stack([core, branch]).astype(jnp.int32)
+    where = jnp.stack([core, branch, lax.axis_index("y"), lax.axis_index("z")]).astype(jnp.int32)
 
     packed = pack(qkv[0, :, 0])
     gathered = lax.all_to_all(packed, ("y", "k"), 0, 0, tiled=True)

time: 127 us -> 143 us (1.13)
  starting transfers between devices: 36.9 us -> 90 us
  blocking collectives: 27.1 us -> 0 us
  between operations: 14.3 us -> 1.19 us
  waiting for transfers between devices: 30.5 us -> 23.8 us
  local copies, waits for them, and re-layouts: 5.43 us -> 10 us
  other arithmetic: 2.82 us -> 6.37 us
  Pallas kernels: 8.73 us -> 10.2 us
    ppermute x1 -> x12, starting transfers between devices: 4.58 us -> 54 us  [the longest x3 17.7 us: gather_weight(): from_above = lax.ppermute(from_above, 'z', down)]
    all_gather x1 -> x0, blocking collectives: 27.1 us -> none  [gather_weight(): unit = lax.all_gather(block, 'y', axis=0, tiled=True)]
    ppermute x1 -> x12, waiting for transfers between devices: 1.88 us -> 21.3 us  [the longest x3 8.02 us: gather_weight(): lax.ppermute(unit, 'y', [(i, i ^ bit) for i in range(8)])]
    all_to_all x1, waiting for transfers between devices: 12 us -> 0.01 us  [shards(): lax.all_to_all(heads.reshape(16, 128, HD), ('c', 'y'), 0, 0, tiled=True)]
    all_to_all x1, waiting for transfers between devices: 12 us -> 0.01 us  [shards(): gathered = lax.all_to_all(packed, ('y', 'k'), 0, 0, tiled=True)]
    ppermute x4, starting transfers between devices: 15.2 us -> 18.7 us  [flip(): return lax.ppermute(array, axis, [(0, 1), (1, 0)])]
    unnamed x19 -> x42, local copies, waits for them, and re-layouts: 2.9 us -> 5.87 us
    another operation x2, other arithmetic: 0.2 us -> 2.51 us  [shards(): jnp.stack([jnp.concatenate([fw_mine, empty, empty, empty, fw_partner, emp...]
  transfers between devices with their start and end apart: 8 -> 18, of which waited for: 5 -> 10; matrix products, arithmetic and copies ran while one was open for 4% -> 7% of each run, Pallas kernels for 6% -> 4%
where the time goes in v2:
time: 143 us; the launch traced here: 142 us
  starting transfers between devices  90 us (63%)
  waiting for transfers between devices  23.8 us (17%)
  Pallas kernels  10.2 us (7%)
  local copies, waits for them, and re-layouts  10 us (7%)
  other arithmetic  6.37 us (4%)
    ppermute x4, starting transfers between devices, flip(): return lax.ppermute(array, axis, [(0, 1), (1, 0)])  18.7 us
    ppermute x3, starting transfers between devices, gather_weight(): from_above = lax.ppermute(from_above, 'z', down)  17.7 us
    ppermute x3, starting transfers between devices, gather_weight(): lax.ppermute(unit, 'y', [(i, i ^ bit) for i in range(8)])  15 us
    ppermute x3, starting transfers between devices, gather_weight(): from_below = lax.ppermute(from_below, 'z', up)  11.3 us
    all_to_all x1, starting transfers between devices, shards(): gathered = lax.all_to_all(packed, ('y', 'k'), 0, 0, tiled=True)  10.4 us
    ppermute x3, waiting for transfers between devices, gather_weight(): lax.ppermute(unit, 'y', [(i, i ^ bit) for i in range(8)])  8.02 us
    all_to_all x1, starting transfers between devices, shards(): lax.all_to_all(heads.reshape(16, 128, HD), ('c', 'y'), 0, 0, tiled=True)  6.93 us
    ppermute x1, waiting for transfers between devices, gather_weight(): unit = lax.ppermute(out_weight.T, ('c', 'y', 'k', 'l'), spread_pairs())  6.17 us
  transfers between devices with their start and end apart: 18, of which 10 were waited for; matrix products, arithmetic and copies ran while one was open for 7% of the time, Pallas kernels for 4%

profile of v2, /device:TPU:1, one launch (start us, length us, event | category | flops | bytes accessed | tf_op | source)
XLA Modules:
  0.0 141.6 jit_solution(9811875791442070520)
XLA Ops:
  0.0 2.2 %pack.1 = bf16[16,3,64,128]{3,2,1,0:T(8,128)(2,1)} custom-call(bf16[3,64,2048]{2,1,0:T(8,128)(2,1)} %bitcast.50), custom_call_target="tpu_custom_call" | custom-call | tf_op jit(solution)/shard_map/pack/pallas_call | solution.py:41
  2.2 10.4 %all-to-all-start = ((bf16[16,3,64,128]{3,2,1,0:T(8,128)(2,1)}), bf16[16,3,64,128]{3,2,1,0:T(8,128)(2,1)S(1)}, u32[]{:S(2)}, u32[]{:S(2)}) async-start(bf16[16,3,64,128]{3,2,1,0:T(8,128)(2,1)} %pack.1), calls=%async_computation | async-start | bytes 1572864 | tf_op jit(solution)/shard_map/all_to_all | solution.py:212
  12.6 3.5 %collective-permute-start = (bf16[192,128]{1,0:T(8,128)(2,1)S(1)}, bf16[192,128]{1,0:T(8,128)(2,1)S(1)}, u32[]{:S(2)}, u32[]{:S(2)}) collective-permute-start(bf16[192,128]{1,0:T(8,128)(2,1)S(1)} %bitcast.53), channel_id=1, source_target_pairs={{0,0},{8,16},{16,32},{24,48},{32,64},{40,80},{48,96},{56,112},{64,... | collective-permute-start | bytes 147464 | tf_op jit(solution)/shard_map/ppermute | solution.py:189
  16.9 2.9 %collective-permute-start.13 = (bf16[64,1536]{1,0:T(8,128)(2,1)}, bf16[64,1536]{1,0:T(8,128)(2,1)}, u32[]{:S(2)}, u32[]{:S(2)}) collective-permute-start(bf16[64,1536]{1,0:T(8,128)(2,1)} %get-tuple-element.23), channel_id=1, source_target_pairs={{0,256},{256,0},{1,257},{257,1},{2,258},{258,2},{3,259},{259,3},{4... | collective-permute-start | bytes 589832 | tf_op jit(solution)/shard_map/ppermute | solution.py:173
  19.9 3.8 %collective-permute-start.14 = (f32[3,3072]{1,0:T(4,128)S(1)}, f32[3,3072]{1,0:T(4,128)}, u32[]{:S(2)}, u32[]{:S(2)}) collective-permute-start(f32[3,3072]{1,0:T(4,128)S(1)} %bitcast.51), channel_id=1, source_target_pairs={{0,256},{256,0},{1,257},{257,1},{2,258},{258,2},{3,259},{259,3},{4... | collective-permute-start | bytes 110600 | tf_op jit(solution)/shard_map/ppermute | solution.py:173
  24.1 6.2 %collective-permute-done = bf16[192,128]{1,0:T(8,128)(2,1)S(1)} collective-permute-done((bf16[192,128]{1,0:T(8,128)(2,1)S(1)}, bf16[192,128]{1,0:T(8,128)(2,1)S(1)}, u32[]{:S(2)}, u32[]{:S(2)}) %collective-permute-start) | collective-permute-done | bytes 49184 | tf_op jit(solution)/shard_map/ppermute | solution.py:189
  30.2 8.7 %collective-permute-start.1 = (bf16[192,128]{1,0:T(8,128)(2,1)S(1)}, bf16[192,128]{1,0:T(8,128)(2,1)S(1)}, u32[]{:S(2)}, u32[]{:S(2)}) collective-permute-start(bf16[192,128]{1,0:T(8,128)(2,1)S(1)} %collective-permute-done), channel_id=1, source_target_pairs={{0,128},{32,160},{64,192},{96,224},{128,0},{160,32},{192,64},{224,... | collective-permute-start | bytes 147464 | tf_op jit(solution)/shard_map/ppermute | solution.py:191
  40.5 4.3 %collective-permute-start.2 = (bf16[384,128]{1,0:T(8,128)(2,1)S(1)}, bf16[384,128]{1,0:T(8,128)(2,1)S(1)}, u32[]{:S(2)}, u32[]{:S(2)}) collective-permute-start(bf16[384,128]{1,0:T(8,128)(2,1)S(1)} %pad_maximum_fusion.2), channel_id=1, source_target_pairs={{0,64},{32,96},{64,0},{96,32},{128,192},{160,224},{192,128},{224,1... | collective-permute-start | bytes 294920 | tf_op jit(solution)/shard_map/ppermute | solution.py:191
  44.9 3.0 %collective-permute-done.2 = bf16[384,128]{1,0:T(8,128)(2,1)S(1)} collective-permute-done((bf16[384,128]{1,0:T(8,128)(2,1)S(1)}, bf16[384,128]{1,0:T(8,128)(2,1)S(1)}, u32[]{:S(2)}, u32[]{:S(2)}) %collective-permute-start.2) | collective-permute-done | bytes 98336 | tf_op jit(solution)/shard_map/ppermute | solution.py:191
  47.9 1.9 %collective-permute-start.3 = (bf16[768,128]{1,0:T(8,128)(2,1)S(1)}, bf16[768,128]{1,0:T(8,128)(2,1)S(1)}, u32[]{:S(2)}, u32[]{:S(2)}) collective-permute-start(bf16[768,128]{1,0:T(8,128)(2,1)S(1)} %pad_maximum_fusion.1), channel_id=1, source_target_pairs={{0,32},{32,0},{64,96},{96,64},{128,160},{160,128},{192,224},{224,1... | collective-permute-start | bytes 589832 | tf_op jit(solution)/shard_map/ppermute | solution.py:191
  49.9 4.4 %collective-permute-done.3 = bf16[768,128]{1,0:T(8,128)(2,1)S(1)} collective-permute-done((bf16[768,128]{1,0:T(8,128)(2,1)S(1)}, bf16[768,128]{1,0:T(8,128)(2,1)S(1)}, u32[]{:S(2)}, u32[]{:S(2)}) %collective-permute-start.3) | collective-permute-done | bytes 196640 | tf_op jit(solution)/shard_map/ppermute | solution.py:191
  54.4 7.5 %collective-permute-start.4 = (bf16[1536,128]{1,0:T(8,128)(2,1)S(1)}, bf16[1536,128]{1,0:T(8,128)(2,1)S(1)}, u32[]{:S(2)}, u32[]{:S(2)}) collective-permute-start(bf16[1536,128]{1,0:T(8,128)(2,1)S(1)} %constant_dynamic-update-slice_fusion.refs_0_), channel_id=1, source_target_pairs={{0,1},{1,2},{2,3},{3,4},{4,5},{5,6},{6,7},{7,0},{8,9},{9,10},{10,1... | collective-permute-start | bytes 1179656 | tf_op jit(solution)/shard_map/ppermute | solution.py:197
  61.8 8.6 %collective-permute-start.5 = (bf16[1536,128]{1,0:T(8,128)(2,1)S(1)}, bf16[1536,128]{1,0:T(8,128)(2,1)}, u32[]{:S(2)}, u32[]{:S(2)}) collective-permute-start(bf16[1536,128]{1,0:T(8,128)(2,1)S(1)} %constant_dynamic-update-slice_fusion.refs_0_), channel_id=1, source_target_pairs={{0,7},{1,0},{2,1},{3,2},{4,3},{5,4},{6,5},{7,6},{8,15},{9,8},{10,9... | collective-permute-start | bytes 1179656 | tf_op jit(solution)/shard_map/ppermute | solution.py:198
  71.5 4.6 %collective-permute-done.4.refs_1_ = bf16[1536,128]{1,0:T(8,128)(2,1)S(1)} collective-permute-done((bf16[1536,128]{1,0:T(8,128)(2,1)S(1)}, bf16[1536,128]{1,0:T(8,128)(2,1)S(1)}, u32[]{:S(2)}, u32[]{:S(2)}) %collective-permute-start.4) | collective-permute-done | bytes 393248 | tf_op jit(solution)/shard_map/ppermute | solution.py:197
  78.0 4.6 %collective-permute-start.7 = (bf16[1536,128]{1,0:T(8,128)(2,1)}, bf16[1536,128]{1,0:T(8,128)(2,1)}, u32[]{:S(2)}, u32[]{:S(2)}) collective-permute-start(bf16[1536,128]{1,0:T(8,128)(2,1)} %collective-permute-done.5.refs_2_), channel_id=1, source_target_pairs={{0,7},{1,0},{2,1},{3,2},{4,3},{5,4},{6,5},{7,6},{8,15},{9,8},{10,9... | collective-permute-start | bytes 1179656 | tf_op jit(solution)/shard_map/ppermute | solution.py:198
  84.2 3.6 %attend.1 = bf16[2,8,128,128]{3,2,1,0:T(8,128)(2,1)} custom-call(s32[8]{0:T(128)S(1)} %bitcast.46, bf16[16,3,64,128]{3,2,1,0:T(8,128)(2,1)S(1)} %all-to-all-done.x_ref), custom_call_target="tpu_custom_call" | custom-call | flops 540000000 | bytes 2000000 | tf_op jit(solution)/shard_map/attend/pallas_call | solution.py:86
  87.9 6.9 %all-to-all-start.1 = ((bf16[16,128,128]{2,1,0:T(8,128)(2,1)}), bf16[16,128,128]{2,1,0:T(8,128)(2,1)S(1)}, u32[]{:S(2)}, u32[]{:S(2)}) async-start(bf16[16,128,128]{2,1,0:T(8,128)(2,1)} %bitcast.7), calls=%async_computation.1 | async-start | bytes 1048576 | tf_op jit(solution)/shard_map/all_to_all | solution.py:240
  98.1 1.9 %collective-permute-start.8 = (bf16[1536,128]{1,0:T(8,128)(2,1)}, bf16[1536,128]{1,0:T(8,128)(2,1)S(1)}, u32[]{:S(2)}, u32[]{:S(2)}) collective-permute-start(bf16[1536,128]{1,0:T(8,128)(2,1)} %collective-permute-done.6.refs_3_), channel_id=1, source_target_pairs={{0,1},{1,2},{2,3},{3,4},{4,5},{5,6},{6,7},{7,0},{8,9},{9,10},{10,1... | collective-permute-start | bytes 1179656 | tf_op jit(solution)/shard_map/ppermute | solution.py:197
  100.0 4.6 %collective-permute-start.9 = (bf16[1536,128]{1,0:T(8,128)(2,1)}, bf16[1536,128]{1,0:T(8,128)(2,1)S(1)}, u32[]{:S(2)}, u32[]{:S(2)}) collective-permute-start(bf16[1536,128]{1,0:T(8,128)(2,1)} %collective-permute-done.7.refs_4_), channel_id=1, source_target_pairs={{0,7},{1,0},{2,1},{3,2},{4,3},{5,4},{6,5},{7,6},{8,15},{9,8},{10,9... | collective-permute-start | bytes 1179656 | tf_op jit(solution)/shard_map/ppermute | solution.py:198
  108.8 1.9 %collective-permute-start.10 = (bf16[768,128]{1,0:T(8,128)(2,1)S(1)}, bf16[768,128]{1,0:T(8,128)(2,1)S(1)}, u32[]{:S(2)}, u32[]{:S(2)}) collective-permute-start(bf16[768,128]{1,0:T(8,128)(2,1)S(1)} %slice.86), channel_id=1, source_target_pairs={{0,1},{1,2},{2,3},{3,4},{4,5},{5,6},{6,7},{7,0},{8,9},{9,10},{10,1... | collective-permute-start | bytes 589832 | tf_op jit(solution)/shard_map/ppermute | solution.py:201
  110.8 4.6 %collective-permute-start.11 = (bf16[768,128]{1,0:T(8,128)(2,1)S(1)}, bf16[768,128]{1,0:T(8,128)(2,1)S(1)}, u32[]{:S(2)}, u32[]{:S(2)}) collective-permute-start(bf16[768,128]{1,0:T(8,128)(2,1)S(1)} %slice.87), channel_id=1, source_target_pairs={{0,7},{1,0},{2,1},{3,2},{4,3},{5,4},{6,5},{7,6},{8,15},{9,8},{10,9... | collective-permute-start | bytes 589832 | tf_op jit(solution)/shard_map/ppermute | solution.py:202
  121.5 2.6 %project.1 = (f32[2,64,1536]{2,1,0:T(8,128)S(1)}, bf16[2,64,1536]{2,1,0:T(8,128)(2,1)S(1)}) custom-call(s32[4]{0:T(128)S(1)} %pad_add_fusion.where_ref, bf16[2,8,128,128]{3,2,1,0:T(8,128)(2,1)S(1)} %bitcast.45, bf16[1536,128]{1,0:T(8,128)(2,1)S(1)} %constant_dynamic-update-slice_fusion.refs_0_, bf16[1536,128]{1,0:T(8,128)(2,1)S(1)} %copy-done.1, ...), custom_call_target="tpu_custom_call" | custom-call | flops 810000000 | bytes 5000000 | tf_op jit(solution)/shard_map/project/pallas_call | solution.py:124
  124.1 7.1 %collective-permute-start.12 = (bf16[2,64,1536]{2,1,0:T(8,128)(2,1)S(1)}, bf16[2,64,1536]{2,1,0:T(8,128)(2,1)S(1)}, u32[]{:S(2)}, u32[]{:S(2)}) collective-permute-start(bf16[2,64,1536]{2,1,0:T(8,128)(2,1)S(1)} %get-tuple-element.10), channel_id=1, source_target_pairs={{0,16},{16,0},{1,17},{17,1},{2,18},{18,2},{3,19},{19,3},{4,20},{20... | collective-permute-start | bytes 1179656 | tf_op jit(solution)/shard_map/ppermute | solution.py:173
  134.3 4.8 %collective-permute-start.15 = (f32[64,128]{1,0:T(8,128)S(1)}, f32[64,128]{1,0:T(8,128)S(1)}, u32[]{:S(2)}, u32[]{:S(2)}) collective-permute-start(f32[64,128]{1,0:T(8,128)S(1)} %get-tuple-element.12), channel_id=1, source_target_pairs={{0,256},{256,0},{1,257},{257,1},{2,258},{258,2},{3,259},{259,3},{4... | collective-permute-start | bytes 98312 | tf_op jit(solution)/shard_map/ppermute | solution.py:173
  (84 shorter events, 25.6 us)
Async XLA Ops:
  0.0 12.6 %copy-start.15 = (bf16[128,192]{0,1:T(8,128)(2,1)S(1)}, bf16[128,192]{0,1:T(8,128)(2,1)}, u32[]{:S(2)}) copy-start(bf16[128,192]{0,1:T(8,128)(2,1)} %param.10) | copy-start | bytes 147460
  0.0 16.2 %copy-start.9 = (bf16[1,1,64,3072]{3,2,1,0:T(8,128)(2,1)S(1)}, bf16[1,1,64,3072]{3,2,1,0:T(8,128)(2,1)}, u32[]{:S(2)}) copy-start(bf16[1,1,64,3072]{3,2,1,0:T(8,128)(2,1)} %param.9) | copy-start | bytes 1179652
  2.2 17.7 %copy-start.13 = (f32[1,3,3072]{2,0,1:T(1,128)S(1)}, f32[1,3,3072]{2,0,1:T(1,128)}, u32[]{:S(2)}) copy-start(f32[1,3,3072]{2,0,1:T(1,128)} %param.12) | copy-start | bytes 110596
  2.2 21.6 %copy-start.10 = (bf16[3072,64]{0,1:T(8,128)(2,1)S(1)}, bf16[3072,64]{0,1:T(8,128)(2,1)}, u32[]{:S(2)}) copy-start(bf16[3072,64]{0,1:T(8,128)(2,1)} %param.11) | copy-start | bytes 1179652
  2.2 82.0 %all-to-all-start = ((bf16[16,3,64,128]{3,2,1,0:T(8,128)(2,1)}), bf16[16,3,64,128]{3,2,1,0:T(8,128)(2,1)S(1)}, u32[]{:S(2)}, u32[]{:S(2)}) async-start(bf16[16,3,64,128]{3,2,1,0:T(8,128)(2,1)} %pack.1), calls=%async_computation | async-start | bytes 1572864 | tf_op jit(solution)/shard_map/all_to_all | solution.py:212
  12.6 17.6 %collective-permute-start = (bf16[192,128]{1,0:T(8,128)(2,1)S(1)}, bf16[192,128]{1,0:T(8,128)(2,1)S(1)}, u32[]{:S(2)}, u32[]{:S(2)}) collective-permute-start(bf16[192,128]{1,0:T(8,128)(2,1)S(1)} %bitcast.53), channel_id=1, source_target_pairs={{0,0},{8,16},{16,32},{24,48},{32,64},{40,80},{48,96},{56,112},{64,... | collective-permute-start | bytes 147464 | tf_op jit(solution)/shard_map/ppermute | solution.py:189
  16.9 114.5 %collective-permute-start.13 = (bf16[64,1536]{1,0:T(8,128)(2,1)}, bf16[64,1536]{1,0:T(8,128)(2,1)}, u32[]{:S(2)}, u32[]{:S(2)}) collective-permute-start(bf16[64,1536]{1,0:T(8,128)(2,1)} %get-tuple-element.23), channel_id=1, source_target_pairs={{0,256},{256,0},{1,257},{257,1},{2,258},{258,2},{3,259},{259,3},{4... | collective-permute-start | bytes 589832 | tf_op jit(solution)/shard_map/ppermute | solution.py:173
  19.9 84.7 %collective-permute-start.14 = (f32[3,3072]{1,0:T(4,128)S(1)}, f32[3,3072]{1,0:T(4,128)}, u32[]{:S(2)}, u32[]{:S(2)}) collective-permute-start(f32[3,3072]{1,0:T(4,128)S(1)} %bitcast.51), channel_id=1, source_target_pairs={{0,256},{256,0},{1,257},{257,1},{2,258},{258,2},{3,259},{259,3},{4... | collective-permute-start | bytes 110600 | tf_op jit(solution)/shard_map/ppermute | solution.py:173
  30.2 10.3 %collective-permute-start.1 = (bf16[192,128]{1,0:T(8,128)(2,1)S(1)}, bf16[192,128]{1,0:T(8,128)(2,1)S(1)}, u32[]{:S(2)}, u32[]{:S(2)}) collective-permute-start(bf16[192,128]{1,0:T(8,128)(2,1)S(1)} %collective-permute-done), channel_id=1, source_target_pairs={{0,128},{32,160},{64,192},{96,224},{128,0},{160,32},{192,64},{224,... | collective-permute-start | bytes 147464 | tf_op jit(solution)/shard_map/ppermute | solution.py:191
  40.5 7.4 %collective-permute-start.2 = (bf16[384,128]{1,0:T(8,128)(2,1)S(1)}, bf16[384,128]{1,0:T(8,128)(2,1)S(1)}, u32[]{:S(2)}, u32[]{:S(2)}) collective-permute-start(bf16[384,128]{1,0:T(8,128)(2,1)S(1)} %pad_maximum_fusion.2), channel_id=1, source_target_pairs={{0,64},{32,96},{64,0},{96,32},{128,192},{160,224},{192,128},{224,1... | collective-permute-start | bytes 294920 | tf_op jit(solution)/shard_map/ppermute | solution.py:191
  47.9 6.4 %collective-permute-start.3 = (bf16[768,128]{1,0:T(8,128)(2,1)S(1)}, bf16[768,128]{1,0:T(8,128)(2,1)S(1)}, u32[]{:S(2)}, u32[]{:S(2)}) collective-permute-start(bf16[768,128]{1,0:T(8,128)(2,1)S(1)} %pad_maximum_fusion.1), channel_id=1, source_target_pairs={{0,32},{32,0},{64,96},{96,64},{128,160},{160,128},{192,224},{224,1... | collective-permute-start | bytes 589832 | tf_op jit(solution)/shard_map/ppermute | solution.py:191
  54.4 21.7 %collective-permute-start.4 = (bf16[1536,128]{1,0:T(8,128)(2,1)S(1)}, bf16[1536,128]{1,0:T(8,128)(2,1)S(1)}, u32[]{:S(2)}, u32[]{:S(2)}) collective-permute-start(bf16[1536,128]{1,0:T(8,128)(2,1)S(1)} %constant_dynamic-update-slice_fusion.refs_0_), channel_id=1, source_target_pairs={{0,1},{1,2},{2,3},{3,4},{4,5},{5,6},{6,7},{7,0},{8,9},{9,10},{10,1... | collective-permute-start | bytes 1179656 | tf_op jit(solution)/shard_map/ppermute | solution.py:197
  61.8 16.2 %collective-permute-start.5 = (bf16[1536,128]{1,0:T(8,128)(2,1)S(1)}, bf16[1536,128]{1,0:T(8,128)(2,1)}, u32[]{:S(2)}, u32[]{:S(2)}) collective-permute-start(bf16[1536,128]{1,0:T(8,128)(2,1)S(1)} %constant_dynamic-update-slice_fusion.refs_0_), channel_id=1, source_target_pairs={{0,7},{1,0},{2,1},{3,2},{4,3},{5,4},{6,5},{7,6},{8,15},{9,8},{10,9... | collective-permute-start | bytes 1179656 | tf_op jit(solution)/shard_map/ppermute | solution.py:198
  70.5 12.2 %copy-start.8 = (bf16[256,1536]{1,0:T(8,128)(2,1)}, bf16[256,1536]{1,0:T(8,128)(2,1)S(1)}, u32[]{:S(2)}) copy-start(bf16[256,1536]{1,0:T(8,128)(2,1)S(1)} %broadcast_dynamic-update-slice_fusion.1) | copy-start | bytes 2359300
  76.1 21.9 %collective-permute-start.6 = (bf16[1536,128]{1,0:T(8,128)(2,1)S(1)}, bf16[1536,128]{1,0:T(8,128)(2,1)}, u32[]{:S(2)}, u32[]{:S(2)}) collective-permute-start(bf16[1536,128]{1,0:T(8,128)(2,1)S(1)} %collective-permute-done.4.refs_1_), channel_id=1, source_target_pairs={{0,1},{1,2},{2,3},{3,4},{4,5},{5,6},{6,7},{7,0},{8,9},{9,10},{10,1... | collective-permute-start | bytes 1179656 | tf_op jit(solution)/shard_map/ppermute | solution.py:197
  78.0 21.9 %collective-permute-start.7 = (bf16[1536,128]{1,0:T(8,128)(2,1)}, bf16[1536,128]{1,0:T(8,128)(2,1)}, u32[]{:S(2)}, u32[]{:S(2)}) collective-permute-start(bf16[1536,128]{1,0:T(8,128)(2,1)} %collective-permute-done.5.refs_2_), channel_id=1, source_target_pairs={{0,7},{1,0},{2,1},{3,2},{4,3},{5,4},{6,5},{7,6},{8,15},{9,8},{10,9... | collective-permute-start | bytes 1179656 | tf_op jit(solution)/shard_map/ppermute | solution.py:198
  84.2 10.7 %copy-start.14 = (f32[1,64,32]{1,2,0:T(8,128)S(1)}, f32[1,64,32]{1,2,0:T(8,128)}, u32[]{:S(2)}) copy-start(f32[1,64,32]{1,2,0:T(8,128)} %param.15) | copy-start | bytes 24580
  87.9 30.8 %all-to-all-start.1 = ((bf16[16,128,128]{2,1,0:T(8,128)(2,1)}), bf16[16,128,128]{2,1,0:T(8,128)(2,1)S(1)}, u32[]{:S(2)}, u32[]{:S(2)}) async-start(bf16[16,128,128]{2,1,0:T(8,128)(2,1)} %bitcast.7), calls=%async_computation.1 | async-start | bytes 1048576 | tf_op jit(solution)/shard_map/all_to_all | solution.py:240
  98.1 10.8 %collective-permute-start.8 = (bf16[1536,128]{1,0:T(8,128)(2,1)}, bf16[1536,128]{1,0:T(8,128)(2,1)S(1)}, u32[]{:S(2)}, u32[]{:S(2)}) collective-permute-start(bf16[1536,128]{1,0:T(8,128)(2,1)} %collective-permute-done.6.refs_3_), channel_id=1, source_target_pairs={{0,1},{1,2},{2,3},{3,4},{4,5},{5,6},{6,7},{7,0},{8,9},{9,10},{10,1... | collective-permute-start | bytes 1179656 | tf_op jit(solution)/shard_map/ppermute | solution.py:197
  100.0 10.8 %collective-permute-start.9 = (bf16[1536,128]{1,0:T(8,128)(2,1)}, bf16[1536,128]{1,0:T(8,128)(2,1)S(1)}, u32[]{:S(2)}, u32[]{:S(2)}) collective-permute-start(bf16[1536,128]{1,0:T(8,128)(2,1)} %collective-permute-done.7.refs_4_), channel_id=1, source_target_pairs={{0,7},{1,0},{2,1},{3,2},{4,3},{5,4},{6,5},{7,6},{8,15},{9,8},{10,9... | collective-permute-start | bytes 1179656 | tf_op jit(solution)/shard_map/ppermute | solution.py:198
  108.8 7.6 %collective-permute-start.10 = (bf16[768,128]{1,0:T(8,128)(2,1)S(1)}, bf16[768,128]{1,0:T(8,128)(2,1)S(1)}, u32[]{:S(2)}, u32[]{:S(2)}) collective-permute-start(bf16[768,128]{1,0:T(8,128)(2,1)S(1)} %slice.86), channel_id=1, source_target_pairs={{0,1},{1,2},{2,3},{3,4},{4,5},{5,6},{6,7},{7,0},{8,9},{9,10},{10,1... | collective-permute-start | bytes 589832 | tf_op jit(solution)/shard_map/ppermute | solution.py:201
  110.8 7.2 %collective-permute-start.11 = (bf16[768,128]{1,0:T(8,128)(2,1)S(1)}, bf16[768,128]{1,0:T(8,128)(2,1)S(1)}, u32[]{:S(2)}, u32[]{:S(2)}) collective-permute-start(bf16[768,128]{1,0:T(8,128)(2,1)S(1)} %slice.87), channel_id=1, source_target_pairs={{0,7},{1,0},{2,1},{3,2},{4,3},{5,4},{6,5},{7,6},{8,15},{9,8},{10,9... | collective-permute-start | bytes 589832 | tf_op jit(solution)/shard_map/ppermute | solution.py:202
  124.1 8.5 %collective-permute-start.12 = (bf16[2,64,1536]{2,1,0:T(8,128)(2,1)S(1)}, bf16[2,64,1536]{2,1,0:T(8,128)(2,1)S(1)}, u32[]{:S(2)}, u32[]{:S(2)}) collective-permute-start(bf16[2,64,1536]{2,1,0:T(8,128)(2,1)S(1)} %get-tuple-element.10), channel_id=1, source_target_pairs={{0,16},{16,0},{1,17},{17,1},{2,18},{18,2},{3,19},{19,3},{4,20},{20... | collective-permute-start | bytes 1179656 | tf_op jit(solution)/shard_map/ppermute | solution.py:173
  134.3 6.2 %collective-permute-start.15 = (f32[64,128]{1,0:T(8,128)S(1)}, f32[64,128]{1,0:T(8,128)S(1)}, u32[]{:S(2)}, u32[]{:S(2)}) collective-permute-start(f32[64,128]{1,0:T(8,128)S(1)} %get-tuple-element.12), channel_id=1, source_target_pairs={{0,256},{256,0},{1,257},{257,1},{2,258},{258,2},{3,259},{259,3},{4... | collective-permute-start | bytes 98312 | tf_op jit(solution)/shard_map/ppermute | solution.py:173
  (10 other events, 32.4 us)

commit v3 on v1

v3 whole, which is shorter than its diff:
```python
import functools

import jax
import jax.numpy as jnp
import numpy as np
from jax import lax
from jax.experimental import pallas as pl
from jax.experimental.pallas import tpu as pltpu
from jax.sharding import Mesh, PartitionSpec as P

HD = 128
STEPS = 50
FRAME_TOK = 2
GUIDE = 6.0
SHIFT = 7.0
EPS = 1e-06
FILL = -1e30
ROWS = 1024
DEV_ROWS = 64
HALF = 1536
WIDTH = 3072
LOG2E = 1.4426950408889634

NT = (((1,), (1,)), ((), ()))
VMEM = pltpu.VMEM
SMEM = pltpu.SMEM


def spec(space):
    return pl.BlockSpec(memory_space=space)


def pack_kernel(in_ref, out_ref):
    for y in range(8):
        for k in range(2):
            head = 8 * k + y
            out_ref[2 * y + k] = in_ref[:, :, head * HD : (head + 1) * HD]


def pack(own):
    return pl.pallas_call(
        pack_kernel,
        out_shape=jax.ShapeDtypeStruct((16, 3, DEV_ROWS, HD), jnp.bfloat16),
        in_specs=[spec(VMEM)],
        out_specs=spec(VMEM),
        name="pack",
    )(own)


BLOCKS = ((0, 128, 0, 256), (128, 256, 0, 1024), (256, 512, 128, 1024), (512, 768, 128, 1024), (768, 1024, 128, 1024))


def attend_kernel(frames_ref, x_ref, out_ref):
    ends = []
    total = jnp.int32(0)
    for r in range(8):
        total = total + ((frames_ref[r] - 1) // 4 + 1) * FRAME_TOK
        ends.append(total)

    def ids(shape, dim, first):
        place = lax.broadcasted_iota(jnp.int32, shape, dim) + first
        found = jnp.zeros(shape, jnp.int32)
        for end in ends:
            found = found + (place >= end).astype(jnp.int32)
        return found

    scale = HD**-0.5 * LOG2E
    for first, last, low, high in BLOCKS:
        n, m = last - first, high - low
        q = x_ref[first // 64 : last // 64, 0].reshape(n, HD)
        k = x_ref[low // 64 : high // 64, 1].reshape(m, HD)
        v = x_ref[low // 64 : high // 64, 2].reshape(m, HD)
        scores = lax.dot_general(q, k, NT, preferred_element_type=jnp.float32)
        same = ids((n, 1), 0, first) == ids((1, m), 1, low)
        scores = jnp.where(same, scores, FILL)
        largest = jnp.max(scores, axis=1, keepdims=True)
        weights = jnp.exp2((scores - largest) * scale)
        denominator = jnp.sum(weights, axis=1, keepdims=True)
        mixed = jnp.dot(weights.astype(jnp.bfloat16), v, preferred_element_type=jnp.float32)
        result = (mixed / denominator).astype(jnp.bfloat16).reshape(n // 128, 128, HD)
        out_ref[0, first // 128 : last // 128] = result
        out_ref[1, first // 128 : last // 128] = result


def attend(frames, gathered):
    return pl.pallas_call(
        attend_kernel,
        out_shape=jax.ShapeDtypeStruct((2, 8, 128, HD), jnp.bfloat16),
        in_specs=[spec(SMEM), spec(VMEM)],
        out_specs=spec(VMEM),
        compiler_params=pltpu.CompilerParams(vmem_limit_bytes=32 * 2**20),
        cost_estimate=pl.CostEstimate(flops=540_000_000, bytes_accessed=2_000_000, transcendentals=1_000_000),
        name="attend",
    )(frames, gathered)


def project_kernel(where_ref, x_ref, w_ref, keep_ref, send_ref):
    core = where_ref[0]
    x = jnp.concatenate([x_ref[:, h].reshape(256, HD) for h in range(8)], axis=1)
    tile = 384
    for t in range(HALF // tile):
        cols = slice(t * tile, (t + 1) * tile)
        w = jnp.concatenate([w_ref[h, cols] for h in range(8)], axis=1)
        part = lax.dot_general(x, w, NT, preferred_element_type=jnp.float32)
        for b in range(2):
            low = part[b * 128 : b * 128 + 64]
            high = part[b * 128 + 64 : b * 128 + 128]
            keep_ref[b, :, cols] = jnp.where(core == 0, low, high)
            send_ref[b, :, cols] = jnp.where(core == 0, high, low).astype(jnp.bfloat16)


def project(where, x, w):
    return pl.pallas_call(
        project_kernel,
        out_shape=(
            jax.ShapeDtypeStruct((2, DEV_ROWS, HALF), jnp.float32),
            jax.ShapeDtypeStruct((2, DEV_ROWS, HALF), jnp.bfloat16),
        ),
        in_specs=[spec(SMEM)] + [spec(VMEM)] * 2,
        out_specs=(spec(VMEM), spec(VMEM)),
        compiler_params=pltpu.CompilerParams(vmem_limit_bytes=24 * 2**20),
        cost_estimate=pl.CostEstimate(flops=810_000_000, bytes_accessed=5_000_000, transcendentals=0),
        name="project",
    )(where, x, w)


def split3(x):
    terms = []
    for _ in range(3):
        terms.append(x.astype(jnp.bfloat16))
        x = x - terms[-1].astype(jnp.float32)
    return terms


def prepare_kernel(where_ref, residual_ref, mod_ref, fw_ref, there_ref, side_ref):
    me = where_ref[1]
    cols = pl.ds(pl.multiple_of((1 - me) * HALF, HD), HALF)
    there_ref[:DEV_ROWS] = residual_ref[:, cols]
    terms = split3(mod_ref[:, cols])
    terms.append(jnp.zeros((7, HALF), jnp.bfloat16))
    there_ref[DEV_ROWS:] = jnp.concatenate([term.astype(jnp.float32) for term in terms]).astype(jnp.bfloat16)
    fw = fw_ref[...].astype(jnp.float32)
    sign = jnp.where(lax.broadcasted_iota(jnp.int32, (1, WIDTH), 1) < HALF, 1.0, -1.0)
    tilt = jnp.sum(fw * ((1.0 + mod_ref[2:3]) * sign), axis=1, keepdims=True)
    offset = jnp.sum(fw * mod_ref[1:2], axis=1, keepdims=True)
    lane = lax.broadcasted_iota(jnp.int32, (64, HD), 1)
    side = jnp.where(lane == 0, tilt, jnp.where(lane == 1, offset, 0.0))
    side_ref[:32] = jnp.where(me == 0, side[:32], side[32:])
    side_ref[32:] = jnp.where(me == 0, side[32:], side[:32])


def prepare(where, residual, mod, fw):
    return pl.pallas_call(
        prepare_kernel,
        out_shape=(
            jax.ShapeDtypeStruct((DEV_ROWS + 16, HALF), jnp.bfloat16),
            jax.ShapeDtypeStruct((64, HD), jnp.float32),
        ),
        in_specs=[spec(SMEM)] + [spec(VMEM)] * 3,
        out_specs=(spec(VMEM), spec(VMEM)),
        compiler_params=pltpu.CompilerParams(vmem_limit_bytes=16 * 2**20),
        name="prepare",
    )(where, residual, mod, fw)


def norm_kernel(where_ref, keep_ref, came_ref, residual_ref, other_ref, mod_ref, fw_ref, side_ref, own_ref, send_ref):
    me = where_ref[1]
    cols = pl.ds(pl.multiple_of(me * HALF, HD), HALF)
    own = residual_ref[:, cols].astype(jnp.float32)
    other = other_ref[:DEV_ROWS].astype(jnp.float32)
    mod_own = mod_ref[:, cols]
    tail = other_ref[DEV_ROWS:].astype(jnp.float32)
    mod_other = tail[0:3] + tail[3:6] + tail[6:9]
    lane = lax.broadcasted_iota(jnp.int32, (DEV_ROWS, HD), 1)
    scaled, stats = [], []
    for b in range(2):
        mod = jnp.where(me == b, mod_own, mod_other)
        attn_out = (keep_ref[b] + came_ref[b].astype(jnp.float32)).astype(jnp.bfloat16).astype(jnp.float32)
        stream = jnp.where(me == b, own, other) + mod[0:1] * attn_out
        mean = jnp.mean(stream, axis=1, keepdims=True)
        centered = stream - mean
        spread = jnp.sum(centered * centered, axis=1, keepdims=True)
        scaled.append((centered * (1.0 + mod[2:3])).astype(jnp.bfloat16))
        stats.append(jnp.where(lane == 0, mean, jnp.where(lane == 1, spread, 0.0)))
    sums = lax.dot_general(fw_ref[:, cols], jnp.concatenate(scaled), NT, preferred_element_type=jnp.float32)
    stats = jnp.concatenate(stats).T[:8]
    own_ref[:32] = jnp.where(me == 0, sums[:32], sums[32:])
    send_ref[:32] = jnp.where(me == 0, sums[32:], sums[:32])
    own_ref[32:40] = stats
    send_ref[32:40] = stats
    own_ref[40:] = side_ref[:32]
    send_ref[40:] = side_ref[32:]


def norm(where, *arrays):
    shape = jax.ShapeDtypeStruct((72, HD), jnp.float32)
    return pl.pallas_call(
        norm_kernel,
        out_shape=(shape, shape),
        in_specs=[spec(SMEM)] + [spec(VMEM)] * 7,
        out_specs=(spec(VMEM), spec(VMEM)),
        compiler_params=pltpu.CompilerParams(vmem_limit_bytes=16 * 2**20),
        name="norm",
    )(where, *arrays)


def finish_kernel(where_ref, time_ref, own_ref, came_ref, noisy_ref, out_ref):
    me = where_ref[1]
    ours = (lax.broadcasted_iota(jnp.int32, (32, HD), 1) < DEV_ROWS) == (me == 0)
    tilt = jnp.where(ours, own_ref[40:, 0:1], came_ref[40:, 0:1])
    offset = jnp.where(ours, own_ref[40:, 1:2], came_ref[40:, 1:2])
    gap = 0.5 * (own_ref[32:33] - came_ref[32:33])
    gap = jnp.where(me == 0, gap, -gap)
    var = (own_ref[33:34] + came_ref[33:34]) / WIDTH + gap * gap
    prediction = (own_ref[:32] + came_ref[:32] + gap * tilt) / jnp.sqrt(var + EPS) + offset
    conditional, unconditional = prediction[:, :DEV_ROWS], pltpu.roll(prediction, DEV_ROWS, 1)[:, :DEV_ROWS]
    guided = unconditional + GUIDE * (conditional - unconditional)
    progress = 1.0 - time_ref[0].astype(jnp.float32) / STEPS
    sigma = SHIFT * progress / (1.0 + (SHIFT - 1.0) * progress)
    out_ref[...] = noisy_ref[...] - sigma * guided


def finish(where, timestep, own, came, noisy):
    return pl.pallas_call(
        finish_kernel,
        out_shape=jax.ShapeDtypeStruct((32, DEV_ROWS), jnp.float32),
        in_specs=[spec(SMEM)] * 2 + [spec(VMEM)] * 3,
        out_specs=spec(VMEM),
        compiler_params=pltpu.CompilerParams(vmem_limit_bytes=16 * 2**20),
        name="finish",
    )(where, timestep, own, came, noisy)


SWAP = [(0, 1), (1, 0)]


def spread_pairs():
    pairs = []
    for c in range(2):
        for y in range(8):
            for k in range(2):
                for l in range(2):
                    source = ((c * 8 + y) * 2 + k) * 2 + l
                    target = (((y // 4) * 8 + (y % 4) * 2 + k) * 2 + l) * 2 + c
                    pairs.append((source, target))
    return pairs


def tie(*arrays):
    return lax.optimization_barrier(arrays)


def shards(qkv, residual, out_weight, final_weight, modulation, frames, timestep, noisy):
    branch = lax.axis_index("c")
    where = jnp.stack([lax.axis_index("k"), branch, lax.axis_index("l")]).astype(jnp.int32)
    fw = final_weight.T

    block = lax.ppermute(out_weight.T, ("c", "y", "k", "l"), spread_pairs())
    packed, block = tie(pack(qkv[0, :, 0]), block)
    unit = lax.all_to_all(jnp.broadcast_to(block, (8, 192, HD)), "y", 0, 0, tiled=True).reshape(HALF, HD)
    weight = lax.all_gather(unit, "z", axis=0, tiled=False)

    gathered = lax.all_to_all(packed, ("y", "k"), 0, 0, tiled=True)
    there, sides = prepare(where, residual[0, 0], modulation[0], fw)
    there, unit = tie(there, unit)
    other = lax.ppermute(there, "c", SWAP)

    gathered, other = tie(gathered, other)
    heads = attend(frames[0], gathered)
    rows = lax.all_to_all(heads.reshape(16, 128, HD), ("c", "y"), 0, 0, tiled=True).reshape(2, 8, 128, HD)
    keep, send = project(where, rows, weight)
    came = lax.ppermute(send, "k", SWAP)
    sums, partner_sums = norm(where, keep, came, residual[0, 0], other, modulation[0], fw, sides)
    came_sums = lax.ppermute(partner_sums, "c", SWAP)
    return finish(where, timestep, sums, came_sums, noisy[0].T).T[None]


def solution(mesh):
    fine = Mesh(mesh.devices.reshape(2, 8, 2, 2, 8), ("c", "y", "k", "l", "z"))
    seq, req = ("y", "k"), ("l", "z")
    return jax.shard_map(
        shards,
        mesh=fine,
        in_specs=(
            P("c", None, req, seq, None),
            P("c", req, seq, None),
            P(req, seq),
            P(),
            P("c", None, None),
            P(req, None),
            P(),
            P(req, seq, "c"),
        ),
        out_specs=P(req, seq, "c"),
        check_vma=False,
    )
```

time: 127 us -> 113 us (0.89)
  starting transfers between devices: 36.9 us -> 20.2 us
  blocking collectives: 27.1 us -> 42.3 us
  waiting for transfers between devices: 30.5 us -> 23 us
  local copies, waits for them, and re-layouts: 5.43 us -> 1.98 us
  other arithmetic: 2.82 us -> 0.08 us
  Pallas kernels: 8.73 us -> 10.1 us
    all_to_all x0 -> x2, blocking collectives: none -> 42.3 us  [the longest x1 23.8 us: shards(): lax.all_to_all(jnp.broadcast_to(block, (8, 192, HD)), 'y', 0, 0, tiled=True)]
    all_gather x1 -> x0, blocking collectives: 27.1 us -> none  [gather_weight(): unit = lax.all_gather(block, 'y', axis=0, tiled=True)]
    all_to_all x1 -> x0, waiting for transfers between devices: 12 us -> none  [shards(): lax.all_to_all(heads.reshape(16, 128, HD), ('c', 'y'), 0, 0, tiled=True)]
    all_to_all x1 -> x0, starting transfers between devices: 6.53 us -> none  [shards(): lax.all_to_all(heads.reshape(16, 128, HD), ('c', 'y'), 0, 0, tiled=True)]
    all_to_all x1, starting transfers between devices: 10.6 us -> 5.06 us  [shards(): gathered = lax.all_to_all(packed, ('y', 'k'), 0, 0, tiled=True)]
    ppermute x5 -> x4, waiting for transfers between devices: 6.52 us -> 11.9 us  [the longest x1 7.66 us: shards(): other = lax.ppermute(there, 'c', SWAP)]
    ppermute x5 -> x4, starting transfers between devices: 19.7 us -> 15.1 us  [the longest x1 4.73 us: shards(): block = lax.ppermute(out_weight.T, ('c', 'y', 'k', 'l'), spread_pairs())]
    pallas_call x1 -> x3, Pallas kernels: 1.35 us -> 3.25 us  [the longest x1 1.31 us: finish(): pl.pallas_call(finish_kernel, out_shape=jax.ShapeDtypeStruct((32, DEV_ROW...]
  transfers between devices with their start and end apart: 8 -> 6, of which waited for: 5 -> 4; matrix products, arithmetic and copies ran while one was open for 4% -> 0% of each run, Pallas kernels for 6% -> 5%
where the time goes in v3:
time: 113 us; the launch traced here: 112 us
  blocking collectives  42.3 us (37%)
  waiting for transfers between devices  23 us (20%)
  starting transfers between devices  20.2 us (18%)
  between operations  14.1 us (12%)
  Pallas kernels  10.1 us (9%)
  local copies, waits for them, and re-layouts  1.98 us (2%)
    all_to_all x1, blocking collectives, shards(): lax.all_to_all(jnp.broadcast_to(block, (8, 192, HD)), 'y', 0, 0, tiled=True)  23.8 us
    all_to_all x1, blocking collectives, shards(): lax.all_to_all(heads.reshape(16, 128, HD), ('c', 'y'), 0, 0, tiled=True)  18.5 us
    all_to_all x1, waiting for transfers between devices, shards(): gathered = lax.all_to_all(packed, ('y', 'k'), 0, 0, tiled=True)  11.1 us
    ppermute x1, waiting for transfers between devices, shards(): other = lax.ppermute(there, 'c', SWAP)  7.66 us
    all_to_all x1, starting transfers between devices, shards(): gathered = lax.all_to_all(packed, ('y', 'k'), 0, 0, tiled=True)  5.06 us
    ppermute x1, starting transfers between devices, shards(): block = lax.ppermute(out_weight.T, ('c', 'y', 'k', 'l'), spread_pairs())  4.73 us
    ppermute x1, starting transfers between devices, shards(): came = lax.ppermute(send, 'k', SWAP)  4.65 us
    ppermute x1, starting transfers between devices, shards(): other = lax.ppermute(there, 'c', SWAP)  3.05 us
  transfers between devices with their start and end apart: 6, of which 4 were waited for; matrix products, arithmetic and copies ran while one was open for 0% of the time, Pallas kernels for 5%

profile of v3, /device:TPU:1, one launch (start us, length us, event | category | flops | bytes accessed | tf_op | source)
XLA Modules:
  0.0 111.8 jit_solution(13866511360924809716)
XLA Ops:
  6.5 0.0 all-gather.2.cloned.1.call-start
  6.6 4.7 %collective-permute-start = (bf16[192,128]{1,0:T(8,128)(2,1)}, bf16[192,128]{1,0:T(8,128)(2,1)S(1)}, u32[]{:S(2)}, u32[]{:S(2)}) collective-permute-start(bf16[192,128]{1,0:T(8,128)(2,1)} %bitcast.32), channel_id=1, source_target_pairs={{0,0},{8,16},{16,32},{24,48},{32,64},{40,80},{48,96},{56,112},{64,... | collective-permute-start | bytes 147464 | tf_op jit(solution)/shard_map/ppermute | solution.py:258
  11.3 2.2 %pack.1 = bf16[16,3,64,128]{3,2,1,0:T(8,128)(2,1)} custom-call(bf16[3,64,2048]{2,1,0:T(8,128)(2,1)} %bitcast.31), custom_call_target="tpu_custom_call" | custom-call | tf_op jit(solution)/shard_map/pack/pallas_call | solution.py:41
  13.5 0.0 collective-permute-done
  13.5 0.1 broadcast_in_dim.6
  13.6 23.8 %all_to_all.15 = bf16[8,192,128]{2,1,0:T(8,128)(2,1)} all-to-all(bf16[8,192,128]{2,1,0:T(8,128)(2,1)S(1)} %broadcast_in_dim.6), channel_id=1, replica_groups=mesh['c'=2,'y'=8,'k'=2,'l'=2,'z'=8] {'y'}, dimensions={0} | all-to-all | bytes 786432 | tf_op jit(solution)/shard_map/all_to_all | solution.py:260
  37.3 0.0 all-gather.2.cloned.1.call-update
  37.4 5.1 %all-to-all-start = ((bf16[16,3,64,128]{3,2,1,0:T(8,128)(2,1)}), bf16[16,3,64,128]{3,2,1,0:T(8,128)(2,1)S(1)}, u32[]{:S(2)}, u32[]{:S(2)}) async-start(bf16[16,3,64,128]{3,2,1,0:T(8,128)(2,1)} %pack.1), calls=%async_computation | async-start | bytes 1572864 | tf_op jit(solution)/shard_map/all_to_all | solution.py:263
  42.4 0.1 pad_add_fusion.where_ref
  42.5 0.8 prepare.1
  43.3 3.0 %collective-permute-start.1 = (bf16[80,1536]{1,0:T(8,128)(2,1)S(1)}, bf16[80,1536]{1,0:T(8,128)(2,1)S(1)}, u32[]{:S(2)}, u32[]{:S(2)}) collective-permute-start(bf16[80,1536]{1,0:T(8,128)(2,1)S(1)} %get-tuple-element.16), channel_id=1, source_target_pairs={{0,256},{256,0},{1,257},{257,1},{2,258},{258,2},{3,259},{259,3},{4... | collective-permute-start | bytes 737288 | tf_op jit(solution)/shard_map/ppermute | solution.py:266
  46.4 7.7 %collective-permute-done.1.other_ref = bf16[80,1536]{1,0:T(8,128)(2,1)S(1)} collective-permute-done((bf16[80,1536]{1,0:T(8,128)(2,1)S(1)}, bf16[80,1536]{1,0:T(8,128)(2,1)S(1)}, u32[]{:S(2)}, u32[]{:S(2)}) %collective-permute-start.1) | collective-permute-done | bytes 245792 | tf_op jit(solution)/shard_map/ppermute | solution.py:266
  54.0 11.1 %all-to-all-done.x_ref = bf16[16,3,64,128]{3,2,1,0:T(8,128)(2,1)S(1)} async-done(((bf16[16,3,64,128]{3,2,1,0:T(8,128)(2,1)}), bf16[16,3,64,128]{3,2,1,0:T(8,128)(2,1)S(1)}, u32[]{:S(2)}, u32[]{:S(2)}) %all-to-all-start) | async-done | bytes 786464 | tf_op jit(solution)/shard_map/all_to_all | solution.py:263
  65.1 2.9 %attend.1 = bf16[2,8,128,128]{3,2,1,0:T(8,128)(2,1)S(1)} custom-call(s32[8]{0:T(128)S(1)} %bitcast.29, bf16[16,3,64,128]{3,2,1,0:T(8,128)(2,1)S(1)} %all-to-all-done.x_ref), custom_call_target="tpu_custom_call" | custom-call | flops 540000000 | bytes 2000000 | tf_op jit(solution)/shard_map/attend/pallas_call | solution.py:86
  68.0 0.0 copy-start.3
  68.0 18.5 %all_to_all.16 = bf16[16,128,128]{2,1,0:T(8,128)(2,1)S(1)} all-to-all(bf16[16,128,128]{2,1,0:T(8,128)(2,1)S(1)} %bitcast.25), channel_id=1, replica_groups=mesh['c'=2,'y'=8,'k'=2,'l'=2,'z'=8] {'c','y'}, dimensions={0} | all-to-all | bytes 1048576 | tf_op jit(solution)/shard_map/all_to_all | solution.py:270
  86.5 1.9 %copy-done = bf16[8,1536,128]{2,1,0:T(8,128)(2,1)S(1)} copy-done((bf16[8,1536,128]{2,1,0:T(8,128)(2,1)S(1)}, bf16[8,1536,128]{2,1,0:T(8,128)(2,1)}, u32[]{:S(2)}) %copy-start) | copy-done | bytes 3145752
  88.4 1.8 %project.1 = (f32[2,64,1536]{2,1,0:T(8,128)S(1)}, bf16[2,64,1536]{2,1,0:T(8,128)(2,1)S(1)}) custom-call(s32[3]{0:T(128)S(1)} %pad_add_fusion.where_ref, bf16[2,8,128,128]{3,2,1,0:T(8,128)(2,1)S(1)} %bitcast.20, bf16[8,1536,128]{2,1,0:T(8,128)(2,1)S(1)} %copy-done), custom_call_target="tpu_custom_call" | custom-call | flops 810000000 | bytes 5000000 | tf_op jit(solution)/shard_map/project/pallas_call | solution.py:113
  90.2 4.6 %collective-permute-start.2 = (bf16[2,64,1536]{2,1,0:T(8,128)(2,1)S(1)}, bf16[2,64,1536]{2,1,0:T(8,128)(2,1)S(1)}, u32[]{:S(2)}, u32[]{:S(2)}) collective-permute-start(bf16[2,64,1536]{2,1,0:T(8,128)(2,1)S(1)} %get-tuple-element.20), channel_id=1, source_target_pairs={{0,16},{16,0},{1,17},{17,1},{2,18},{18,2},{3,19},{19,3},{4,20},{20... | collective-permute-start | bytes 1179656 | tf_op jit(solution)/shard_map/ppermute | solution.py:272
  94.9 1.3 %collective-permute-done.2.came_ref = bf16[2,64,1536]{2,1,0:T(8,128)(2,1)S(1)} collective-permute-done((bf16[2,64,1536]{2,1,0:T(8,128)(2,1)S(1)}, bf16[2,64,1536]{2,1,0:T(8,128)(2,1)S(1)}, u32[]{:S(2)}, u32[]{:S(2)}) %collective-permute-start.2) | collective-permute-done | bytes 393248 | tf_op jit(solution)/shard_map/ppermute | solution.py:272
  96.2 1.2 %norm.1 = (f32[72,128]{1,0:T(8,128)S(1)}, f32[72,128]{1,0:T(8,128)S(1)}) custom-call(s32[3]{0:T(128)S(1)} %pad_add_fusion.where_ref, f32[2,64,1536]{2,1,0:T(8,128)S(1)} %get-tuple-element.19.keep_ref, bf16[2,64,1536]{2,1,0:T(8,128)(2,1)S(1)} %collective-permute-done.2.came_ref, bf16[64,3072]{1,0:T(8,128)(2,1)S(1)} %bitcast.22, ...), custom_call_target="tpu_custom_call" | custom-call | tf_op jit(solution)/shard_map/norm/pallas_call | solution.py:197
  97.4 2.6 %collective-permute-start.3 = (f32[72,128]{1,0:T(8,128)S(1)}, f32[72,128]{1,0:T(8,128)S(1)}, u32[]{:S(2)}, u32[]{:S(2)}) collective-permute-start(f32[72,128]{1,0:T(8,128)S(1)} %get-tuple-element.24), channel_id=1, source_target_pairs={{0,256},{256,0},{1,257},{257,1},{2,258},{258,2},{3,259},{259,3},{4... | collective-permute-start | bytes 110600 | tf_op jit(solution)/shard_map/ppermute | solution.py:274
  100.7 2.9 %collective-permute-done.3.came_ref = f32[72,128]{1,0:T(8,128)S(1)} collective-permute-done((f32[72,128]{1,0:T(8,128)S(1)}, f32[72,128]{1,0:T(8,128)S(1)}, u32[]{:S(2)}, u32[]{:S(2)}) %collective-permute-start.3) | collective-permute-done | bytes 36896 | tf_op jit(solution)/shard_map/ppermute | solution.py:274
  103.6 1.3 %finish.1 = f32[32,64]{1,0:T(8,128)} custom-call(s32[3]{0:T(128)S(1)} %pad_add_fusion.where_ref, s32[1]{0:T(128)S(6)} %copy.12.time_ref, f32[72,128]{1,0:T(8,128)S(1)} %get-tuple-element.23.own_ref, f32[72,128]{1,0:T(8,128)S(1)} %collective-permute-done.3.came_ref, f32[32,64]{1,0:T(8,128)S(1)} %bitcast.28), custom_call_target="tpu_custom_call" | custom-call | tf_op jit(solution)/shard_map/finish/pallas_call | solution.py:224
  (12 shorter events, 0.0 us)
Async XLA Ops:
  6.5 35.9 %copy-start.5 = (f32[1,3,3072]{2,0,1:T(1,128)S(1)}, f32[1,3,3072]{2,0,1:T(1,128)}, u32[]{:S(2)}) copy-start(f32[1,3,3072]{2,0,1:T(1,128)} %param.12) | copy-start | bytes 110596
  6.5 36.0 %copy-start.1 = (bf16[1,1,64,3072]{3,2,1,0:T(8,128)(2,1)S(1)}, bf16[1,1,64,3072]{3,2,1,0:T(8,128)(2,1)}, u32[]{:S(2)}) copy-start(bf16[1,1,64,3072]{3,2,1,0:T(8,128)(2,1)} %param.9) | copy-start | bytes 1179652
  6.5 36.0 %copy-start.2 = (bf16[3072,64]{0,1:T(8,128)(2,1)S(1)}, bf16[3072,64]{0,1:T(8,128)(2,1)}, u32[]{:S(2)}) copy-start(bf16[3072,64]{0,1:T(8,128)(2,1)} %param.11) | copy-start | bytes 1179652
  6.5 58.6 %copy-start.4 = (s32[1,8]{1,0:T(1,128)S(1)}, s32[1,8]{1,0:T(1,128)}, u32[]{:S(2)}) copy-start(s32[1,8]{1,0:T(1,128)} %param.13) | copy-start | bytes 100
  6.5 80.0 %all-gather.2.cloned.1.call-start = ((), (), s32[]{:S(2)}) async-start(), calls=%async_computation.3 | async-start | bytes 3538944 | tf_op jit(solution)/shard_map/all_gather | solution.py:261
  6.6 6.9 %collective-permute-start = (bf16[192,128]{1,0:T(8,128)(2,1)}, bf16[192,128]{1,0:T(8,128)(2,1)S(1)}, u32[]{:S(2)}, u32[]{:S(2)}) collective-permute-start(bf16[192,128]{1,0:T(8,128)(2,1)} %bitcast.32), channel_id=1, source_target_pairs={{0,0},{8,16},{16,32},{24,48},{32,64},{40,80},{48,96},{56,112},{64,... | collective-permute-start | bytes 147464 | tf_op jit(solution)/shard_map/ppermute | solution.py:258
  37.4 27.8 %all-to-all-start = ((bf16[16,3,64,128]{3,2,1,0:T(8,128)(2,1)}), bf16[16,3,64,128]{3,2,1,0:T(8,128)(2,1)S(1)}, u32[]{:S(2)}, u32[]{:S(2)}) async-start(bf16[16,3,64,128]{3,2,1,0:T(8,128)(2,1)} %pack.1), calls=%async_computation | async-start | bytes 1572864 | tf_op jit(solution)/shard_map/all_to_all | solution.py:263
  43.3 10.7 %collective-permute-start.1 = (bf16[80,1536]{1,0:T(8,128)(2,1)S(1)}, bf16[80,1536]{1,0:T(8,128)(2,1)S(1)}, u32[]{:S(2)}, u32[]{:S(2)}) collective-permute-start(bf16[80,1536]{1,0:T(8,128)(2,1)S(1)} %get-tuple-element.16), channel_id=1, source_target_pairs={{0,256},{256,0},{1,257},{257,1},{2,258},{258,2},{3,259},{259,3},{4... | collective-permute-start | bytes 737288 | tf_op jit(solution)/shard_map/ppermute | solution.py:266
  68.0 35.6 %copy-start.3 = (f32[1,64,32]{1,2,0:T(8,128)S(1)}, f32[1,64,32]{1,2,0:T(8,128)}, u32[]{:S(2)}) copy-start(f32[1,64,32]{1,2,0:T(8,128)} %param.15) | copy-start | bytes 24580
  86.5 1.9 %copy-start = (bf16[8,1536,128]{2,1,0:T(8,128)(2,1)S(1)}, bf16[8,1536,128]{2,1,0:T(8,128)(2,1)}, u32[]{:S(2)}) copy-start(bf16[8,1536,128]{2,1,0:T(8,128)(2,1)} %all-gather.2.cloned.1.call-done.w_ref) | copy-start | bytes 9437188
  90.2 6.0 %collective-permute-start.2 = (bf16[2,64,1536]{2,1,0:T(8,128)(2,1)S(1)}, bf16[2,64,1536]{2,1,0:T(8,128)(2,1)S(1)}, u32[]{:S(2)}, u32[]{:S(2)}) collective-permute-start(bf16[2,64,1536]{2,1,0:T(8,128)(2,1)S(1)} %get-tuple-element.20), channel_id=1, source_target_pairs={{0,16},{16,0},{1,17},{17,1},{2,18},{18,2},{3,19},{19,3},{4,20},{20... | collective-permute-start | bytes 1179656 | tf_op jit(solution)/shard_map/ppermute | solution.py:272
  97.4 6.2 %collective-permute-start.3 = (f32[72,128]{1,0:T(8,128)S(1)}, f32[72,128]{1,0:T(8,128)S(1)}, u32[]{:S(2)}, u32[]{:S(2)}) collective-permute-start(f32[72,128]{1,0:T(8,128)S(1)} %get-tuple-element.24), channel_id=1, source_target_pairs={{0,256},{256,0},{1,257},{257,1},{2,258},{258,2},{3,259},{259,3},{4... | collective-permute-start | bytes 110600 | tf_op jit(solution)/shard_map/ppermute | solution.py:274
Sparse Core Ops, SparseCore 0:
  37.5 48.7 all-gather.1

commit v4 on v3

--- a/solution.py
+++ b/solution.py
@@ -94,13 +94,21 @@
     )(frames, gathered)
 
 
-def project_kernel(where_ref, x_ref, w_ref, keep_ref, send_ref):
-    core = where_ref[0]
-    x = jnp.concatenate([x_ref[:, h].reshape(256, HD) for h in range(8)], axis=1)
+def project_kernel(where_ref, x_ref, *refs):
+    units, (keep_ref, send_ref, *buffers, arrived) = refs[:4], refs[4:]
+    copies = [pltpu.make_async_copy(unit, buffer, arrived.at[i]) for i, (unit, buffer) in enumerate(zip(units, buffers))]
+    for copy in copies:
+        copy.start()
+    core, z = where_ref[0], where_ref[2]
+    sign = (2 * lax.rem(z, 2) - 1) * (1 - 2 * core)
+    heads = [lax.rem(z + offset * sign + 8, 8) for offset in (0, -1, 1, 2, -2, -3, 3, 4)]
+    x = jnp.concatenate([x_ref[:, h].reshape(256, HD) for h in heads], axis=1)
+    for copy in copies:
+        copy.wait()
     tile = 384
     for t in range(HALF // tile):
         cols = slice(t * tile, (t + 1) * tile)
-        w = jnp.concatenate([w_ref[h, cols] for h in range(8)], axis=1)
+        w = jnp.concatenate([buffers[i // 2][i % 2, cols] for i in range(8)], axis=1)
         part = lax.dot_general(x, w, NT, preferred_element_type=jnp.float32)
         for b in range(2):
             low = part[b * 128 : b * 128 + 64]
@@ -109,19 +117,20 @@
             send_ref[b, :, cols] = jnp.where(core == 0, high, low).astype(jnp.bfloat16)
 
 
-def project(where, x, w):
+def project(where, x, units):
     return pl.pallas_call(
         project_kernel,
         out_shape=(
             jax.ShapeDtypeStruct((2, DEV_ROWS, HALF), jnp.float32),
             jax.ShapeDtypeStruct((2, DEV_ROWS, HALF), jnp.bfloat16),
         ),
-        in_specs=[spec(SMEM)] + [spec(VMEM)] * 2,
+        in_specs=[spec(SMEM), spec(VMEM)] + [spec(pl.ANY)] * 4,
         out_specs=(spec(VMEM), spec(VMEM)),
+        scratch_shapes=[VMEM((2, HALF, HD), jnp.bfloat16)] * 4 + [pltpu.SemaphoreType.DMA((4,))],
         compiler_params=pltpu.CompilerParams(vmem_limit_bytes=24 * 2**20),
         cost_estimate=pl.CostEstimate(flops=810_000_000, bytes_accessed=5_000_000, transcendentals=0),
         name="project",
-    )(where, x, w)
+    )(where, x, *units)
 
 
 def split3(x):
@@ -132,15 +141,25 @@
     return terms
 
 
-def prepare_kernel(where_ref, residual_ref, mod_ref, fw_ref, there_ref, side_ref):
+def blocks_of(array, branch):
+    even, odd = [
+        jnp.concatenate([array[:, (2 * i + k) * 192 : (2 * i + k + 1) * 192] for i in range(8)], axis=1) for k in range(2)
+    ]
+    return jnp.where(branch == 0, even, odd)
+
+
+def prepare_kernel(where_ref, residual_ref, mod_ref, fw_ref, own_ref, there_ref, mod_half_ref, fw_half_ref, side_ref):
     me = where_ref[1]
-    cols = pl.ds(pl.multiple_of((1 - me) * HALF, HD), HALF)
-    there_ref[:DEV_ROWS] = residual_ref[:, cols]
-    terms = split3(mod_ref[:, cols])
+    residual = residual_ref[...].astype(jnp.float32)
+    own_ref[...] = blocks_of(residual, me).astype(jnp.bfloat16)
+    mod_half_ref[...] = blocks_of(mod_ref[...], me)
+    fw_half_ref[...] = blocks_of(fw_ref[...].astype(jnp.float32), me).astype(jnp.bfloat16)
+    there_ref[:DEV_ROWS] = blocks_of(residual, 1 - me).astype(jnp.bfloat16)
+    terms = split3(blocks_of(mod_ref[...], 1 - me))
     terms.append(jnp.zeros((7, HALF), jnp.bfloat16))
     there_ref[DEV_ROWS:] = jnp.concatenate([term.astype(jnp.float32) for term in terms]).astype(jnp.bfloat16)
     fw = fw_ref[...].astype(jnp.float32)
-    sign = jnp.where(lax.broadcasted_iota(jnp.int32, (1, WIDTH), 1) < HALF, 1.0, -1.0)
+    sign = jnp.where(lax.rem(lax.broadcasted_iota(jnp.int32, (1, WIDTH), 1) // 192, 2) == 0, 1.0, -1.0)
     tilt = jnp.sum(fw * ((1.0 + mod_ref[2:3]) * sign), axis=1, keepdims=True)
     offset = jnp.sum(fw * mod_ref[1:2], axis=1, keepdims=True)
     lane = lax.broadcasted_iota(jnp.int32, (64, HD), 1)
@@ -153,24 +172,25 @@
     return pl.pallas_call(
         prepare_kernel,
         out_shape=(
+            jax.ShapeDtypeStruct((DEV_ROWS, HALF), jnp.bfloat16),
             jax.ShapeDtypeStruct((DEV_ROWS + 16, HALF), jnp.bfloat16),
+            jax.ShapeDtypeStruct((3, HALF), jnp.float32),
+            jax.ShapeDtypeStruct((64, HALF), jnp.bfloat16),
             jax.ShapeDtypeStruct((64, HD), jnp.float32),
         ),
         in_specs=[spec(SMEM)] + [spec(VMEM)] * 3,
-        out_specs=(spec(VMEM), spec(VMEM)),
+        out_specs=(spec(VMEM),) * 5,
         compiler_params=pltpu.CompilerParams(vmem_limit_bytes=16 * 2**20),
         name="prepare",
     )(where, residual, mod, fw)
 
 
-def norm_kernel(where_ref, keep_ref, came_ref, residual_ref, other_ref, mod_ref, fw_ref, side_ref, own_ref, send_ref):
+def norm_kernel(where_ref, keep_ref, came_ref, own_ref, other_ref, mod_ref, fw_ref, side_ref, sums_ref, send_ref):
     me = where_ref[1]
-    cols = pl.ds(pl.multiple_of(me * HALF, HD), HALF)
-    own = residual_ref[:, cols].astype(jnp.float32)
+    own = own_ref[...].astype(jnp.float32)
     other = other_ref[:DEV_ROWS].astype(jnp.float32)
-    mod_own = mod_ref[:, cols]
     tail = other_ref[DEV_ROWS:].astype(jnp.float32)
-    mod_other = tail[0:3] + tail[3:6] + tail[6:9]
+    mod_own, mod_other = mod_ref[...], tail[0:3] + tail[3:6] + tail[6:9]
     lane = lax.broadcasted_iota(jnp.int32, (DEV_ROWS, HD), 1)
     scaled, stats = [], []
     for b in range(2):
@@ -182,13 +202,13 @@
         spread = jnp.sum(centered * centered, axis=1, keepdims=True)
         scaled.append((centered * (1.0 + mod[2:3])).astype(jnp.bfloat16))
         stats.append(jnp.where(lane == 0, mean, jnp.where(lane == 1, spread, 0.0)))
-    sums = lax.dot_general(fw_ref[:, cols], jnp.concatenate(scaled), NT, preferred_element_type=jnp.float32)
+    sums = lax.dot_general(fw_ref[...], jnp.concatenate(scaled), NT, preferred_element_type=jnp.float32)
     stats = jnp.concatenate(stats).T[:8]
-    own_ref[:32] = jnp.where(me == 0, sums[:32], sums[32:])
+    sums_ref[:32] = jnp.where(me == 0, sums[:32], sums[32:])
     send_ref[:32] = jnp.where(me == 0, sums[32:], sums[:32])
-    own_ref[32:40] = stats
+    sums_ref[32:40] = stats
     send_ref[32:40] = stats
-    own_ref[40:] = side_ref[:32]
+    sums_ref[40:] = side_ref[:32]
     send_ref[40:] = side_ref[32:]
 
 
@@ -232,17 +252,17 @@
 
 
 SWAP = [(0, 1), (1, 0)]
+EVEN = [(i, i ^ 1) for i in range(8)]
+ODD = [(i, ((i ^ 1) + (2 if i % 2 else -2)) % 8) for i in range(8)]
+CORES = [EVEN + [(8 + i, 8 + j) for i, j in ODD], ODD + [(8 + i, 8 + j) for i, j in EVEN]]
 
 
 def spread_pairs():
     pairs = []
     for c in range(2):
-        for y in range(8):
-            for k in range(2):
-                for l in range(2):
-                    source = ((c * 8 + y) * 2 + k) * 2 + l
-                    target = (((y // 4) * 8 + (y % 4) * 2 + k) * 2 + l) * 2 + c
-                    pairs.append((source, target))
+        for k in range(2):
+            for l in range(2):
+                pairs.append(((c * 2 + k) * 2 + l, (k * 2 + l) * 2 + c))
     return pairs
 
 
@@ -252,25 +272,31 @@
 
 def shards(qkv, residual, out_weight, final_weight, modulation, frames, timestep, noisy):
     branch = lax.axis_index("c")
-    where = jnp.stack([lax.axis_index("k"), branch, lax.axis_index("l")]).astype(jnp.int32)
+    where = jnp.stack([lax.axis_index("k"), branch, lax.axis_index("z")]).astype(jnp.int32)
     fw = final_weight.T
 
-    block = lax.ppermute(out_weight.T, ("c", "y", "k", "l"), spread_pairs())
+    block = lax.ppermute(out_weight.T, ("c", "k", "l"), spread_pairs())
     packed, block = tie(pack(qkv[0, :, 0]), block)
     unit = lax.all_to_all(jnp.broadcast_to(block, (8, 192, HD)), "y", 0, 0, tiled=True).reshape(HALF, HD)
-    weight = lax.all_gather(unit, "z", axis=0, tiled=False)
-
     gathered = lax.all_to_all(packed, ("y", "k"), 0, 0, tiled=True)
-    there, sides = prepare(where, residual[0, 0], modulation[0], fw)
-    there, unit = tie(there, unit)
+
+    residual_rows, _ = tie(residual[0, 0], block)
+    own, there, mod_half, fw_half, sides = prepare(where, residual_rows, modulation[0], fw)
     other = lax.ppermute(there, "c", SWAP)
-
-    gathered, other = tie(gathered, other)
+    unit, other = tie(unit, other)
+
+    units = [jnp.stack([unit, lax.ppermute(unit, ("k", "z"), CORES[0])])]
+    units.append(lax.ppermute(units[0], ("k", "z"), CORES[1]))
     heads = attend(frames[0], gathered)
+    heads, latest = tie(heads, units[1])
+    for step in (0, 1):
+        latest = lax.ppermute(latest, ("k", "z"), CORES[step])
+        units.append(latest)
     rows = lax.all_to_all(heads.reshape(16, 128, HD), ("c", "y"), 0, 0, tiled=True).reshape(2, 8, 128, HD)
-    keep, send = project(where, rows, weight)
+
+    keep, send = project(where, rows, units)
     came = lax.ppermute(send, "k", SWAP)
-    sums, partner_sums = norm(where, keep, came, residual[0, 0], other, modulation[0], fw, sides)
+    sums, partner_sums = norm(where, keep, came, own, other, mod_half, fw_half, sides)
     came_sums = lax.ppermute(partner_sums, "c", SWAP)
     return finish(where, timestep, sums, came_sums, noisy[0].T).T[None]
 

time: 113 us -> 111 us (0.982)
  blocking collectives: 42.3 us -> 0 us
  starting transfers between devices: 20.2 us -> 52.4 us
  waiting for transfers between devices: 23 us -> 41.1 us
  between operations: 14.1 us -> 0.78 us
  Pallas kernels: 10.1 us -> 12.5 us
    all_to_all x2 -> x0, blocking collectives: 42.3 us -> none  [the longest x1 23.8 us: shards(): lax.all_to_all(jnp.broadcast_to(block, (8, 192, HD)), 'y', 0, 0, tiled=True)]
    all_to_all x0 -> x2, waiting for transfers between devices: none -> 23.3 us  [the longest x1 14 us: shards(): lax.all_to_all(heads.reshape(16, 128, HD), ('c', 'y'), 0, 0, tiled=True)]
    ppermute x1 -> x5, starting transfers between devices: 4.73 us -> 25.2 us  [the longest x2 8.72 us: shards(): latest = lax.ppermute(latest, ('k', 'z'), CORES[step])]
    all_to_all x0 -> x2, starting transfers between devices: none -> 15 us  [the longest x1 8.04 us: shards(): lax.all_to_all(heads.reshape(16, 128, HD), ('c', 'y'), 0, 0, tiled=True)]
    ppermute x1, waiting for transfers between devices: 7.66 us -> 0.01 us  [shards(): other = lax.ppermute(there, 'c', SWAP)]
    ppermute x1 -> x5, waiting for transfers between devices: 0.01 us -> 7.5 us  [the longest x1 5.45 us: shards(): units = [jnp.stack([unit, lax.ppermute(unit, ('k', 'z'), CORES[0])])]]
    all_to_all x1, waiting for transfers between devices: 11.1 us -> 6.71 us  [shards(): gathered = lax.all_to_all(packed, ('y', 'k'), 0, 0, tiled=True)]
    ppermute x1, starting transfers between devices: 4.65 us -> 2.3 us  [shards(): came = lax.ppermute(send, 'k', SWAP)]
  transfers between devices with their start and end apart: 6 -> 11, of which waited for: 4 -> 8; matrix products, arithmetic and copies ran while one was open for 0% -> 0% of each run, Pallas kernels for 5% -> 6%
where the time goes in v4:
time: 111 us; the launch traced here: 110 us
  starting transfers between devices  52.4 us (47%)
  waiting for transfers between devices  41.1 us (37%)
  Pallas kernels  12.5 us (11%)
  local copies, waits for them, and re-layouts  2.61 us (2%)
    all_to_all x1, waiting for transfers between devices, shards(): lax.all_to_all(heads.reshape(16, 128, HD), ('c', 'y'), 0, 0, tiled=True)  14 us
    all_to_all x1, waiting for transfers between devices, shards(): lax.all_to_all(jnp.broadcast_to(block, (8, 192, HD)), 'y', 0, 0, tiled=True)  9.33 us
    ppermute x2, starting transfers between devices, shards(): latest = lax.ppermute(latest, ('k', 'z'), CORES[step])  8.72 us
    ppermute x1, starting transfers between devices, shards(): units = [jnp.stack([unit, lax.ppermute(unit, ('k', 'z'), CORES[0])])]  8.52 us
    all_to_all x1, starting transfers between devices, shards(): lax.all_to_all(heads.reshape(16, 128, HD), ('c', 'y'), 0, 0, tiled=True)  8.04 us
    all_to_all x1, starting transfers between devices, shards(): lax.all_to_all(jnp.broadcast_to(block, (8, 192, HD)), 'y', 0, 0, tiled=True)  6.95 us
    all_to_all x1, waiting for transfers between devices, shards(): gathered = lax.all_to_all(packed, ('y', 'k'), 0, 0, tiled=True)  6.71 us
    ppermute x1, starting transfers between devices, shards(): block = lax.ppermute(out_weight.T, ('c', 'k', 'l'), spread_pairs())  6.03 us
  transfers between devices with their start and end apart: 11, of which 8 were waited for; matrix products, arithmetic and copies ran while one was open for 0% of the time, Pallas kernels for 6%

profile of v4, /device:TPU:1, one launch (start us, length us, event | category | flops | bytes accessed | tf_op | source)
XLA Modules:
  0.0 109.6 jit_solution(7322826898190522499)
XLA Ops:
  0.0 6.0 %collective-permute-start = (bf16[192,128]{1,0:T(8,128)(2,1)}, bf16[192,128]{1,0:T(8,128)(2,1)S(1)}, u32[]{:S(2)}, u32[]{:S(2)}) collective-permute-start(bf16[192,128]{1,0:T(8,128)(2,1)} %bitcast.32), channel_id=1, source_target_pairs={{0,0},{8,16},{16,256},{24,272},{256,8},{264,24},{272,264},{280,280... | collective-permute-start | bytes 147464 | tf_op jit(solution)/shard_map/ppermute | solution.py:278
  6.0 2.2 %pack.1 = bf16[16,3,64,128]{3,2,1,0:T(8,128)(2,1)} custom-call(bf16[3,64,2048]{2,1,0:T(8,128)(2,1)} %bitcast.30), custom_call_target="tpu_custom_call" | custom-call | tf_op jit(solution)/shard_map/pack/pallas_call | solution.py:41
  9.0 7.0 %all-to-all-start.1 = ((bf16[8,192,128]{2,1,0:T(8,128)(2,1)}), bf16[8,192,128]{2,1,0:T(8,128)(2,1)S(1)}, u32[]{:S(2)}, u32[]{:S(2)}) async-start(bf16[8,192,128]{2,1,0:T(8,128)(2,1)} %broadcast_in_dim.6), calls=%async_computation.1 | async-start | bytes 786432 | tf_op jit(solution)/shard_map/all_to_all | solution.py:280
  16.6 1.1 %prepare.1 = (bf16[64,1536]{1,0:T(8,128)(2,1)S(1)}, bf16[80,1536]{1,0:T(8,128)(2,1)S(1)}, f32[3,1536]{1,0:T(4,128)S(1)}, bf16[64,1536]{1,0:T(8,128)(2,1)S(1)}, f32[64,128]{1,0:T(8,128)S(1)}) custom-call(s32[3]{0:T(128)S(1)} %pad_add_fusion.where_ref, bf16[64,3072]{1,0:T(8,128)(2,1)S(1)} %bitcast.23, f32[3,3072]{1,0:T(4,128)S(1)} %bitcast.25, ...), custom_call_target="tpu_custom_call" | custom-call | tf_op jit(solution)/shard_map/prepare/pallas_call | solution.py:172
  18.3 2.8 %collective-permute-start.1 = (bf16[80,1536]{1,0:T(8,128)(2,1)S(1)}, bf16[80,1536]{1,0:T(8,128)(2,1)S(1)}, u32[]{:S(2)}, u32[]{:S(2)}) collective-permute-start(bf16[80,1536]{1,0:T(8,128)(2,1)S(1)} %get-tuple-element.24), channel_id=1, source_target_pairs={{0,256},{256,0},{1,257},{257,1},{2,258},{258,2},{3,259},{259,3},{4... | collective-permute-start | bytes 737288 | tf_op jit(solution)/shard_map/ppermute | solution.py:285
  21.1 9.3 %all-to-all-done.1 = bf16[8,192,128]{2,1,0:T(8,128)(2,1)S(1)} async-done(((bf16[8,192,128]{2,1,0:T(8,128)(2,1)}), bf16[8,192,128]{2,1,0:T(8,128)(2,1)S(1)}, u32[]{:S(2)}, u32[]{:S(2)}) %all-to-all-start.1) | async-done | bytes 393248 | tf_op jit(solution)/shard_map/all_to_all | solution.py:280
  30.4 3.8 %all-to-all-start = ((bf16[16,3,64,128]{3,2,1,0:T(8,128)(2,1)}), bf16[16,3,64,128]{3,2,1,0:T(8,128)(2,1)S(1)}, u32[]{:S(2)}, u32[]{:S(2)}) async-start(bf16[16,3,64,128]{3,2,1,0:T(8,128)(2,1)} %pack.1), calls=%async_computation | async-start | bytes 1572864 | tf_op jit(solution)/shard_map/all_to_all | solution.py:281
  34.2 8.5 %collective-permute-start.2 = (bf16[1536,128]{1,0:T(8,128)(2,1)S(1)}, bf16[1536,128]{1,0:T(8,128)(2,1)S(1)}, u32[]{:S(2)}, u32[]{:S(2)}) collective-permute-start(bf16[1536,128]{1,0:T(8,128)(2,1)S(1)} %bitcast.28), channel_id=1, source_target_pairs={{0,1},{1,0},{2,3},{3,2},{4,5},{5,4},{6,7},{7,6},{16,23},{17,18},{1... | collective-permute-start | bytes 1179656 | tf_op jit(solution)/shard_map/ppermute | solution.py:288
  42.8 5.4 %collective-permute-done.2 = bf16[1536,128]{1,0:T(8,128)(2,1)S(1)} collective-permute-done((bf16[1536,128]{1,0:T(8,128)(2,1)S(1)}, bf16[1536,128]{1,0:T(8,128)(2,1)S(1)}, u32[]{:S(2)}, u32[]{:S(2)}) %collective-permute-start.2) | collective-permute-done | bytes 393248 | tf_op jit(solution)/shard_map/ppermute | solution.py:288
  48.3 1.9 %collective-permute-start.3 = (bf16[2,1536,128]{2,1,0:T(8,128)(2,1)S(1)}, bf16[2,1536,128]{2,1,0:T(8,128)(2,1)S(1)}, u32[]{:S(2)}, u32[]{:S(2)}) collective-permute-start(bf16[2,1536,128]{2,1,0:T(8,128)(2,1)S(1)} %pad_maximum_fusion.refs_0_), channel_id=1, source_target_pairs={{0,7},{1,2},{2,1},{3,4},{4,3},{5,6},{6,5},{7,0},{16,17},{17,16},{1... | collective-permute-start | bytes 2359304 | tf_op jit(solution)/shard_map/ppermute | solution.py:289
  50.2 6.7 %all-to-all-done.x_ref = bf16[16,3,64,128]{3,2,1,0:T(8,128)(2,1)S(1)} async-done(((bf16[16,3,64,128]{3,2,1,0:T(8,128)(2,1)}), bf16[16,3,64,128]{3,2,1,0:T(8,128)(2,1)S(1)}, u32[]{:S(2)}, u32[]{:S(2)}) %all-to-all-start) | async-done | bytes 786464 | tf_op jit(solution)/shard_map/all_to_all | solution.py:281
  56.9 3.7 %attend.1 = bf16[2,8,128,128]{3,2,1,0:T(8,128)(2,1)} custom-call(s32[8]{0:T(128)S(1)} %bitcast.27, bf16[16,3,64,128]{3,2,1,0:T(8,128)(2,1)S(1)} %all-to-all-done.x_ref), custom_call_target="tpu_custom_call" | custom-call | flops 540000000 | bytes 2000000 | tf_op jit(solution)/shard_map/attend/pallas_call | solution.py:86
  61.3 6.8 %collective-permute-start.4 = (bf16[2,1536,128]{2,1,0:T(8,128)(2,1)S(1)}, bf16[2,1536,128]{2,1,0:T(8,128)(2,1)S(1)}, u32[]{:S(2)}, u32[]{:S(2)}) collective-permute-start(bf16[2,1536,128]{2,1,0:T(8,128)(2,1)S(1)} %collective-permute-done.3.refs_1_), channel_id=1, source_target_pairs={{0,1},{1,0},{2,3},{3,2},{4,5},{5,4},{6,7},{7,6},{16,23},{17,18},{1... | collective-permute-start | bytes 2359304 | tf_op jit(solution)/shard_map/ppermute | solution.py:293
  68.2 8.0 %all-to-all-start.2 = ((bf16[16,128,128]{2,1,0:T(8,128)(2,1)}), bf16[16,128,128]{2,1,0:T(8,128)(2,1)S(1)}, u32[]{:S(2)}, u32[]{:S(2)}) async-start(bf16[16,128,128]{2,1,0:T(8,128)(2,1)} %bitcast.11), calls=%async_computation.2 | async-start | bytes 1048576 | tf_op jit(solution)/shard_map/all_to_all | solution.py:295
  76.2 1.3 %collective-permute-done.4.refs_2_ = bf16[2,1536,128]{2,1,0:T(8,128)(2,1)S(1)} collective-permute-done((bf16[2,1536,128]{2,1,0:T(8,128)(2,1)S(1)}, bf16[2,1536,128]{2,1,0:T(8,128)(2,1)S(1)}, u32[]{:S(2)}, u32[]{:S(2)}) %collective-permute-start.4) | collective-permute-done | bytes 786464 | tf_op jit(solution)/shard_map/ppermute | solution.py:293
  77.5 1.9 %collective-permute-start.5 = (bf16[2,1536,128]{2,1,0:T(8,128)(2,1)S(1)}, bf16[2,1536,128]{2,1,0:T(8,128)(2,1)}, u32[]{:S(2)}, u32[]{:S(2)}) collective-permute-start(bf16[2,1536,128]{2,1,0:T(8,128)(2,1)S(1)} %collective-permute-done.4.refs_2_), channel_id=1, source_target_pairs={{0,7},{1,2},{2,1},{3,4},{4,3},{5,6},{6,5},{7,0},{16,17},{17,16},{1... | collective-permute-start | bytes 2359304 | tf_op jit(solution)/shard_map/ppermute | solution.py:293
  79.4 14.0 %all-to-all-done.2 = bf16[16,128,128]{2,1,0:T(8,128)(2,1)S(1)} async-done(((bf16[16,128,128]{2,1,0:T(8,128)(2,1)}), bf16[16,128,128]{2,1,0:T(8,128)(2,1)S(1)}, u32[]{:S(2)}, u32[]{:S(2)}) %all-to-all-start.2) | async-done | bytes 524320 | tf_op jit(solution)/shard_map/all_to_all | solution.py:295
  94.1 3.1 %project.1 = (f32[2,64,1536]{2,1,0:T(8,128)S(1)}, bf16[2,64,1536]{2,1,0:T(8,128)(2,1)S(1)}) custom-call(s32[3]{0:T(128)S(1)} %copy-done.6, bf16[2,8,128,128]{3,2,1,0:T(8,128)(2,1)S(1)} %bitcast.22, bf16[2,1536,128]{2,1,0:T(8,128)(2,1)S(1)} %pad_maximum_fusion.refs_0_, bf16[2,1536,128]{2,1,0:T(8,128)(2,1)S(1)} %collective-permute-done.3.refs_1_, ...), custom_call_target="tpu_custom_call" | custom-call | flops 810000000 | bytes 5000000 | tf_op jit(solution)/shard_map/project/pallas_call | solution.py:121
  97.2 2.3 %collective-permute-start.6 = (bf16[2,64,1536]{2,1,0:T(8,128)(2,1)S(1)}, bf16[2,64,1536]{2,1,0:T(8,128)(2,1)S(1)}, u32[]{:S(2)}, u32[]{:S(2)}) collective-permute-start(bf16[2,64,1536]{2,1,0:T(8,128)(2,1)S(1)} %get-tuple-element.29), channel_id=1, source_target_pairs={{0,16},{16,0},{1,17},{17,1},{2,18},{18,2},{3,19},{19,3},{4,20},{20... | collective-permute-start | bytes 1179656 | tf_op jit(solution)/shard_map/ppermute | solution.py:298
  99.6 1.3 %collective-permute-done.6.came_ref = bf16[2,64,1536]{2,1,0:T(8,128)(2,1)S(1)} collective-permute-done((bf16[2,64,1536]{2,1,0:T(8,128)(2,1)S(1)}, bf16[2,64,1536]{2,1,0:T(8,128)(2,1)S(1)}, u32[]{:S(2)}, u32[]{:S(2)}) %collective-permute-start.6) | collective-permute-done | bytes 393248 | tf_op jit(solution)/shard_map/ppermute | solution.py:298
  100.9 1.2 %norm.1 = (f32[72,128]{1,0:T(8,128)S(1)}, f32[72,128]{1,0:T(8,128)S(1)}) custom-call(s32[3]{0:T(128)S(1)} %copy-done.6, f32[2,64,1536]{2,1,0:T(8,128)S(1)} %get-tuple-element.28.keep_ref, bf16[2,64,1536]{2,1,0:T(8,128)(2,1)S(1)} %collective-permute-done.6.came_ref, bf16[64,1536]{1,0:T(8,128)(2,1)S(1)} %get-tuple-element.30.own_ref, ...), custom_call_target="tpu_custom_call" | custom-call | tf_op jit(solution)/shard_map/norm/pallas_call | solution.py:217
  102.0 3.3 %collective-permute-start.7 = (f32[72,128]{1,0:T(8,128)S(1)}, f32[72,128]{1,0:T(8,128)S(1)}, u32[]{:S(2)}, u32[]{:S(2)}) collective-permute-start(f32[72,128]{1,0:T(8,128)S(1)} %get-tuple-element.36), channel_id=1, source_target_pairs={{0,256},{256,0},{1,257},{257,1},{2,258},{258,2},{3,259},{259,3},{4... | collective-permute-start | bytes 110600 | tf_op jit(solution)/shard_map/ppermute | solution.py:300
  106.0 2.3 %collective-permute-done.7.came_ref = f32[72,128]{1,0:T(8,128)S(1)} collective-permute-done((f32[72,128]{1,0:T(8,128)S(1)}, f32[72,128]{1,0:T(8,128)S(1)}, u32[]{:S(2)}, u32[]{:S(2)}) %collective-permute-start.7) | collective-permute-done | bytes 36896 | tf_op jit(solution)/shard_map/ppermute | solution.py:300
  108.3 1.3 %finish.1 = f32[32,64]{1,0:T(8,128)} custom-call(s32[3]{0:T(128)S(1)} %copy-done.6, s32[1]{0:T(128)S(6)} %copy.12.time_ref, f32[72,128]{1,0:T(8,128)S(1)} %get-tuple-element.35.own_ref, f32[72,128]{1,0:T(8,128)S(1)} %collective-permute-done.7.came_ref, f32[32,64]{1,0:T(8,128)S(1)} %bitcast.26), custom_call_target="tpu_custom_call" | custom-call | tf_op jit(solution)/shard_map/finish/pallas_call | solution.py:244
  (26 shorter events, 3.5 us)
Async XLA Ops:
  0.0 8.2 %collective-permute-start = (bf16[192,128]{1,0:T(8,128)(2,1)}, bf16[192,128]{1,0:T(8,128)(2,1)S(1)}, u32[]{:S(2)}, u32[]{:S(2)}) collective-permute-start(bf16[192,128]{1,0:T(8,128)(2,1)} %bitcast.32), channel_id=1, source_target_pairs={{0,0},{8,16},{16,256},{24,272},{256,8},{264,24},{272,264},{280,280... | collective-permute-start | bytes 147464 | tf_op jit(solution)/shard_map/ppermute | solution.py:278
  8.2 7.8 %copy-start.8 = (f32[1,3,3072]{2,0,1:T(1,128)S(1)}, f32[1,3,3072]{2,0,1:T(1,128)}, u32[]{:S(2)}) copy-start(f32[1,3,3072]{2,0,1:T(1,128)} %param.12) | copy-start | bytes 110596
  9.0 7.6 %copy-start = (bf16[1,1,64,3072]{3,2,1,0:T(8,128)(2,1)S(1)}, bf16[1,1,64,3072]{3,2,1,0:T(8,128)(2,1)}, u32[]{:S(2)}) copy-start(bf16[1,1,64,3072]{3,2,1,0:T(8,128)(2,1)} %param.9) | copy-start | bytes 1179652
  9.0 7.6 %copy-start.1 = (bf16[3072,64]{0,1:T(8,128)(2,1)S(1)}, bf16[3072,64]{0,1:T(8,128)(2,1)}, u32[]{:S(2)}) copy-start(bf16[3072,64]{0,1:T(8,128)(2,1)} %param.11) | copy-start | bytes 1179652
  9.0 21.4 %all-to-all-start.1 = ((bf16[8,192,128]{2,1,0:T(8,128)(2,1)}), bf16[8,192,128]{2,1,0:T(8,128)(2,1)S(1)}, u32[]{:S(2)}, u32[]{:S(2)}) async-start(bf16[8,192,128]{2,1,0:T(8,128)(2,1)} %broadcast_in_dim.6), calls=%async_computation.1 | async-start | bytes 786432 | tf_op jit(solution)/shard_map/all_to_all | solution.py:280
  16.1 0.5 copy-start.5
  17.7 0.6 copy-start.2
  18.3 15.9 %collective-permute-start.1 = (bf16[80,1536]{1,0:T(8,128)(2,1)S(1)}, bf16[80,1536]{1,0:T(8,128)(2,1)S(1)}, u32[]{:S(2)}, u32[]{:S(2)}) collective-permute-start(bf16[80,1536]{1,0:T(8,128)(2,1)S(1)} %get-tuple-element.24), channel_id=1, source_target_pairs={{0,256},{256,0},{1,257},{257,1},{2,258},{258,2},{3,259},{259,3},{4... | collective-permute-start | bytes 737288 | tf_op jit(solution)/shard_map/ppermute | solution.py:285
  30.4 26.5 %all-to-all-start = ((bf16[16,3,64,128]{3,2,1,0:T(8,128)(2,1)}), bf16[16,3,64,128]{3,2,1,0:T(8,128)(2,1)S(1)}, u32[]{:S(2)}, u32[]{:S(2)}) async-start(bf16[16,3,64,128]{3,2,1,0:T(8,128)(2,1)} %pack.1), calls=%async_computation | async-start | bytes 1572864 | tf_op jit(solution)/shard_map/all_to_all | solution.py:281
  34.2 14.0 %collective-permute-start.2 = (bf16[1536,128]{1,0:T(8,128)(2,1)S(1)}, bf16[1536,128]{1,0:T(8,128)(2,1)S(1)}, u32[]{:S(2)}, u32[]{:S(2)}) collective-permute-start(bf16[1536,128]{1,0:T(8,128)(2,1)S(1)} %bitcast.28), channel_id=1, source_target_pairs={{0,1},{1,0},{2,3},{3,2},{4,5},{5,4},{6,7},{7,6},{16,23},{17,18},{1... | collective-permute-start | bytes 1179656 | tf_op jit(solution)/shard_map/ppermute | solution.py:288
  48.3 8.7 %copy-start.7 = (s32[1,8]{1,0:T(1,128)S(1)}, s32[1,8]{1,0:T(1,128)}, u32[]{:S(2)}) copy-start(s32[1,8]{1,0:T(1,128)} %param.13) | copy-start | bytes 100
  48.3 13.0 %collective-permute-start.3 = (bf16[2,1536,128]{2,1,0:T(8,128)(2,1)S(1)}, bf16[2,1536,128]{2,1,0:T(8,128)(2,1)S(1)}, u32[]{:S(2)}, u32[]{:S(2)}) collective-permute-start(bf16[2,1536,128]{2,1,0:T(8,128)(2,1)S(1)} %pad_maximum_fusion.refs_0_), channel_id=1, source_target_pairs={{0,7},{1,2},{2,1},{3,4},{4,3},{5,6},{6,5},{7,0},{16,17},{17,16},{1... | collective-permute-start | bytes 2359304 | tf_op jit(solution)/shard_map/ppermute | solution.py:289
  61.3 16.2 %collective-permute-start.4 = (bf16[2,1536,128]{2,1,0:T(8,128)(2,1)S(1)}, bf16[2,1536,128]{2,1,0:T(8,128)(2,1)S(1)}, u32[]{:S(2)}, u32[]{:S(2)}) collective-permute-start(bf16[2,1536,128]{2,1,0:T(8,128)(2,1)S(1)} %collective-permute-done.3.refs_1_), channel_id=1, source_target_pairs={{0,1},{1,0},{2,3},{3,2},{4,5},{5,4},{6,7},{7,6},{16,23},{17,18},{1... | collective-permute-start | bytes 2359304 | tf_op jit(solution)/shard_map/ppermute | solution.py:293
  68.2 25.3 %all-to-all-start.2 = ((bf16[16,128,128]{2,1,0:T(8,128)(2,1)}), bf16[16,128,128]{2,1,0:T(8,128)(2,1)S(1)}, u32[]{:S(2)}, u32[]{:S(2)}) async-start(bf16[16,128,128]{2,1,0:T(8,128)(2,1)} %bitcast.11), calls=%async_computation.2 | async-start | bytes 1048576 | tf_op jit(solution)/shard_map/all_to_all | solution.py:295
  77.5 15.9 %collective-permute-start.5 = (bf16[2,1536,128]{2,1,0:T(8,128)(2,1)S(1)}, bf16[2,1536,128]{2,1,0:T(8,128)(2,1)}, u32[]{:S(2)}, u32[]{:S(2)}) collective-permute-start(bf16[2,1536,128]{2,1,0:T(8,128)(2,1)S(1)} %collective-permute-done.4.refs_2_), channel_id=1, source_target_pairs={{0,7},{1,2},{2,1},{3,4},{4,3},{5,6},{6,5},{7,0},{16,17},{17,16},{1... | collective-permute-start | bytes 2359304 | tf_op jit(solution)/shard_map/ppermute | solution.py:293
  93.5 0.7 copy-start.6
  94.1 6.8 %copy-start.3 = (f32[3,1536]{1,0:T(4,128)S(1)}, f32[3,1536]{1,0:T(4,128)}, u32[]{:S(2)}) copy-start(f32[3,1536]{1,0:T(4,128)} %copy-done.2) | copy-start | bytes 55300
  97.2 3.6 %collective-permute-start.6 = (bf16[2,64,1536]{2,1,0:T(8,128)(2,1)S(1)}, bf16[2,64,1536]{2,1,0:T(8,128)(2,1)S(1)}, u32[]{:S(2)}, u32[]{:S(2)}) collective-permute-start(bf16[2,64,1536]{2,1,0:T(8,128)(2,1)S(1)} %get-tuple-element.29), channel_id=1, source_target_pairs={{0,16},{16,0},{1,17},{17,1},{2,18},{18,2},{3,19},{19,3},{4,20},{20... | collective-permute-start | bytes 1179656 | tf_op jit(solution)/shard_map/ppermute | solution.py:298
  100.9 7.4 %copy-start.4 = (f32[1,64,32]{1,2,0:T(8,128)S(1)}, f32[1,64,32]{1,2,0:T(8,128)}, u32[]{:S(2)}) copy-start(f32[1,64,32]{1,2,0:T(8,128)} %param.15) | copy-start | bytes 24580
  102.0 6.2 %collective-permute-start.7 = (f32[72,128]{1,0:T(8,128)S(1)}, f32[72,128]{1,0:T(8,128)S(1)}, u32[]{:S(2)}, u32[]{:S(2)}) collective-permute-start(f32[72,128]{1,0:T(8,128)S(1)} %get-tuple-element.36), channel_id=1, source_target_pairs={{0,256},{256,0},{1,257},{257,1},{2,258},{258,2},{3,259},{259,3},{4... | collective-permute-start | bytes 110600 | tf_op jit(solution)/shard_map/ppermute | solution.py:300

commit v5 on v4

--- a/solution.py
+++ b/solution.py
@@ -280,18 +280,17 @@
     unit = lax.all_to_all(jnp.broadcast_to(block, (8, 192, HD)), "y", 0, 0, tiled=True).reshape(HALF, HD)
     gathered = lax.all_to_all(packed, ("y", "k"), 0, 0, tiled=True)
 
-    residual_rows, _ = tie(residual[0, 0], block)
+    units = [jnp.stack([unit, lax.ppermute(unit, ("k", "z"), CORES[0])])]
+    residual_rows, _ = tie(residual[0, 0], units[0])
     own, there, mod_half, fw_half, sides = prepare(where, residual_rows, modulation[0], fw)
     other = lax.ppermute(there, "c", SWAP)
-    unit, other = tie(unit, other)
-
-    units = [jnp.stack([unit, lax.ppermute(unit, ("k", "z"), CORES[0])])]
     units.append(lax.ppermute(units[0], ("k", "z"), CORES[1]))
+    units[1], other = tie(units[1], other)
+    for step in (0, 1):
+        units.append(lax.ppermute(units[-1], ("k", "z"), CORES[step]))
+
+    gathered, _ = tie(gathered, units[0])
     heads = attend(frames[0], gathered)
-    heads, latest = tie(heads, units[1])
-    for step in (0, 1):
-        latest = lax.ppermute(latest, ("k", "z"), CORES[step])
-        units.append(latest)
     rows = lax.all_to_all(heads.reshape(16, 128, HD), ("c", "y"), 0, 0, tiled=True).reshape(2, 8, 128, HD)
 
     keep, send = project(where, rows, units)

time: 111 us -> 108 us (0.973)
  blocking collectives: 0 us -> 20.1 us
  waiting for transfers between devices: 41.1 us -> 25.6 us
  starting transfers between devices: 52.4 us -> 46 us
    all_to_all x0 -> x1, blocking collectives: none -> 20.1 us  [shards(): lax.all_to_all(jnp.broadcast_to(block, (8, 192, HD)), 'y', 0, 0, tiled=True)]
    all_to_all x1 -> x0, waiting for transfers between devices: 9.33 us -> none  [shards(): lax.all_to_all(jnp.broadcast_to(block, (8, 192, HD)), 'y', 0, 0, tiled=True)]
    all_to_all x1 -> x0, starting transfers between devices: 6.95 us -> none  [shards(): lax.all_to_all(jnp.broadcast_to(block, (8, 192, HD)), 'y', 0, 0, tiled=True)]
    all_to_all x1, waiting for transfers between devices: 6.71 us -> 0.01 us  [shards(): gathered = lax.all_to_all(packed, ('y', 'k'), 0, 0, tiled=True)]
    ppermute x1, waiting for transfers between devices: 0.01 us -> 6.53 us  [shards(): other = lax.ppermute(there, 'c', SWAP)]
    ppermute x1, waiting for transfers between devices: 5.45 us -> 1.62 us  [shards(): units = [jnp.stack([unit, lax.ppermute(unit, ('k', 'z'), CORES[0])])]]
    ppermute x2, waiting for transfers between devices: 1.32 us -> 0.01 us  [shards(): units.append(lax.ppermute(units[-1], ('k', 'z'), CORES[step]))]
    ppermute x1, starting transfers between devices: 8.52 us -> 9.8 us  [shards(): units = [jnp.stack([unit, lax.ppermute(unit, ('k', 'z'), CORES[0])])]]
  transfers between devices with their start and end apart: 11 -> 10, of which waited for: 8 -> 5; matrix products, arithmetic and copies ran while one was open for 0% -> 0% of each run, Pallas kernels for 6% -> 6%
where the time goes in v5:
time: 108 us; the launch traced here: 107 us
  starting transfers between devices  46 us (43%)
  waiting for transfers between devices  25.6 us (24%)
  blocking collectives  20.1 us (19%)
  Pallas kernels  11.7 us (11%)
  local copies, waits for them, and re-layouts  2.25 us (2%)
    all_to_all x1, blocking collectives, shards(): lax.all_to_all(jnp.broadcast_to(block, (8, 192, HD)), 'y', 0, 0, tiled=True)  20.1 us
    all_to_all x1, waiting for transfers between devices, shards(): lax.all_to_all(heads.reshape(16, 128, HD), ('c', 'y'), 0, 0, tiled=True)  14.2 us
    ppermute x1, starting transfers between devices, shards(): units = [jnp.stack([unit, lax.ppermute(unit, ('k', 'z'), CORES[0])])]  9.8 us
    ppermute x2, starting transfers between devices, shards(): units.append(lax.ppermute(units[-1], ('k', 'z'), CORES[step]))  8.89 us
    all_to_all x1, starting transfers between devices, shards(): lax.all_to_all(heads.reshape(16, 128, HD), ('c', 'y'), 0, 0, tiled=True)  7.74 us
    ppermute x1, waiting for transfers between devices, shards(): other = lax.ppermute(there, 'c', SWAP)  6.53 us
    ppermute x1, starting transfers between devices, shards(): block = lax.ppermute(out_weight.T, ('c', 'k', 'l'), spread_pairs())  6.03 us
    ppermute x1, starting transfers between devices, shards(): came_sums = lax.ppermute(partner_sums, 'c', SWAP)  3.99 us
  transfers between devices with their start and end apart: 10, of which 5 were waited for; matrix products, arithmetic and copies ran while one was open for 0% of the time, Pallas kernels for 6%

profile of v5, /device:TPU:1, one launch (start us, length us, event | category | flops | bytes accessed | tf_op | source)
XLA Modules:
  0.0 106.6 jit_solution(634347526308094106)
XLA Ops:
  0.0 6.0 %collective-permute-start = (bf16[192,128]{1,0:T(8,128)(2,1)}, bf16[192,128]{1,0:T(8,128)(2,1)S(1)}, u32[]{:S(2)}, u32[]{:S(2)}) collective-permute-start(bf16[192,128]{1,0:T(8,128)(2,1)} %bitcast.33), channel_id=1, source_target_pairs={{0,0},{8,16},{16,256},{24,272},{256,8},{264,24},{272,264},{280,280... | collective-permute-start | bytes 147464 | tf_op jit(solution)/shard_map/ppermute | solution.py:278
  6.0 2.2 %pack.1 = bf16[16,3,64,128]{3,2,1,0:T(8,128)(2,1)} custom-call(bf16[3,64,2048]{2,1,0:T(8,128)(2,1)} %bitcast.31), custom_call_target="tpu_custom_call" | custom-call | tf_op jit(solution)/shard_map/pack/pallas_call | solution.py:41
  8.3 20.1 %all_to_all.15 = bf16[8,192,128]{2,1,0:T(8,128)(2,1)S(1)} all-to-all(bf16[8,192,128]{2,1,0:T(8,128)(2,1)S(1)} %broadcast_in_dim.6), channel_id=1, replica_groups=mesh['c'=2,'y'=8,'k'=2,'l'=2,'z'=8] {'y'}, dimensions={0} | all-to-all | bytes 786432 | tf_op jit(solution)/shard_map/all_to_all | solution.py:280
  28.3 9.8 %collective-permute-start.1 = (bf16[1536,128]{1,0:T(8,128)(2,1)S(1)}, bf16[1536,128]{1,0:T(8,128)(2,1)S(1)}, u32[]{:S(2)}, u32[]{:S(2)}) collective-permute-start(bf16[1536,128]{1,0:T(8,128)(2,1)S(1)} %bitcast.29), channel_id=1, source_target_pairs={{0,1},{1,0},{2,3},{3,2},{4,5},{5,4},{6,7},{7,6},{16,23},{17,18},{1... | collective-permute-start | bytes 1179656 | tf_op jit(solution)/shard_map/ppermute | solution.py:283
  38.1 3.5 %all-to-all-start = ((bf16[16,3,64,128]{3,2,1,0:T(8,128)(2,1)}), bf16[16,3,64,128]{3,2,1,0:T(8,128)(2,1)S(1)}, u32[]{:S(2)}, u32[]{:S(2)}) async-start(bf16[16,3,64,128]{3,2,1,0:T(8,128)(2,1)} %pack.1), calls=%async_computation | async-start | bytes 1572864 | tf_op jit(solution)/shard_map/all_to_all | solution.py:281
  41.7 1.6 %collective-permute-done.1 = bf16[1536,128]{1,0:T(8,128)(2,1)S(1)} collective-permute-done((bf16[1536,128]{1,0:T(8,128)(2,1)S(1)}, bf16[1536,128]{1,0:T(8,128)(2,1)S(1)}, u32[]{:S(2)}, u32[]{:S(2)}) %collective-permute-start.1) | collective-permute-done | bytes 393248 | tf_op jit(solution)/shard_map/ppermute | solution.py:283
  43.4 2.1 %collective-permute-start.2 = (bf16[2,1536,128]{2,1,0:T(8,128)(2,1)S(1)}, bf16[2,1536,128]{2,1,0:T(8,128)(2,1)S(1)}, u32[]{:S(2)}, u32[]{:S(2)}) collective-permute-start(bf16[2,1536,128]{2,1,0:T(8,128)(2,1)S(1)} %pad_maximum_fusion.refs_0_), channel_id=1, source_target_pairs={{0,7},{1,2},{2,1},{3,4},{4,3},{5,6},{6,5},{7,0},{16,17},{17,16},{1... | collective-permute-start | bytes 2359304 | tf_op jit(solution)/shard_map/ppermute | solution.py:287
  45.6 1.1 %prepare.1 = (bf16[64,1536]{1,0:T(8,128)(2,1)S(1)}, bf16[80,1536]{1,0:T(8,128)(2,1)S(1)}, f32[3,1536]{1,0:T(4,128)S(1)}, bf16[64,1536]{1,0:T(8,128)(2,1)S(1)}, f32[64,128]{1,0:T(8,128)S(1)}) custom-call(s32[3]{0:T(128)S(1)} %pad_add_fusion.where_ref, bf16[64,3072]{1,0:T(8,128)(2,1)S(1)} %bitcast.24, f32[3,3072]{1,0:T(4,128)S(1)} %bitcast.26, ...), custom_call_target="tpu_custom_call" | custom-call | tf_op jit(solution)/shard_map/prepare/pallas_call | solution.py:172
  46.7 0.7 copy-done.3
  48.0 2.0 %collective-permute-start.3 = (bf16[80,1536]{1,0:T(8,128)(2,1)S(1)}, bf16[80,1536]{1,0:T(8,128)(2,1)S(1)}, u32[]{:S(2)}, u32[]{:S(2)}) collective-permute-start(bf16[80,1536]{1,0:T(8,128)(2,1)S(1)} %get-tuple-element.24), channel_id=1, source_target_pairs={{0,256},{256,0},{1,257},{257,1},{2,258},{258,2},{3,259},{259,3},{4... | collective-permute-start | bytes 737288 | tf_op jit(solution)/shard_map/ppermute | solution.py:286
  50.1 6.5 %collective-permute-done.3.other_ref = bf16[80,1536]{1,0:T(8,128)(2,1)S(1)} collective-permute-done((bf16[80,1536]{1,0:T(8,128)(2,1)S(1)}, bf16[80,1536]{1,0:T(8,128)(2,1)S(1)}, u32[]{:S(2)}, u32[]{:S(2)}) %collective-permute-start.3) | collective-permute-done | bytes 245792 | tf_op jit(solution)/shard_map/ppermute | solution.py:286
  56.6 7.0 %collective-permute-start.4 = (bf16[2,1536,128]{2,1,0:T(8,128)(2,1)S(1)}, bf16[2,1536,128]{2,1,0:T(8,128)(2,1)S(1)}, u32[]{:S(2)}, u32[]{:S(2)}) collective-permute-start(bf16[2,1536,128]{2,1,0:T(8,128)(2,1)S(1)} %collective-permute-done.2.refs_1_), channel_id=1, source_target_pairs={{0,1},{1,0},{2,3},{3,2},{4,5},{5,4},{6,7},{7,6},{16,23},{17,18},{1... | collective-permute-start | bytes 2359304 | tf_op jit(solution)/shard_map/ppermute | solution.py:290
  63.6 2.8 %attend.1 = bf16[2,8,128,128]{3,2,1,0:T(8,128)(2,1)S(1)} custom-call(s32[8]{0:T(128)S(1)} %bitcast.28, bf16[16,3,64,128]{3,2,1,0:T(8,128)(2,1)S(1)} %all-to-all-done.x_ref), custom_call_target="tpu_custom_call" | custom-call | flops 540000000 | bytes 2000000 | tf_op jit(solution)/shard_map/attend/pallas_call | solution.py:86
  66.5 0.8 copy-done
  67.3 7.7 %all-to-all-start.2 = ((bf16[16,128,128]{2,1,0:T(8,128)(2,1)}), bf16[16,128,128]{2,1,0:T(8,128)(2,1)S(1)}, u32[]{:S(2)}, u32[]{:S(2)}) async-start(bf16[16,128,128]{2,1,0:T(8,128)(2,1)} %bitcast.23), calls=%async_computation.2 | async-start | bytes 1048576 | tf_op jit(solution)/shard_map/all_to_all | solution.py:294
  75.0 1.9 %collective-permute-start.5 = (bf16[2,1536,128]{2,1,0:T(8,128)(2,1)S(1)}, bf16[2,1536,128]{2,1,0:T(8,128)(2,1)}, u32[]{:S(2)}, u32[]{:S(2)}) collective-permute-start(bf16[2,1536,128]{2,1,0:T(8,128)(2,1)S(1)} %collective-permute-done.4.refs_2_), channel_id=1, source_target_pairs={{0,7},{1,2},{2,1},{3,4},{4,3},{5,6},{6,5},{7,0},{16,17},{17,16},{1... | collective-permute-start | bytes 2359304 | tf_op jit(solution)/shard_map/ppermute | solution.py:290
  77.0 14.2 %all-to-all-done.2 = bf16[16,128,128]{2,1,0:T(8,128)(2,1)S(1)} async-done(((bf16[16,128,128]{2,1,0:T(8,128)(2,1)}), bf16[16,128,128]{2,1,0:T(8,128)(2,1)S(1)}, u32[]{:S(2)}, u32[]{:S(2)}) %all-to-all-start.2) | async-done | bytes 524320 | tf_op jit(solution)/shard_map/all_to_all | solution.py:294
  91.2 3.1 %project.1 = (f32[2,64,1536]{2,1,0:T(8,128)S(1)}, bf16[2,64,1536]{2,1,0:T(8,128)(2,1)S(1)}) custom-call(s32[3]{0:T(128)S(1)} %pad_add_fusion.where_ref, bf16[2,8,128,128]{3,2,1,0:T(8,128)(2,1)S(1)} %bitcast.22, bf16[2,1536,128]{2,1,0:T(8,128)(2,1)S(1)} %pad_maximum_fusion.refs_0_, bf16[2,1536,128]{2,1,0:T(8,128)(2,1)S(1)} %collective-permute-done.2.refs_1_, ...), custom_call_target="tpu_custom_call" | custom-call | flops 810000000 | bytes 5000000 | tf_op jit(solution)/shard_map/project/pallas_call | solution.py:121
  94.3 1.9 %collective-permute-start.6 = (bf16[2,64,1536]{2,1,0:T(8,128)(2,1)S(1)}, bf16[2,64,1536]{2,1,0:T(8,128)(2,1)S(1)}, u32[]{:S(2)}, u32[]{:S(2)}) collective-permute-start(bf16[2,64,1536]{2,1,0:T(8,128)(2,1)S(1)} %get-tuple-element.27), channel_id=1, source_target_pairs={{0,16},{16,0},{1,17},{17,1},{2,18},{18,2},{3,19},{19,3},{4,20},{20... | collective-permute-start | bytes 1179656 | tf_op jit(solution)/shard_map/ppermute | solution.py:297
  96.3 1.7 %collective-permute-done.6.came_ref = bf16[2,64,1536]{2,1,0:T(8,128)(2,1)S(1)} collective-permute-done((bf16[2,64,1536]{2,1,0:T(8,128)(2,1)S(1)}, bf16[2,64,1536]{2,1,0:T(8,128)(2,1)S(1)}, u32[]{:S(2)}, u32[]{:S(2)}) %collective-permute-start.6) | collective-permute-done | bytes 393248 | tf_op jit(solution)/shard_map/ppermute | solution.py:297
  97.9 1.2 %norm.1 = (f32[72,128]{1,0:T(8,128)S(1)}, f32[72,128]{1,0:T(8,128)S(1)}) custom-call(s32[3]{0:T(128)S(1)} %pad_add_fusion.where_ref, f32[2,64,1536]{2,1,0:T(8,128)S(1)} %get-tuple-element.26.keep_ref, bf16[2,64,1536]{2,1,0:T(8,128)(2,1)S(1)} %collective-permute-done.6.came_ref, bf16[64,1536]{1,0:T(8,128)(2,1)S(1)} %copy-done.4, ...), custom_call_target="tpu_custom_call" | custom-call | tf_op jit(solution)/shard_map/norm/pallas_call | solution.py:217
  99.1 4.0 %collective-permute-start.7 = (f32[72,128]{1,0:T(8,128)S(1)}, f32[72,128]{1,0:T(8,128)S(1)}, u32[]{:S(2)}, u32[]{:S(2)}) collective-permute-start(f32[72,128]{1,0:T(8,128)S(1)} %get-tuple-element.34), channel_id=1, source_target_pairs={{0,256},{256,0},{1,257},{257,1},{2,258},{258,2},{3,259},{259,3},{4... | collective-permute-start | bytes 110600 | tf_op jit(solution)/shard_map/ppermute | solution.py:299
  103.8 1.6 %collective-permute-done.7.came_ref = f32[72,128]{1,0:T(8,128)S(1)} collective-permute-done((f32[72,128]{1,0:T(8,128)S(1)}, f32[72,128]{1,0:T(8,128)S(1)}, u32[]{:S(2)}, u32[]{:S(2)}) %collective-permute-start.7) | collective-permute-done | bytes 36896 | tf_op jit(solution)/shard_map/ppermute | solution.py:299
  105.3 1.3 %finish.1 = f32[32,64]{1,0:T(8,128)} custom-call(s32[3]{0:T(128)S(1)} %pad_add_fusion.where_ref, s32[1]{0:T(128)S(6)} %copy.12.time_ref, f32[72,128]{1,0:T(8,128)S(1)} %get-tuple-element.33.own_ref, f32[72,128]{1,0:T(8,128)S(1)} %collective-permute-done.7.came_ref, f32[32,64]{1,0:T(8,128)S(1)} %bitcast.27), custom_call_target="tpu_custom_call" | custom-call | tf_op jit(solution)/shard_map/finish/pallas_call | solution.py:244
  (27 shorter events, 0.9 us)
Async XLA Ops:
  0.0 8.2 %collective-permute-start = (bf16[192,128]{1,0:T(8,128)(2,1)}, bf16[192,128]{1,0:T(8,128)(2,1)S(1)}, u32[]{:S(2)}, u32[]{:S(2)}) collective-permute-start(bf16[192,128]{1,0:T(8,128)(2,1)} %bitcast.33), channel_id=1, source_target_pairs={{0,0},{8,16},{16,256},{24,272},{256,8},{264,24},{272,264},{280,280... | collective-permute-start | bytes 147464 | tf_op jit(solution)/shard_map/ppermute | solution.py:278
  28.3 15.0 %collective-permute-start.1 = (bf16[1536,128]{1,0:T(8,128)(2,1)S(1)}, bf16[1536,128]{1,0:T(8,128)(2,1)S(1)}, u32[]{:S(2)}, u32[]{:S(2)}) collective-permute-start(bf16[1536,128]{1,0:T(8,128)(2,1)S(1)} %bitcast.29), channel_id=1, source_target_pairs={{0,1},{1,0},{2,3},{3,2},{4,5},{5,4},{6,7},{7,6},{16,23},{17,18},{1... | collective-permute-start | bytes 1179656 | tf_op jit(solution)/shard_map/ppermute | solution.py:283
  38.1 25.5 %all-to-all-start = ((bf16[16,3,64,128]{3,2,1,0:T(8,128)(2,1)}), bf16[16,3,64,128]{3,2,1,0:T(8,128)(2,1)S(1)}, u32[]{:S(2)}, u32[]{:S(2)}) async-start(bf16[16,3,64,128]{3,2,1,0:T(8,128)(2,1)} %pack.1), calls=%async_computation | async-start | bytes 1572864 | tf_op jit(solution)/shard_map/all_to_all | solution.py:281
  43.3 2.2 %copy-start.9 = (f32[1,3,3072]{2,0,1:T(1,128)S(1)}, f32[1,3,3072]{2,0,1:T(1,128)}, u32[]{:S(2)}) copy-start(f32[1,3,3072]{2,0,1:T(1,128)} %param.12) | copy-start | bytes 110596
  43.3 2.3 %copy-start.1 = (bf16[1,1,64,3072]{3,2,1,0:T(8,128)(2,1)S(1)}, bf16[1,1,64,3072]{3,2,1,0:T(8,128)(2,1)}, u32[]{:S(2)}) copy-start(bf16[1,1,64,3072]{3,2,1,0:T(8,128)(2,1)} %param.9) | copy-start | bytes 1179652
  43.3 2.3 %copy-start.2 = (bf16[3072,64]{0,1:T(8,128)(2,1)S(1)}, bf16[3072,64]{0,1:T(8,128)(2,1)}, u32[]{:S(2)}) copy-start(bf16[3072,64]{0,1:T(8,128)(2,1)} %param.11) | copy-start | bytes 1179652
  43.4 13.2 %collective-permute-start.2 = (bf16[2,1536,128]{2,1,0:T(8,128)(2,1)S(1)}, bf16[2,1536,128]{2,1,0:T(8,128)(2,1)S(1)}, u32[]{:S(2)}, u32[]{:S(2)}) collective-permute-start(bf16[2,1536,128]{2,1,0:T(8,128)(2,1)S(1)} %pad_maximum_fusion.refs_0_), channel_id=1, source_target_pairs={{0,7},{1,2},{2,1},{3,4},{4,3},{5,6},{6,5},{7,0},{16,17},{17,16},{1... | collective-permute-start | bytes 2359304 | tf_op jit(solution)/shard_map/ppermute | solution.py:287
  46.7 0.7 copy-start.3
  47.4 0.7 copy-start.5
  48.0 15.6 %copy-start.8 = (s32[1,8]{1,0:T(1,128)S(1)}, s32[1,8]{1,0:T(1,128)}, u32[]{:S(2)}) copy-start(s32[1,8]{1,0:T(1,128)} %param.13) | copy-start | bytes 100
  48.0 8.6 %collective-permute-start.3 = (bf16[80,1536]{1,0:T(8,128)(2,1)S(1)}, bf16[80,1536]{1,0:T(8,128)(2,1)S(1)}, u32[]{:S(2)}, u32[]{:S(2)}) collective-permute-start(bf16[80,1536]{1,0:T(8,128)(2,1)S(1)} %get-tuple-element.24), channel_id=1, source_target_pairs={{0,256},{256,0},{1,257},{257,1},{2,258},{258,2},{3,259},{259,3},{4... | collective-permute-start | bytes 737288 | tf_op jit(solution)/shard_map/ppermute | solution.py:286
  56.6 18.4 %collective-permute-start.4 = (bf16[2,1536,128]{2,1,0:T(8,128)(2,1)S(1)}, bf16[2,1536,128]{2,1,0:T(8,128)(2,1)S(1)}, u32[]{:S(2)}, u32[]{:S(2)}) collective-permute-start(bf16[2,1536,128]{2,1,0:T(8,128)(2,1)S(1)} %collective-permute-done.2.refs_1_), channel_id=1, source_target_pairs={{0,1},{1,0},{2,3},{3,2},{4,5},{5,4},{6,7},{7,6},{16,23},{17,18},{1... | collective-permute-start | bytes 2359304 | tf_op jit(solution)/shard_map/ppermute | solution.py:290
  66.5 0.8 copy-start
  67.3 23.9 %all-to-all-start.2 = ((bf16[16,128,128]{2,1,0:T(8,128)(2,1)}), bf16[16,128,128]{2,1,0:T(8,128)(2,1)S(1)}, u32[]{:S(2)}, u32[]{:S(2)}) async-start(bf16[16,128,128]{2,1,0:T(8,128)(2,1)} %bitcast.23), calls=%async_computation.2 | async-start | bytes 1048576 | tf_op jit(solution)/shard_map/all_to_all | solution.py:294
  75.0 16.2 %collective-permute-start.5 = (bf16[2,1536,128]{2,1,0:T(8,128)(2,1)S(1)}, bf16[2,1536,128]{2,1,0:T(8,128)(2,1)}, u32[]{:S(2)}, u32[]{:S(2)}) collective-permute-start(bf16[2,1536,128]{2,1,0:T(8,128)(2,1)S(1)} %collective-permute-done.4.refs_2_), channel_id=1, source_target_pairs={{0,7},{1,2},{2,1},{3,4},{4,3},{5,6},{6,5},{7,0},{16,17},{17,16},{1... | collective-permute-start | bytes 2359304 | tf_op jit(solution)/shard_map/ppermute | solution.py:290
  91.2 6.8 %copy-start.4 = (bf16[64,1536]{1,0:T(8,128)(2,1)S(1)}, bf16[64,1536]{1,0:T(8,128)(2,1)}, u32[]{:S(2)}) copy-start(bf16[64,1536]{1,0:T(8,128)(2,1)} %copy-done.3) | copy-start | bytes 589828
  91.2 6.8 %copy-start.6 = (bf16[64,1536]{1,0:T(8,128)(2,1)S(1)}, bf16[64,1536]{1,0:T(8,128)(2,1)}, u32[]{:S(2)}) copy-start(bf16[64,1536]{1,0:T(8,128)(2,1)} %copy-done.5) | copy-start | bytes 589828
  94.3 3.6 %collective-permute-start.6 = (bf16[2,64,1536]{2,1,0:T(8,128)(2,1)S(1)}, bf16[2,64,1536]{2,1,0:T(8,128)(2,1)S(1)}, u32[]{:S(2)}, u32[]{:S(2)}) collective-permute-start(bf16[2,64,1536]{2,1,0:T(8,128)(2,1)S(1)} %get-tuple-element.27), channel_id=1, source_target_pairs={{0,16},{16,0},{1,17},{17,1},{2,18},{18,2},{3,19},{19,3},{4,20},{20... | collective-permute-start | bytes 1179656 | tf_op jit(solution)/shard_map/ppermute | solution.py:297
  97.9 7.4 %copy-start.7 = (f32[1,64,32]{1,2,0:T(8,128)S(1)}, f32[1,64,32]{1,2,0:T(8,128)}, u32[]{:S(2)}) copy-start(f32[1,64,32]{1,2,0:T(8,128)} %param.15) | copy-start | bytes 24580
  99.1 6.2 %collective-permute-start.7 = (f32[72,128]{1,0:T(8,128)S(1)}, f32[72,128]{1,0:T(8,128)S(1)}, u32[]{:S(2)}, u32[]{:S(2)}) collective-permute-start(f32[72,128]{1,0:T(8,128)S(1)} %get-tuple-element.34), channel_id=1, source_target_pairs={{0,256},{256,0},{1,257},{257,1},{2,258},{258,2},{3,259},{259,3},{4... | collective-permute-start | bytes 110600 | tf_op jit(solution)/shard_map/ppermute | solution.py:299

commit v6 on v5

--- a/solution.py
+++ b/solution.py
@@ -280,9 +280,12 @@
     unit = lax.all_to_all(jnp.broadcast_to(block, (8, 192, HD)), "y", 0, 0, tiled=True).reshape(HALF, HD)
     gathered = lax.all_to_all(packed, ("y", "k"), 0, 0, tiled=True)
 
+    residual_rows, _ = tie(residual[0, 0], block)
+    own, there, mod_half, fw_half, sides = prepare(where, residual_rows, modulation[0], fw)
+    unit, there = tie(unit, there)
+
     units = [jnp.stack([unit, lax.ppermute(unit, ("k", "z"), CORES[0])])]
-    residual_rows, _ = tie(residual[0, 0], units[0])
-    own, there, mod_half, fw_half, sides = prepare(where, residual_rows, modulation[0], fw)
+    there, _ = tie(there, units[0])
     other = lax.ppermute(there, "c", SWAP)
     units.append(lax.ppermute(units[0], ("k", "z"), CORES[1]))
     units[1], other = tie(units[1], other)

time: 108 us -> 107 us (level)
  blocking collectives: 20.1 us -> 0 us
  waiting for transfers between devices: 25.6 us -> 41.6 us
  starting transfers between devices: 46 us -> 47.9 us
    all_to_all x1 -> x0, blocking collectives: 20.1 us -> none  [shards(): lax.all_to_all(jnp.broadcast_to(block, (8, 192, HD)), 'y', 0, 0, tiled=True)]
    all_to_all x0 -> x1, waiting for transfers between devices: none -> 11.9 us  [shards(): lax.all_to_all(jnp.broadcast_to(block, (8, 192, HD)), 'y', 0, 0, tiled=True)]
    all_to_all x0 -> x1, starting transfers between devices: none -> 6.95 us  [shards(): lax.all_to_all(jnp.broadcast_to(block, (8, 192, HD)), 'y', 0, 0, tiled=True)]
    ppermute x1, waiting for transfers between devices: 0.01 us -> 2.36 us  [shards(): units.append(lax.ppermute(units[0], ('k', 'z'), CORES[1]))]
    ppermute x2, starting transfers between devices: 8.89 us -> 6.78 us  [shards(): units.append(lax.ppermute(units[-1], ('k', 'z'), CORES[step]))]
    all_to_all x1, starting transfers between devices: 7.74 us -> 5.89 us  [shards(): lax.all_to_all(heads.reshape(16, 128, HD), ('c', 'y'), 0, 0, tiled=True)]
    all_to_all x1, waiting for transfers between devices: 0.01 us -> 1.49 us  [shards(): gathered = lax.all_to_all(packed, ('y', 'k'), 0, 0, tiled=True)]
  transfers between devices with their start and end apart: 10 -> 11, of which waited for: 5 -> 8; matrix products, arithmetic and copies ran while one was open for 0% -> 0% of each run, Pallas kernels for 6% -> 6%
where the time goes in v6:
time: 107 us; the launch traced here: 105 us
  starting transfers between devices  47.9 us (45%)
  waiting for transfers between devices  41.6 us (39%)
  Pallas kernels  11.7 us (11%)
  local copies, waits for them, and re-layouts  3.02 us (3%)
    all_to_all x1, waiting for transfers between devices, shards(): lax.all_to_all(heads.reshape(16, 128, HD), ('c', 'y'), 0, 0, tiled=True)  14.4 us
    all_to_all x1, waiting for transfers between devices, shards(): lax.all_to_all(jnp.broadcast_to(block, (8, 192, HD)), 'y', 0, 0, tiled=True)  11.9 us
    ppermute x1, starting transfers between devices, shards(): units = [jnp.stack([unit, lax.ppermute(unit, ('k', 'z'), CORES[0])])]  8.78 us
    all_to_all x1, starting transfers between devices, shards(): lax.all_to_all(jnp.broadcast_to(block, (8, 192, HD)), 'y', 0, 0, tiled=True)  6.95 us
    ppermute x2, starting transfers between devices, shards(): units.append(lax.ppermute(units[-1], ('k', 'z'), CORES[step]))  6.78 us
    ppermute x1, waiting for transfers between devices, shards(): other = lax.ppermute(there, 'c', SWAP)  6.63 us
    ppermute x1, starting transfers between devices, shards(): block = lax.ppermute(out_weight.T, ('c', 'k', 'l'), spread_pairs())  6.03 us
    all_to_all x1, starting transfers between devices, shards(): lax.all_to_all(heads.reshape(16, 128, HD), ('c', 'y'), 0, 0, tiled=True)  5.89 us
  transfers between devices with their start and end apart: 11, of which 8 were waited for; matrix products, arithmetic and copies ran while one was open for 0% of the time, Pallas kernels for 6%

profile of v6, /device:TPU:1, one launch (start us, length us, event | category | flops | bytes accessed | tf_op | source)
XLA Modules:
  0.0 105.2 jit_solution(7382166703259614308)
XLA Ops:
  0.0 6.0 %collective-permute-start = (bf16[192,128]{1,0:T(8,128)(2,1)}, bf16[192,128]{1,0:T(8,128)(2,1)S(1)}, u32[]{:S(2)}, u32[]{:S(2)}) collective-permute-start(bf16[192,128]{1,0:T(8,128)(2,1)} %bitcast.33), channel_id=1, source_target_pairs={{0,0},{8,16},{16,256},{24,272},{256,8},{264,24},{272,264},{280,280... | collective-permute-start | bytes 147464 | tf_op jit(solution)/shard_map/ppermute | solution.py:278
  6.0 2.2 %pack.1 = bf16[16,3,64,128]{3,2,1,0:T(8,128)(2,1)} custom-call(bf16[3,64,2048]{2,1,0:T(8,128)(2,1)} %bitcast.31), custom_call_target="tpu_custom_call" | custom-call | tf_op jit(solution)/shard_map/pack/pallas_call | solution.py:41
  9.0 7.0 %all-to-all-start.1 = ((bf16[8,192,128]{2,1,0:T(8,128)(2,1)}), bf16[8,192,128]{2,1,0:T(8,128)(2,1)S(1)}, u32[]{:S(2)}, u32[]{:S(2)}) async-start(bf16[8,192,128]{2,1,0:T(8,128)(2,1)} %broadcast_in_dim.6), calls=%async_computation.1 | async-start | bytes 786432 | tf_op jit(solution)/shard_map/all_to_all | solution.py:280
  18.5 11.9 %all-to-all-done.1 = bf16[8,192,128]{2,1,0:T(8,128)(2,1)S(1)} async-done(((bf16[8,192,128]{2,1,0:T(8,128)(2,1)}), bf16[8,192,128]{2,1,0:T(8,128)(2,1)S(1)}, u32[]{:S(2)}, u32[]{:S(2)}) %all-to-all-start.1) | async-done | bytes 393248 | tf_op jit(solution)/shard_map/all_to_all | solution.py:280
  30.5 8.8 %collective-permute-start.1 = (bf16[1536,128]{1,0:T(8,128)(2,1)S(1)}, bf16[1536,128]{1,0:T(8,128)(2,1)S(1)}, u32[]{:S(2)}, u32[]{:S(2)}) collective-permute-start(bf16[1536,128]{1,0:T(8,128)(2,1)S(1)} %bitcast.29), channel_id=1, source_target_pairs={{0,1},{1,0},{2,3},{3,2},{4,5},{5,4},{6,7},{7,6},{16,23},{17,18},{1... | collective-permute-start | bytes 1179656 | tf_op jit(solution)/shard_map/ppermute | solution.py:287
  39.2 3.5 %all-to-all-start = ((bf16[16,3,64,128]{3,2,1,0:T(8,128)(2,1)}), bf16[16,3,64,128]{3,2,1,0:T(8,128)(2,1)S(1)}, u32[]{:S(2)}, u32[]{:S(2)}) async-start(bf16[16,3,64,128]{3,2,1,0:T(8,128)(2,1)} %pack.1), calls=%async_computation | async-start | bytes 1572864 | tf_op jit(solution)/shard_map/all_to_all | solution.py:281
  42.8 1.6 %collective-permute-done.1 = bf16[1536,128]{1,0:T(8,128)(2,1)S(1)} collective-permute-done((bf16[1536,128]{1,0:T(8,128)(2,1)S(1)}, bf16[1536,128]{1,0:T(8,128)(2,1)S(1)}, u32[]{:S(2)}, u32[]{:S(2)}) %collective-permute-start.1) | collective-permute-done | bytes 393248 | tf_op jit(solution)/shard_map/ppermute | solution.py:287
  44.5 1.9 %collective-permute-start.2 = (bf16[2,1536,128]{2,1,0:T(8,128)(2,1)S(1)}, bf16[2,1536,128]{2,1,0:T(8,128)(2,1)S(1)}, u32[]{:S(2)}, u32[]{:S(2)}) collective-permute-start(bf16[2,1536,128]{2,1,0:T(8,128)(2,1)S(1)} %pad_maximum_fusion.refs_0_), channel_id=1, source_target_pairs={{0,7},{1,2},{2,1},{3,4},{4,3},{5,6},{6,5},{7,0},{16,17},{17,16},{1... | collective-permute-start | bytes 2359304 | tf_op jit(solution)/shard_map/ppermute | solution.py:290
  46.4 2.1 %collective-permute-start.3 = (bf16[80,1536]{1,0:T(8,128)(2,1)S(1)}, bf16[80,1536]{1,0:T(8,128)(2,1)S(1)}, u32[]{:S(2)}, u32[]{:S(2)}) collective-permute-start(bf16[80,1536]{1,0:T(8,128)(2,1)S(1)} %get-tuple-element.30), channel_id=1, source_target_pairs={{0,256},{256,0},{1,257},{257,1},{2,258},{258,2},{3,259},{259,3},{4... | collective-permute-start | bytes 737288 | tf_op jit(solution)/shard_map/ppermute | solution.py:289
  48.5 6.6 %collective-permute-done.3.other_ref = bf16[80,1536]{1,0:T(8,128)(2,1)S(1)} collective-permute-done((bf16[80,1536]{1,0:T(8,128)(2,1)S(1)}, bf16[80,1536]{1,0:T(8,128)(2,1)S(1)}, u32[]{:S(2)}, u32[]{:S(2)}) %collective-permute-start.3) | collective-permute-done | bytes 245792 | tf_op jit(solution)/shard_map/ppermute | solution.py:289
  55.2 2.4 %collective-permute-done.2.refs_1_ = bf16[2,1536,128]{2,1,0:T(8,128)(2,1)S(1)} collective-permute-done((bf16[2,1536,128]{2,1,0:T(8,128)(2,1)S(1)}, bf16[2,1536,128]{2,1,0:T(8,128)(2,1)S(1)}, u32[]{:S(2)}, u32[]{:S(2)}) %collective-permute-start.2) | collective-permute-done | bytes 786464 | tf_op jit(solution)/shard_map/ppermute | solution.py:290
  57.5 4.9 %collective-permute-start.4 = (bf16[2,1536,128]{2,1,0:T(8,128)(2,1)S(1)}, bf16[2,1536,128]{2,1,0:T(8,128)(2,1)S(1)}, u32[]{:S(2)}, u32[]{:S(2)}) collective-permute-start(bf16[2,1536,128]{2,1,0:T(8,128)(2,1)S(1)} %collective-permute-done.2.refs_1_), channel_id=1, source_target_pairs={{0,1},{1,0},{2,3},{3,2},{4,5},{5,4},{6,7},{7,6},{16,23},{17,18},{1... | collective-permute-start | bytes 2359304 | tf_op jit(solution)/shard_map/ppermute | solution.py:293
  62.4 1.5 %all-to-all-done.x_ref = bf16[16,3,64,128]{3,2,1,0:T(8,128)(2,1)S(1)} async-done(((bf16[16,3,64,128]{3,2,1,0:T(8,128)(2,1)}), bf16[16,3,64,128]{3,2,1,0:T(8,128)(2,1)S(1)}, u32[]{:S(2)}, u32[]{:S(2)}) %all-to-all-start) | async-done | bytes 786464 | tf_op jit(solution)/shard_map/all_to_all | solution.py:281
  63.9 2.8 %attend.1 = bf16[2,8,128,128]{3,2,1,0:T(8,128)(2,1)S(1)} custom-call(s32[8]{0:T(128)S(1)} %bitcast.28, bf16[16,3,64,128]{3,2,1,0:T(8,128)(2,1)S(1)} %all-to-all-done.x_ref), custom_call_target="tpu_custom_call" | custom-call | flops 540000000 | bytes 2000000 | tf_op jit(solution)/shard_map/attend/pallas_call | solution.py:86
  67.6 5.9 %all-to-all-start.2 = ((bf16[16,128,128]{2,1,0:T(8,128)(2,1)}), bf16[16,128,128]{2,1,0:T(8,128)(2,1)S(1)}, u32[]{:S(2)}, u32[]{:S(2)}) async-start(bf16[16,128,128]{2,1,0:T(8,128)(2,1)} %bitcast.23), calls=%async_computation.2 | async-start | bytes 1048576 | tf_op jit(solution)/shard_map/all_to_all | solution.py:297
  73.5 1.9 %collective-permute-start.5 = (bf16[2,1536,128]{2,1,0:T(8,128)(2,1)S(1)}, bf16[2,1536,128]{2,1,0:T(8,128)(2,1)}, u32[]{:S(2)}, u32[]{:S(2)}) collective-permute-start(bf16[2,1536,128]{2,1,0:T(8,128)(2,1)S(1)} %collective-permute-done.4.refs_2_), channel_id=1, source_target_pairs={{0,7},{1,2},{2,1},{3,4},{4,3},{5,6},{6,5},{7,0},{16,17},{17,16},{1... | collective-permute-start | bytes 2359304 | tf_op jit(solution)/shard_map/ppermute | solution.py:293
  75.4 14.4 %all-to-all-done.2 = bf16[16,128,128]{2,1,0:T(8,128)(2,1)S(1)} async-done(((bf16[16,128,128]{2,1,0:T(8,128)(2,1)}), bf16[16,128,128]{2,1,0:T(8,128)(2,1)S(1)}, u32[]{:S(2)}, u32[]{:S(2)}) %all-to-all-start.2) | async-done | bytes 524320 | tf_op jit(solution)/shard_map/all_to_all | solution.py:297
  89.8 3.1 %project.1 = (f32[2,64,1536]{2,1,0:T(8,128)S(1)}, bf16[2,64,1536]{2,1,0:T(8,128)(2,1)S(1)}) custom-call(s32[3]{0:T(128)S(1)} %pad_add_fusion.where_ref, bf16[2,8,128,128]{3,2,1,0:T(8,128)(2,1)S(1)} %bitcast.22, bf16[2,1536,128]{2,1,0:T(8,128)(2,1)S(1)} %pad_maximum_fusion.refs_0_, bf16[2,1536,128]{2,1,0:T(8,128)(2,1)S(1)} %collective-permute-done.2.refs_1_, ...), custom_call_target="tpu_custom_call" | custom-call | flops 810000000 | bytes 5000000 | tf_op jit(solution)/shard_map/project/pallas_call | solution.py:121
  92.9 1.9 %collective-permute-start.6 = (bf16[2,64,1536]{2,1,0:T(8,128)(2,1)S(1)}, bf16[2,64,1536]{2,1,0:T(8,128)(2,1)S(1)}, u32[]{:S(2)}, u32[]{:S(2)}) collective-permute-start(bf16[2,64,1536]{2,1,0:T(8,128)(2,1)S(1)} %get-tuple-element.33), channel_id=1, source_target_pairs={{0,16},{16,0},{1,17},{17,1},{2,18},{18,2},{3,19},{19,3},{4,20},{20... | collective-permute-start | bytes 1179656 | tf_op jit(solution)/shard_map/ppermute | solution.py:300
  94.8 1.7 %collective-permute-done.6.came_ref = bf16[2,64,1536]{2,1,0:T(8,128)(2,1)S(1)} collective-permute-done((bf16[2,64,1536]{2,1,0:T(8,128)(2,1)S(1)}, bf16[2,64,1536]{2,1,0:T(8,128)(2,1)S(1)}, u32[]{:S(2)}, u32[]{:S(2)}) %collective-permute-start.6) | collective-permute-done | bytes 393248 | tf_op jit(solution)/shard_map/ppermute | solution.py:300
  96.5 1.2 %norm.1 = (f32[72,128]{1,0:T(8,128)S(1)}, f32[72,128]{1,0:T(8,128)S(1)}) custom-call(s32[3]{0:T(128)S(1)} %pad_add_fusion.where_ref, f32[2,64,1536]{2,1,0:T(8,128)S(1)} %get-tuple-element.32.keep_ref, bf16[2,64,1536]{2,1,0:T(8,128)(2,1)S(1)} %collective-permute-done.6.came_ref, bf16[64,1536]{1,0:T(8,128)(2,1)S(1)} %copy-done.4, ...), custom_call_target="tpu_custom_call" | custom-call | tf_op jit(solution)/shard_map/norm/pallas_call | solution.py:217
  97.7 4.0 %collective-permute-start.7 = (f32[72,128]{1,0:T(8,128)S(1)}, f32[72,128]{1,0:T(8,128)S(1)}, u32[]{:S(2)}, u32[]{:S(2)}) collective-permute-start(f32[72,128]{1,0:T(8,128)S(1)} %get-tuple-element.40), channel_id=1, source_target_pairs={{0,256},{256,0},{1,257},{257,1},{2,258},{258,2},{3,259},{259,3},{4... | collective-permute-start | bytes 110600 | tf_op jit(solution)/shard_map/ppermute | solution.py:302
  102.4 1.5 %collective-permute-done.7.came_ref = f32[72,128]{1,0:T(8,128)S(1)} collective-permute-done((f32[72,128]{1,0:T(8,128)S(1)}, f32[72,128]{1,0:T(8,128)S(1)}, u32[]{:S(2)}, u32[]{:S(2)}) %collective-permute-start.7) | collective-permute-done | bytes 36896 | tf_op jit(solution)/shard_map/ppermute | solution.py:302
  103.9 1.3 %finish.1 = f32[32,64]{1,0:T(8,128)} custom-call(s32[3]{0:T(128)S(1)} %pad_add_fusion.where_ref, s32[1]{0:T(128)S(6)} %copy.12.time_ref, f32[72,128]{1,0:T(8,128)S(1)} %get-tuple-element.39.own_ref, f32[72,128]{1,0:T(8,128)S(1)} %collective-permute-done.7.came_ref, f32[32,64]{1,0:T(8,128)S(1)} %bitcast.27), custom_call_target="tpu_custom_call" | custom-call | tf_op jit(solution)/shard_map/finish/pallas_call | solution.py:244
  (28 shorter events, 4.3 us)
Async XLA Ops:
  0.0 8.2 %collective-permute-start = (bf16[192,128]{1,0:T(8,128)(2,1)}, bf16[192,128]{1,0:T(8,128)(2,1)S(1)}, u32[]{:S(2)}, u32[]{:S(2)}) collective-permute-start(bf16[192,128]{1,0:T(8,128)(2,1)} %bitcast.33), channel_id=1, source_target_pairs={{0,0},{8,16},{16,256},{24,272},{256,8},{264,24},{272,264},{280,280... | collective-permute-start | bytes 147464 | tf_op jit(solution)/shard_map/ppermute | solution.py:278
  8.2 7.8 %copy-start.9 = (f32[1,3,3072]{2,0,1:T(1,128)S(1)}, f32[1,3,3072]{2,0,1:T(1,128)}, u32[]{:S(2)}) copy-start(f32[1,3,3072]{2,0,1:T(1,128)} %param.12) | copy-start | bytes 110596
  9.0 7.1 %copy-start.1 = (bf16[1,1,64,3072]{3,2,1,0:T(8,128)(2,1)S(1)}, bf16[1,1,64,3072]{3,2,1,0:T(8,128)(2,1)}, u32[]{:S(2)}) copy-start(bf16[1,1,64,3072]{3,2,1,0:T(8,128)(2,1)} %param.9) | copy-start | bytes 1179652
  9.0 7.1 %copy-start.2 = (bf16[3072,64]{0,1:T(8,128)(2,1)S(1)}, bf16[3072,64]{0,1:T(8,128)(2,1)}, u32[]{:S(2)}) copy-start(bf16[3072,64]{0,1:T(8,128)(2,1)} %param.11) | copy-start | bytes 1179652
  9.0 21.4 %all-to-all-start.1 = ((bf16[8,192,128]{2,1,0:T(8,128)(2,1)}), bf16[8,192,128]{2,1,0:T(8,128)(2,1)S(1)}, u32[]{:S(2)}, u32[]{:S(2)}) async-start(bf16[8,192,128]{2,1,0:T(8,128)(2,1)} %broadcast_in_dim.6), calls=%async_computation.1 | async-start | bytes 786432 | tf_op jit(solution)/shard_map/all_to_all | solution.py:280
  17.2 0.7 copy-start.3
  17.9 0.7 copy-start.5
  30.5 13.9 %collective-permute-start.1 = (bf16[1536,128]{1,0:T(8,128)(2,1)S(1)}, bf16[1536,128]{1,0:T(8,128)(2,1)S(1)}, u32[]{:S(2)}, u32[]{:S(2)}) collective-permute-start(bf16[1536,128]{1,0:T(8,128)(2,1)S(1)} %bitcast.29), channel_id=1, source_target_pairs={{0,1},{1,0},{2,3},{3,2},{4,5},{5,4},{6,7},{7,6},{16,23},{17,18},{1... | collective-permute-start | bytes 1179656 | tf_op jit(solution)/shard_map/ppermute | solution.py:287
  39.2 24.6 %all-to-all-start = ((bf16[16,3,64,128]{3,2,1,0:T(8,128)(2,1)}), bf16[16,3,64,128]{3,2,1,0:T(8,128)(2,1)S(1)}, u32[]{:S(2)}, u32[]{:S(2)}) async-start(bf16[16,3,64,128]{3,2,1,0:T(8,128)(2,1)} %pack.1), calls=%async_computation | async-start | bytes 1572864 | tf_op jit(solution)/shard_map/all_to_all | solution.py:281
  44.5 19.4 %copy-start.8 = (s32[1,8]{1,0:T(1,128)S(1)}, s32[1,8]{1,0:T(1,128)}, u32[]{:S(2)}) copy-start(s32[1,8]{1,0:T(1,128)} %param.13) | copy-start | bytes 100
  44.5 13.0 %collective-permute-start.2 = (bf16[2,1536,128]{2,1,0:T(8,128)(2,1)S(1)}, bf16[2,1536,128]{2,1,0:T(8,128)(2,1)S(1)}, u32[]{:S(2)}, u32[]{:S(2)}) collective-permute-start(bf16[2,1536,128]{2,1,0:T(8,128)(2,1)S(1)} %pad_maximum_fusion.refs_0_), channel_id=1, source_target_pairs={{0,7},{1,2},{2,1},{3,4},{4,3},{5,6},{6,5},{7,0},{16,17},{17,16},{1... | collective-permute-start | bytes 2359304 | tf_op jit(solution)/shard_map/ppermute | solution.py:290
  46.4 8.7 %collective-permute-start.3 = (bf16[80,1536]{1,0:T(8,128)(2,1)S(1)}, bf16[80,1536]{1,0:T(8,128)(2,1)S(1)}, u32[]{:S(2)}, u32[]{:S(2)}) collective-permute-start(bf16[80,1536]{1,0:T(8,128)(2,1)S(1)} %get-tuple-element.30), channel_id=1, source_target_pairs={{0,256},{256,0},{1,257},{257,1},{2,258},{258,2},{3,259},{259,3},{4... | collective-permute-start | bytes 737288 | tf_op jit(solution)/shard_map/ppermute | solution.py:289
  57.5 15.9 %collective-permute-start.4 = (bf16[2,1536,128]{2,1,0:T(8,128)(2,1)S(1)}, bf16[2,1536,128]{2,1,0:T(8,128)(2,1)S(1)}, u32[]{:S(2)}, u32[]{:S(2)}) collective-permute-start(bf16[2,1536,128]{2,1,0:T(8,128)(2,1)S(1)} %collective-permute-done.2.refs_1_), channel_id=1, source_target_pairs={{0,1},{1,0},{2,3},{3,2},{4,5},{5,4},{6,7},{7,6},{16,23},{17,18},{1... | collective-permute-start | bytes 2359304 | tf_op jit(solution)/shard_map/ppermute | solution.py:293
  66.7 0.8 copy-start
  67.6 22.2 %all-to-all-start.2 = ((bf16[16,128,128]{2,1,0:T(8,128)(2,1)}), bf16[16,128,128]{2,1,0:T(8,128)(2,1)S(1)}, u32[]{:S(2)}, u32[]{:S(2)}) async-start(bf16[16,128,128]{2,1,0:T(8,128)(2,1)} %bitcast.23), calls=%async_computation.2 | async-start | bytes 1048576 | tf_op jit(solution)/shard_map/all_to_all | solution.py:297
  73.5 16.3 %collective-permute-start.5 = (bf16[2,1536,128]{2,1,0:T(8,128)(2,1)S(1)}, bf16[2,1536,128]{2,1,0:T(8,128)(2,1)}, u32[]{:S(2)}, u32[]{:S(2)}) collective-permute-start(bf16[2,1536,128]{2,1,0:T(8,128)(2,1)S(1)} %collective-permute-done.4.refs_2_), channel_id=1, source_target_pairs={{0,7},{1,2},{2,1},{3,4},{4,3},{5,6},{6,5},{7,0},{16,17},{17,16},{1... | collective-permute-start | bytes 2359304 | tf_op jit(solution)/shard_map/ppermute | solution.py:293
  89.8 6.8 %copy-start.4 = (bf16[64,1536]{1,0:T(8,128)(2,1)S(1)}, bf16[64,1536]{1,0:T(8,128)(2,1)}, u32[]{:S(2)}) copy-start(bf16[64,1536]{1,0:T(8,128)(2,1)} %copy-done.3) | copy-start | bytes 589828
  89.8 6.8 %copy-start.6 = (bf16[64,1536]{1,0:T(8,128)(2,1)S(1)}, bf16[64,1536]{1,0:T(8,128)(2,1)}, u32[]{:S(2)}) copy-start(bf16[64,1536]{1,0:T(8,128)(2,1)} %copy-done.5) | copy-start | bytes 589828
  92.9 3.6 %collective-permute-start.6 = (bf16[2,64,1536]{2,1,0:T(8,128)(2,1)S(1)}, bf16[2,64,1536]{2,1,0:T(8,128)(2,1)S(1)}, u32[]{:S(2)}, u32[]{:S(2)}) collective-permute-start(bf16[2,64,1536]{2,1,0:T(8,128)(2,1)S(1)} %get-tuple-element.33), channel_id=1, source_target_pairs={{0,16},{16,0},{1,17},{17,1},{2,18},{18,2},{3,19},{19,3},{4,20},{20... | collective-permute-start | bytes 1179656 | tf_op jit(solution)/shard_map/ppermute | solution.py:300
  96.5 7.4 %copy-start.7 = (f32[1,64,32]{1,2,0:T(8,128)S(1)}, f32[1,64,32]{1,2,0:T(8,128)}, u32[]{:S(2)}) copy-start(f32[1,64,32]{1,2,0:T(8,128)} %param.15) | copy-start | bytes 24580
  97.7 6.2 %collective-permute-start.7 = (f32[72,128]{1,0:T(8,128)S(1)}, f32[72,128]{1,0:T(8,128)S(1)}, u32[]{:S(2)}, u32[]{:S(2)}) collective-permute-start(f32[72,128]{1,0:T(8,128)S(1)} %get-tuple-element.40), channel_id=1, source_target_pairs={{0,256},{256,0},{1,257},{257,1},{2,258},{258,2},{3,259},{259,3},{4... | collective-permute-start | bytes 110600 | tf_op jit(solution)/shard_map/ppermute | solution.py:302

commit v7 on v6

--- a/solution.py
+++ b/solution.py
@@ -30,21 +30,22 @@
     return pl.BlockSpec(memory_space=space)
 
 
-def pack_kernel(in_ref, out_ref):
+def pack_kernel(where_ref, in_ref, out_ref):
+    l = where_ref[4]
     for y in range(8):
         for k in range(2):
-            head = 8 * k + y
-            out_ref[2 * y + k] = in_ref[:, :, head * HD : (head + 1) * HD]
-
-
-def pack(own):
+            first = pl.multiple_of((8 * lax.bitwise_xor(l, k) + y) * HD, HD)
+            out_ref[2 * y + k] = in_ref[:, :, pl.ds(first, HD)]
+
+
+def pack(where, own):
     return pl.pallas_call(
         pack_kernel,
         out_shape=jax.ShapeDtypeStruct((16, 3, DEV_ROWS, HD), jnp.bfloat16),
-        in_specs=[spec(VMEM)],
+        in_specs=[spec(SMEM), spec(VMEM)],
         out_specs=spec(VMEM),
         name="pack",
-    )(own)
+    )(where, own)
 
 
 BLOCKS = ((0, 128, 0, 256), (128, 256, 0, 1024), (256, 512, 128, 1024), (512, 768, 128, 1024), (768, 1024, 128, 1024))
@@ -95,16 +96,15 @@
 
 
 def project_kernel(where_ref, x_ref, *refs):
-    units, (keep_ref, send_ref, *buffers, arrived) = refs[:4], refs[4:]
-    copies = [pltpu.make_async_copy(unit, buffer, arrived.at[i]) for i, (unit, buffer) in enumerate(zip(units, buffers))]
-    for copy in copies:
-        copy.start()
+    units, (keep_ref, send_ref, buffer, arrived) = refs[:4], refs[4:]
+    copy = pltpu.make_async_copy(units[3], buffer, arrived)
+    copy.start()
+    buffers = [*units[:3], buffer]
     core, z = where_ref[0], where_ref[2]
     sign = (2 * lax.rem(z, 2) - 1) * (1 - 2 * core)
     heads = [lax.rem(z + offset * sign + 8, 8) for offset in (0, -1, 1, 2, -2, -3, 3, 4)]
     x = jnp.concatenate([x_ref[:, h].reshape(256, HD) for h in heads], axis=1)
-    for copy in copies:
-        copy.wait()
+    copy.wait()
     tile = 384
     for t in range(HALF // tile):
         cols = slice(t * tile, (t + 1) * tile)
@@ -124,9 +124,9 @@
             jax.ShapeDtypeStruct((2, DEV_ROWS, HALF), jnp.float32),
             jax.ShapeDtypeStruct((2, DEV_ROWS, HALF), jnp.bfloat16),
         ),
-        in_specs=[spec(SMEM), spec(VMEM)] + [spec(pl.ANY)] * 4,
+        in_specs=[spec(SMEM)] + [spec(VMEM)] * 4 + [spec(pl.ANY)],
         out_specs=(spec(VMEM), spec(VMEM)),
-        scratch_shapes=[VMEM((2, HALF, HD), jnp.bfloat16)] * 4 + [pltpu.SemaphoreType.DMA((4,))],
+        scratch_shapes=[VMEM((2, HALF, HD), jnp.bfloat16), pltpu.SemaphoreType.DMA],
         compiler_params=pltpu.CompilerParams(vmem_limit_bytes=24 * 2**20),
         cost_estimate=pl.CostEstimate(flops=810_000_000, bytes_accessed=5_000_000, transcendentals=0),
         name="project",
@@ -141,21 +141,21 @@
     return terms
 
 
-def blocks_of(array, branch):
+def blocks_of(array, half):
     even, odd = [
         jnp.concatenate([array[:, (2 * i + k) * 192 : (2 * i + k + 1) * 192] for i in range(8)], axis=1) for k in range(2)
     ]
-    return jnp.where(branch == 0, even, odd)
+    return jnp.where(half == 0, even, odd)
 
 
 def prepare_kernel(where_ref, residual_ref, mod_ref, fw_ref, own_ref, there_ref, mod_half_ref, fw_half_ref, side_ref):
-    me = where_ref[1]
+    me, half = where_ref[1], where_ref[3]
     residual = residual_ref[...].astype(jnp.float32)
-    own_ref[...] = blocks_of(residual, me).astype(jnp.bfloat16)
-    mod_half_ref[...] = blocks_of(mod_ref[...], me)
-    fw_half_ref[...] = blocks_of(fw_ref[...].astype(jnp.float32), me).astype(jnp.bfloat16)
-    there_ref[:DEV_ROWS] = blocks_of(residual, 1 - me).astype(jnp.bfloat16)
-    terms = split3(blocks_of(mod_ref[...], 1 - me))
+    own_ref[...] = blocks_of(residual, half).astype(jnp.bfloat16)
+    mod_half_ref[...] = blocks_of(mod_ref[...], half)
+    fw_half_ref[...] = blocks_of(fw_ref[...].astype(jnp.float32), half).astype(jnp.bfloat16)
+    there_ref[:DEV_ROWS] = blocks_of(residual, 1 - half).astype(jnp.bfloat16)
+    terms = split3(blocks_of(mod_ref[...], 1 - half))
     terms.append(jnp.zeros((7, HALF), jnp.bfloat16))
     there_ref[DEV_ROWS:] = jnp.concatenate([term.astype(jnp.float32) for term in terms]).astype(jnp.bfloat16)
     fw = fw_ref[...].astype(jnp.float32)
@@ -230,7 +230,7 @@
     tilt = jnp.where(ours, own_ref[40:, 0:1], came_ref[40:, 0:1])
     offset = jnp.where(ours, own_ref[40:, 1:2], came_ref[40:, 1:2])
     gap = 0.5 * (own_ref[32:33] - came_ref[32:33])
-    gap = jnp.where(me == 0, gap, -gap)
+    gap = jnp.where(where_ref[3] == 0, gap, -gap)
     var = (own_ref[33:34] + came_ref[33:34]) / WIDTH + gap * gap
     prediction = (own_ref[:32] + came_ref[:32] + gap * tilt) / jnp.sqrt(var + EPS) + offset
     conditional, unconditional = prediction[:, :DEV_ROWS], pltpu.roll(prediction, DEV_ROWS, 1)[:, :DEV_ROWS]
@@ -262,7 +262,8 @@
     for c in range(2):
         for k in range(2):
             for l in range(2):
-                pairs.append(((c * 2 + k) * 2 + l, (k * 2 + l) * 2 + c))
+                chip = c ^ k
+                pairs.append(((c * 2 + k) * 2 + l, (c * 2 + (chip ^ l)) * 2 + chip))
     return pairs
 
 
@@ -272,17 +273,18 @@
 
 def shards(qkv, residual, out_weight, final_weight, modulation, frames, timestep, noisy):
     branch = lax.axis_index("c")
-    where = jnp.stack([lax.axis_index("k"), branch, lax.axis_index("z")]).astype(jnp.int32)
+    l = lax.axis_index("l")
+    where = jnp.stack([lax.axis_index("k"), branch, lax.axis_index("z"), lax.bitwise_xor(branch, l), l]).astype(jnp.int32)
     fw = final_weight.T
 
     block = lax.ppermute(out_weight.T, ("c", "k", "l"), spread_pairs())
-    packed, block = tie(pack(qkv[0, :, 0]), block)
     unit = lax.all_to_all(jnp.broadcast_to(block, (8, 192, HD)), "y", 0, 0, tiled=True).reshape(HALF, HD)
+
+    qkv_rows, residual_rows, _ = tie(qkv[0, :, 0], residual[0, 0], block)
+    packed = pack(where, qkv_rows)
+    own, there, mod_half, fw_half, sides = prepare(where, residual_rows, modulation[0], fw)
+    unit, there, packed = tie(unit, there, packed)
     gathered = lax.all_to_all(packed, ("y", "k"), 0, 0, tiled=True)
-
-    residual_rows, _ = tie(residual[0, 0], block)
-    own, there, mod_half, fw_half, sides = prepare(where, residual_rows, modulation[0], fw)
-    unit, there = tie(unit, there)
 
     units = [jnp.stack([unit, lax.ppermute(unit, ("k", "z"), CORES[0])])]
     there, _ = tie(there, units[0])
@@ -292,7 +294,6 @@
     for step in (0, 1):
         units.append(lax.ppermute(units[-1], ("k", "z"), CORES[step]))
 
-    gathered, _ = tie(gathered, units[0])
     heads = attend(frames[0], gathered)
     rows = lax.all_to_all(heads.reshape(16, 128, HD), ("c", "y"), 0, 0, tiled=True).reshape(2, 8, 128, HD)
 

time: 107 us -> 107 us (level)
  waiting for transfers between devices: 41.6 us -> 34.4 us
  starting transfers between devices: 47.9 us -> 54.7 us
  local copies, waits for them, and re-layouts: 3.02 us -> 4.14 us
    ppermute x1, starting transfers between devices: 2.1 us -> 7.02 us  [shards(): other = lax.ppermute(there, 'c', SWAP)]
    all_to_all x1, waiting for transfers between devices: 11.9 us -> 7.87 us  [shards(): lax.all_to_all(jnp.broadcast_to(block, (8, 192, HD)), 'y', 0, 0, tiled=True)]
    ppermute x1, waiting for transfers between devices: 6.63 us -> 3.87 us  [shards(): other = lax.ppermute(there, 'c', SWAP)]
    ppermute x1, waiting for transfers between devices: 0.01 us -> 2.53 us  [shards(): block = lax.ppermute(out_weight.T, ('c', 'k', 'l'), spread_pairs())]
    ppermute x1, waiting for transfers between devices: 2.36 us -> 0.2 us  [shards(): units.append(lax.ppermute(units[0], ('k', 'z'), CORES[1]))]
    ppermute x1, starting transfers between devices: 6.03 us -> 3.94 us  [shards(): block = lax.ppermute(out_weight.T, ('c', 'k', 'l'), spread_pairs())]
    all_to_all x1, starting transfers between devices: 5.89 us -> 7.68 us  [shards(): lax.all_to_all(heads.reshape(16, 128, HD), ('c', 'y'), 0, 0, tiled=True)]
    ppermute x1, starting transfers between devices: 1.92 us -> 3.57 us  [shards(): came = lax.ppermute(send, 'k', SWAP)]
  transfers between devices with their start and end apart: 11 -> 11, of which waited for: 8 -> 8; matrix products, arithmetic and copies ran while one was open for 0% -> 1% of each run, Pallas kernels for 6% -> 6%
where the time goes in v7:
time: 107 us; the launch traced here: 106 us
  starting transfers between devices  54.7 us (51%)
  waiting for transfers between devices  34.4 us (32%)
  Pallas kernels  11.7 us (11%)
  local copies, waits for them, and re-layouts  4.14 us (4%)
    all_to_all x1, waiting for transfers between devices, shards(): lax.all_to_all(heads.reshape(16, 128, HD), ('c', 'y'), 0, 0, tiled=True)  14.2 us
    ppermute x1, starting transfers between devices, shards(): units = [jnp.stack([unit, lax.ppermute(unit, ('k', 'z'), CORES[0])])]  9.01 us
    ppermute x2, starting transfers between devices, shards(): units.append(lax.ppermute(units[-1], ('k', 'z'), CORES[step]))  8.36 us
    all_to_all x1, waiting for transfers between devices, shards(): lax.all_to_all(jnp.broadcast_to(block, (8, 192, HD)), 'y', 0, 0, tiled=True)  7.87 us
    all_to_all x1, starting transfers between devices, shards(): lax.all_to_all(heads.reshape(16, 128, HD), ('c', 'y'), 0, 0, tiled=True)  7.68 us
    ppermute x1, starting transfers between devices, shards(): other = lax.ppermute(there, 'c', SWAP)  7.02 us
    all_to_all x1, starting transfers between devices, shards(): lax.all_to_all(jnp.broadcast_to(block, (8, 192, HD)), 'y', 0, 0, tiled=True)  6.95 us
    ppermute x1, starting transfers between devices, shards(): block = lax.ppermute(out_weight.T, ('c', 'k', 'l'), spread_pairs())  3.94 us
  transfers between devices with their start and end apart: 11, of which 8 were waited for; matrix products, arithmetic and copies ran while one was open for 1% of the time, Pallas kernels for 6%

profile of v7, /device:TPU:1, one launch (start us, length us, event | category | flops | bytes accessed | tf_op | source)
XLA Modules:
  0.0 105.8 jit_solution(9444484609207751746)
XLA Ops:
  0.0 3.9 %collective-permute-start = (bf16[192,128]{1,0:T(8,128)(2,1)}, bf16[192,128]{1,0:T(8,128)(2,1)S(1)}, u32[]{:S(2)}, u32[]{:S(2)}) collective-permute-start(bf16[192,128]{1,0:T(8,128)(2,1)} %bitcast.35), channel_id=1, source_target_pairs={{0,0},{8,16},{16,24},{24,8},{256,280},{264,264},{272,256},{280,272... | collective-permute-start | bytes 147464 | tf_op jit(solution)/shard_map/ppermute | solution.py:280
  3.9 2.5 %collective-permute-done = bf16[192,128]{1,0:T(8,128)(2,1)S(1)} collective-permute-done((bf16[192,128]{1,0:T(8,128)(2,1)}, bf16[192,128]{1,0:T(8,128)(2,1)S(1)}, u32[]{:S(2)}, u32[]{:S(2)}) %collective-permute-start) | collective-permute-done | bytes 49184 | tf_op jit(solution)/shard_map/ppermute | solution.py:280
  7.3 7.0 %all-to-all-start = ((bf16[8,192,128]{2,1,0:T(8,128)(2,1)}), bf16[8,192,128]{2,1,0:T(8,128)(2,1)S(1)}, u32[]{:S(2)}, u32[]{:S(2)}) async-start(bf16[8,192,128]{2,1,0:T(8,128)(2,1)} %broadcast_in_dim.6), calls=%async_computation | async-start | bytes 786432 | tf_op jit(solution)/shard_map/all_to_all | solution.py:281
  14.9 2.3 %pack.1 = bf16[16,3,64,128]{3,2,1,0:T(8,128)(2,1)} custom-call(s32[5]{0:T(128)} %stack.32.where_ref, bf16[3,64,2048]{2,1,0:T(8,128)(2,1)} %bitcast.33), custom_call_target="tpu_custom_call" | custom-call | tf_op jit(solution)/shard_map/pack/pallas_call | solution.py:42
  17.7 1.1 %prepare.1 = (bf16[64,1536]{1,0:T(8,128)(2,1)S(1)}, bf16[80,1536]{1,0:T(8,128)(2,1)S(1)}, f32[3,1536]{1,0:T(4,128)S(1)}, bf16[64,1536]{1,0:T(8,128)(2,1)S(1)}, f32[64,128]{1,0:T(8,128)S(1)}) custom-call(s32[5]{0:T(128)S(1)} %copy-done.7, bf16[64,3072]{1,0:T(8,128)(2,1)S(1)} %bitcast.26, f32[3,3072]{1,0:T(4,128)S(1)} %bitcast.28, bf16[64,3072]{1,0:T(8,128)(2,1)S(1)} %bitcast.27), custom_call_target="tpu_custom_call" | custom-call | tf_op jit(solution)/shard_map/prepare/pallas_call | solution.py:172
  20.2 7.9 %all-to-all-done = bf16[8,192,128]{2,1,0:T(8,128)(2,1)S(1)} async-done(((bf16[8,192,128]{2,1,0:T(8,128)(2,1)}), bf16[8,192,128]{2,1,0:T(8,128)(2,1)S(1)}, u32[]{:S(2)}, u32[]{:S(2)}) %all-to-all-start) | async-done | bytes 393248 | tf_op jit(solution)/shard_map/all_to_all | solution.py:281
  28.1 9.0 %collective-permute-start.1 = (bf16[1536,128]{1,0:T(8,128)(2,1)S(1)}, bf16[1536,128]{1,0:T(8,128)(2,1)S(1)}, u32[]{:S(2)}, u32[]{:S(2)}) collective-permute-start(bf16[1536,128]{1,0:T(8,128)(2,1)S(1)} %bitcast.31), channel_id=1, source_target_pairs={{0,1},{1,0},{2,3},{3,2},{4,5},{5,4},{6,7},{7,6},{16,23},{17,18},{1... | collective-permute-start | bytes 1179656 | tf_op jit(solution)/shard_map/ppermute | solution.py:289
  37.1 3.5 %all-to-all-start.1 = ((bf16[16,3,64,128]{3,2,1,0:T(8,128)(2,1)}), bf16[16,3,64,128]{3,2,1,0:T(8,128)(2,1)S(1)}, u32[]{:S(2)}, u32[]{:S(2)}) async-start(bf16[16,3,64,128]{3,2,1,0:T(8,128)(2,1)} %pack.1), calls=%async_computation.1 | async-start | bytes 1572864 | tf_op jit(solution)/shard_map/all_to_all | solution.py:287
  40.6 1.6 %collective-permute-done.1 = bf16[1536,128]{1,0:T(8,128)(2,1)S(1)} collective-permute-done((bf16[1536,128]{1,0:T(8,128)(2,1)S(1)}, bf16[1536,128]{1,0:T(8,128)(2,1)S(1)}, u32[]{:S(2)}, u32[]{:S(2)}) %collective-permute-start.1) | collective-permute-done | bytes 393248 | tf_op jit(solution)/shard_map/ppermute | solution.py:289
  42.3 1.9 %collective-permute-start.2 = (bf16[2,1536,128]{2,1,0:T(8,128)(2,1)S(1)}, bf16[2,1536,128]{2,1,0:T(8,128)(2,1)S(1)}, u32[]{:S(2)}, u32[]{:S(2)}) collective-permute-start(bf16[2,1536,128]{2,1,0:T(8,128)(2,1)S(1)} %pad_maximum_fusion.refs_0_), channel_id=1, source_target_pairs={{0,7},{1,2},{2,1},{3,4},{4,3},{5,6},{6,5},{7,0},{16,17},{17,16},{1... | collective-permute-start | bytes 2359304 | tf_op jit(solution)/shard_map/ppermute | solution.py:292
  44.3 7.0 %collective-permute-start.3 = (bf16[80,1536]{1,0:T(8,128)(2,1)S(1)}, bf16[80,1536]{1,0:T(8,128)(2,1)S(1)}, u32[]{:S(2)}, u32[]{:S(2)}) collective-permute-start(bf16[80,1536]{1,0:T(8,128)(2,1)S(1)} %get-tuple-element.28), channel_id=1, source_target_pairs={{0,256},{256,0},{1,257},{257,1},{2,258},{258,2},{3,259},{259,3},{4... | collective-permute-start | bytes 737288 | tf_op jit(solution)/shard_map/ppermute | solution.py:291
  51.3 3.9 %collective-permute-done.3.other_ref = bf16[80,1536]{1,0:T(8,128)(2,1)S(1)} collective-permute-done((bf16[80,1536]{1,0:T(8,128)(2,1)S(1)}, bf16[80,1536]{1,0:T(8,128)(2,1)S(1)}, u32[]{:S(2)}, u32[]{:S(2)}) %collective-permute-start.3) | collective-permute-done | bytes 245792 | tf_op jit(solution)/shard_map/ppermute | solution.py:291
  55.4 6.4 %collective-permute-start.4 = (bf16[2,1536,128]{2,1,0:T(8,128)(2,1)S(1)}, bf16[2,1536,128]{2,1,0:T(8,128)(2,1)S(1)}, u32[]{:S(2)}, u32[]{:S(2)}) collective-permute-start(bf16[2,1536,128]{2,1,0:T(8,128)(2,1)S(1)} %collective-permute-done.2.refs_1_), channel_id=1, source_target_pairs={{0,1},{1,0},{2,3},{3,2},{4,5},{5,4},{6,7},{7,6},{16,23},{17,18},{1... | collective-permute-start | bytes 2359304 | tf_op jit(solution)/shard_map/ppermute | solution.py:295
  61.8 2.9 %attend.1 = bf16[2,8,128,128]{3,2,1,0:T(8,128)(2,1)S(1)} custom-call(s32[8]{0:T(128)S(1)} %bitcast.30, bf16[16,3,64,128]{3,2,1,0:T(8,128)(2,1)S(1)} %all-to-all-done.1.x_ref), custom_call_target="tpu_custom_call" | custom-call | flops 540000000 | bytes 2000000 | tf_op jit(solution)/shard_map/attend/pallas_call | solution.py:87
  65.5 7.7 %all-to-all-start.2 = ((bf16[16,128,128]{2,1,0:T(8,128)(2,1)}), bf16[16,128,128]{2,1,0:T(8,128)(2,1)S(1)}, u32[]{:S(2)}, u32[]{:S(2)}) async-start(bf16[16,128,128]{2,1,0:T(8,128)(2,1)} %bitcast.25), calls=%async_computation.2 | async-start | bytes 1048576 | tf_op jit(solution)/shard_map/all_to_all | solution.py:298
  73.2 1.9 %collective-permute-start.5 = (bf16[2,1536,128]{2,1,0:T(8,128)(2,1)S(1)}, bf16[2,1536,128]{2,1,0:T(8,128)(2,1)}, u32[]{:S(2)}, u32[]{:S(2)}) collective-permute-start(bf16[2,1536,128]{2,1,0:T(8,128)(2,1)S(1)} %collective-permute-done.4.refs_2_), channel_id=1, source_target_pairs={{0,7},{1,2},{2,1},{3,4},{4,3},{5,6},{6,5},{7,0},{16,17},{17,16},{1... | collective-permute-start | bytes 2359304 | tf_op jit(solution)/shard_map/ppermute | solution.py:295
  75.1 14.2 %all-to-all-done.2 = bf16[16,128,128]{2,1,0:T(8,128)(2,1)S(1)} async-done(((bf16[16,128,128]{2,1,0:T(8,128)(2,1)}), bf16[16,128,128]{2,1,0:T(8,128)(2,1)S(1)}, u32[]{:S(2)}, u32[]{:S(2)}) %all-to-all-start.2) | async-done | bytes 524320 | tf_op jit(solution)/shard_map/all_to_all | solution.py:298
  89.3 2.9 %project.1 = (f32[2,64,1536]{2,1,0:T(8,128)S(1)}, bf16[2,64,1536]{2,1,0:T(8,128)(2,1)S(1)}) custom-call(s32[5]{0:T(128)S(1)} %copy-done.7, bf16[2,8,128,128]{3,2,1,0:T(8,128)(2,1)S(1)} %bitcast.24, bf16[2,1536,128]{2,1,0:T(8,128)(2,1)S(1)} %pad_maximum_fusion.refs_0_, bf16[2,1536,128]{2,1,0:T(8,128)(2,1)S(1)} %collective-permute-done.2.refs_1_, ...), custom_call_target="tpu_custom_call" | custom-call | flops 810000000 | bytes 5000000 | tf_op jit(solution)/shard_map/project/pallas_call | solution.py:121
  92.2 3.6 %collective-permute-start.6 = (bf16[2,64,1536]{2,1,0:T(8,128)(2,1)S(1)}, bf16[2,64,1536]{2,1,0:T(8,128)(2,1)S(1)}, u32[]{:S(2)}, u32[]{:S(2)}) collective-permute-start(bf16[2,64,1536]{2,1,0:T(8,128)(2,1)S(1)} %get-tuple-element.31), channel_id=1, source_target_pairs={{0,16},{16,0},{1,17},{17,1},{2,18},{18,2},{3,19},{19,3},{4,20},{20... | collective-permute-start | bytes 1179656 | tf_op jit(solution)/shard_map/ppermute | solution.py:301
  95.8 1.3 %collective-permute-done.6.came_ref = bf16[2,64,1536]{2,1,0:T(8,128)(2,1)S(1)} collective-permute-done((bf16[2,64,1536]{2,1,0:T(8,128)(2,1)S(1)}, bf16[2,64,1536]{2,1,0:T(8,128)(2,1)S(1)}, u32[]{:S(2)}, u32[]{:S(2)}) %collective-permute-start.6) | collective-permute-done | bytes 393248 | tf_op jit(solution)/shard_map/ppermute | solution.py:301
  97.2 1.2 %norm.1 = (f32[72,128]{1,0:T(8,128)S(1)}, f32[72,128]{1,0:T(8,128)S(1)}) custom-call(s32[5]{0:T(128)S(1)} %copy-done.7, f32[2,64,1536]{2,1,0:T(8,128)S(1)} %get-tuple-element.30.keep_ref, bf16[2,64,1536]{2,1,0:T(8,128)(2,1)S(1)} %collective-permute-done.6.came_ref, bf16[64,1536]{1,0:T(8,128)(2,1)S(1)} %copy-done.4, ...), custom_call_target="tpu_custom_call" | custom-call | tf_op jit(solution)/shard_map/norm/pallas_call | solution.py:217
  98.3 2.7 %collective-permute-start.7 = (f32[72,128]{1,0:T(8,128)S(1)}, f32[72,128]{1,0:T(8,128)S(1)}, u32[]{:S(2)}, u32[]{:S(2)}) collective-permute-start(f32[72,128]{1,0:T(8,128)S(1)} %get-tuple-element.38), channel_id=1, source_target_pairs={{0,256},{256,0},{1,257},{257,1},{2,258},{258,2},{3,259},{259,3},{4... | collective-permute-start | bytes 110600 | tf_op jit(solution)/shard_map/ppermute | solution.py:303
  101.7 2.9 %collective-permute-done.7.came_ref = f32[72,128]{1,0:T(8,128)S(1)} collective-permute-done((f32[72,128]{1,0:T(8,128)S(1)}, f32[72,128]{1,0:T(8,128)S(1)}, u32[]{:S(2)}, u32[]{:S(2)}) %collective-permute-start.7) | collective-permute-done | bytes 36896 | tf_op jit(solution)/shard_map/ppermute | solution.py:303
  104.5 1.3 %finish.1 = f32[32,64]{1,0:T(8,128)} custom-call(s32[5]{0:T(128)S(1)} %copy-done.7, s32[1]{0:T(128)S(6)} %copy.12.time_ref, f32[72,128]{1,0:T(8,128)S(1)} %get-tuple-element.37.own_ref, f32[72,128]{1,0:T(8,128)S(1)} %collective-permute-done.7.came_ref, f32[32,64]{1,0:T(8,128)S(1)} %bitcast.29), custom_call_target="tpu_custom_call" | custom-call | tf_op jit(solution)/shard_map/finish/pallas_call | solution.py:244
  (30 shorter events, 4.4 us)
Async XLA Ops:
  0.0 6.5 %collective-permute-start = (bf16[192,128]{1,0:T(8,128)(2,1)}, bf16[192,128]{1,0:T(8,128)(2,1)S(1)}, u32[]{:S(2)}, u32[]{:S(2)}) collective-permute-start(bf16[192,128]{1,0:T(8,128)(2,1)} %bitcast.35), channel_id=1, source_target_pairs={{0,0},{8,16},{16,24},{24,8},{256,280},{264,264},{272,256},{280,272... | collective-permute-start | bytes 147464 | tf_op jit(solution)/shard_map/ppermute | solution.py:280
  7.3 7.0 %copy-start.10 = (f32[1,3,3072]{2,0,1:T(1,128)S(1)}, f32[1,3,3072]{2,0,1:T(1,128)}, u32[]{:S(2)}) copy-start(f32[1,3,3072]{2,0,1:T(1,128)} %param.12) | copy-start | bytes 110596
  7.3 20.8 %all-to-all-start = ((bf16[8,192,128]{2,1,0:T(8,128)(2,1)}), bf16[8,192,128]{2,1,0:T(8,128)(2,1)S(1)}, u32[]{:S(2)}, u32[]{:S(2)}) async-start(bf16[8,192,128]{2,1,0:T(8,128)(2,1)} %broadcast_in_dim.6), calls=%async_computation | async-start | bytes 786432 | tf_op jit(solution)/shard_map/all_to_all | solution.py:281
  14.9 2.3 %copy-start.1 = (bf16[1,1,64,3072]{3,2,1,0:T(8,128)(2,1)S(1)}, bf16[1,1,64,3072]{3,2,1,0:T(8,128)(2,1)}, u32[]{:S(2)}) copy-start(bf16[1,1,64,3072]{3,2,1,0:T(8,128)(2,1)} %param.9) | copy-start | bytes 1179652
  14.9 2.3 %copy-start.2 = (bf16[3072,64]{0,1:T(8,128)(2,1)S(1)}, bf16[3072,64]{0,1:T(8,128)(2,1)}, u32[]{:S(2)}) copy-start(bf16[3072,64]{0,1:T(8,128)(2,1)} %param.11) | copy-start | bytes 1179652
  17.2 0.6 copy-start.7
  18.9 0.7 copy-start.3
  19.5 0.7 copy-start.5
  28.1 14.2 %collective-permute-start.1 = (bf16[1536,128]{1,0:T(8,128)(2,1)S(1)}, bf16[1536,128]{1,0:T(8,128)(2,1)S(1)}, u32[]{:S(2)}, u32[]{:S(2)}) collective-permute-start(bf16[1536,128]{1,0:T(8,128)(2,1)S(1)} %bitcast.31), channel_id=1, source_target_pairs={{0,1},{1,0},{2,3},{3,2},{4,5},{5,4},{6,7},{7,6},{16,23},{17,18},{1... | collective-permute-start | bytes 1179656 | tf_op jit(solution)/shard_map/ppermute | solution.py:289
  37.1 24.7 %all-to-all-start.1 = ((bf16[16,3,64,128]{3,2,1,0:T(8,128)(2,1)}), bf16[16,3,64,128]{3,2,1,0:T(8,128)(2,1)S(1)}, u32[]{:S(2)}, u32[]{:S(2)}) async-start(bf16[16,3,64,128]{3,2,1,0:T(8,128)(2,1)} %pack.1), calls=%async_computation.1 | async-start | bytes 1572864 | tf_op jit(solution)/shard_map/all_to_all | solution.py:287
  42.3 19.5 %copy-start.9 = (s32[1,8]{1,0:T(1,128)S(1)}, s32[1,8]{1,0:T(1,128)}, u32[]{:S(2)}) copy-start(s32[1,8]{1,0:T(1,128)} %param.13) | copy-start | bytes 100
  42.3 13.0 %collective-permute-start.2 = (bf16[2,1536,128]{2,1,0:T(8,128)(2,1)S(1)}, bf16[2,1536,128]{2,1,0:T(8,128)(2,1)S(1)}, u32[]{:S(2)}, u32[]{:S(2)}) collective-permute-start(bf16[2,1536,128]{2,1,0:T(8,128)(2,1)S(1)} %pad_maximum_fusion.refs_0_), channel_id=1, source_target_pairs={{0,7},{1,2},{2,1},{3,4},{4,3},{5,6},{6,5},{7,0},{16,17},{17,16},{1... | collective-permute-start | bytes 2359304 | tf_op jit(solution)/shard_map/ppermute | solution.py:292
  44.3 10.9 %collective-permute-start.3 = (bf16[80,1536]{1,0:T(8,128)(2,1)S(1)}, bf16[80,1536]{1,0:T(8,128)(2,1)S(1)}, u32[]{:S(2)}, u32[]{:S(2)}) collective-permute-start(bf16[80,1536]{1,0:T(8,128)(2,1)S(1)} %get-tuple-element.28), channel_id=1, source_target_pairs={{0,256},{256,0},{1,257},{257,1},{2,258},{258,2},{3,259},{259,3},{4... | collective-permute-start | bytes 737288 | tf_op jit(solution)/shard_map/ppermute | solution.py:291
  55.4 17.8 %collective-permute-start.4 = (bf16[2,1536,128]{2,1,0:T(8,128)(2,1)S(1)}, bf16[2,1536,128]{2,1,0:T(8,128)(2,1)S(1)}, u32[]{:S(2)}, u32[]{:S(2)}) collective-permute-start(bf16[2,1536,128]{2,1,0:T(8,128)(2,1)S(1)} %collective-permute-done.2.refs_1_), channel_id=1, source_target_pairs={{0,1},{1,0},{2,3},{3,2},{4,5},{5,4},{6,7},{7,6},{16,23},{17,18},{1... | collective-permute-start | bytes 2359304 | tf_op jit(solution)/shard_map/ppermute | solution.py:295
  64.7 0.8 copy-start
  65.5 23.8 %all-to-all-start.2 = ((bf16[16,128,128]{2,1,0:T(8,128)(2,1)}), bf16[16,128,128]{2,1,0:T(8,128)(2,1)S(1)}, u32[]{:S(2)}, u32[]{:S(2)}) async-start(bf16[16,128,128]{2,1,0:T(8,128)(2,1)} %bitcast.25), calls=%async_computation.2 | async-start | bytes 1048576 | tf_op jit(solution)/shard_map/all_to_all | solution.py:298
  73.2 16.1 %collective-permute-start.5 = (bf16[2,1536,128]{2,1,0:T(8,128)(2,1)S(1)}, bf16[2,1536,128]{2,1,0:T(8,128)(2,1)}, u32[]{:S(2)}, u32[]{:S(2)}) collective-permute-start(bf16[2,1536,128]{2,1,0:T(8,128)(2,1)S(1)} %collective-permute-done.4.refs_2_), channel_id=1, source_target_pairs={{0,7},{1,2},{2,1},{3,4},{4,3},{5,6},{6,5},{7,0},{16,17},{17,16},{1... | collective-permute-start | bytes 2359304 | tf_op jit(solution)/shard_map/ppermute | solution.py:295
  89.3 7.9 %copy-start.4 = (bf16[64,1536]{1,0:T(8,128)(2,1)S(1)}, bf16[64,1536]{1,0:T(8,128)(2,1)}, u32[]{:S(2)}) copy-start(bf16[64,1536]{1,0:T(8,128)(2,1)} %copy-done.3) | copy-start | bytes 589828
  89.3 7.9 %copy-start.6 = (bf16[64,1536]{1,0:T(8,128)(2,1)S(1)}, bf16[64,1536]{1,0:T(8,128)(2,1)}, u32[]{:S(2)}) copy-start(bf16[64,1536]{1,0:T(8,128)(2,1)} %copy-done.5) | copy-start | bytes 589828
  92.2 4.9 %collective-permute-start.6 = (bf16[2,64,1536]{2,1,0:T(8,128)(2,1)S(1)}, bf16[2,64,1536]{2,1,0:T(8,128)(2,1)S(1)}, u32[]{:S(2)}, u32[]{:S(2)}) collective-permute-start(bf16[2,64,1536]{2,1,0:T(8,128)(2,1)S(1)} %get-tuple-element.31), channel_id=1, source_target_pairs={{0,16},{16,0},{1,17},{17,1},{2,18},{18,2},{3,19},{19,3},{4,20},{20... | collective-permute-start | bytes 1179656 | tf_op jit(solution)/shard_map/ppermute | solution.py:301
  97.2 7.4 %copy-start.8 = (f32[1,64,32]{1,2,0:T(8,128)S(1)}, f32[1,64,32]{1,2,0:T(8,128)}, u32[]{:S(2)}) copy-start(f32[1,64,32]{1,2,0:T(8,128)} %param.15) | copy-start | bytes 24580
  98.3 6.2 %collective-permute-start.7 = (f32[72,128]{1,0:T(8,128)S(1)}, f32[72,128]{1,0:T(8,128)S(1)}, u32[]{:S(2)}, u32[]{:S(2)}) collective-permute-start(f32[72,128]{1,0:T(8,128)S(1)} %get-tuple-element.38), channel_id=1, source_target_pairs={{0,256},{256,0},{1,257},{257,1},{2,258},{258,2},{3,259},{259,3},{4... | collective-permute-start | bytes 110600 | tf_op jit(solution)/shard_map/ppermute | solution.py:303

commit v8 on v7

--- a/solution.py
+++ b/solution.py
@@ -79,14 +79,13 @@
         denominator = jnp.sum(weights, axis=1, keepdims=True)
         mixed = jnp.dot(weights.astype(jnp.bfloat16), v, preferred_element_type=jnp.float32)
         result = (mixed / denominator).astype(jnp.bfloat16).reshape(n // 128, 128, HD)
-        out_ref[0, first // 128 : last // 128] = result
-        out_ref[1, first // 128 : last // 128] = result
+        out_ref[first // 128 : last // 128] = result
 
 
 def attend(frames, gathered):
     return pl.pallas_call(
         attend_kernel,
-        out_shape=jax.ShapeDtypeStruct((2, 8, 128, HD), jnp.bfloat16),
+        out_shape=jax.ShapeDtypeStruct((8, 128, HD), jnp.bfloat16),
         in_specs=[spec(SMEM), spec(VMEM)],
         out_specs=spec(VMEM),
         compiler_params=pltpu.CompilerParams(vmem_limit_bytes=32 * 2**20),
@@ -295,7 +294,8 @@
         units.append(lax.ppermute(units[-1], ("k", "z"), CORES[step]))
 
     heads = attend(frames[0], gathered)
-    rows = lax.all_to_all(heads.reshape(16, 128, HD), ("c", "y"), 0, 0, tiled=True).reshape(2, 8, 128, HD)
+    heads = jnp.broadcast_to(heads, (2, 8, 128, HD)).reshape(16, 128, HD)
+    rows = lax.all_to_all(heads, ("c", "y"), 0, 0, tiled=True).reshape(2, 8, 128, HD)
 
     keep, send = project(where, rows, units)
     came = lax.ppermute(send, "k", SWAP)

time: 107 us -> 107 us (level)
    unnamed x23 -> x21, local copies, waits for them, and re-layouts: 2.75 us -> 2.03 us
  transfers between devices with their start and end apart: 11 -> 11, of which waited for: 8 -> 8; matrix products, arithmetic and copies ran while one was open for 1% -> 2% of each run, Pallas kernels for 6% -> 6%
where the time goes in v8:
time: 107 us; the launch traced here: 106 us
  starting transfers between devices  54.7 us (51%)
  waiting for transfers between devices  34.3 us (32%)
  Pallas kernels  11.7 us (11%)
  local copies, waits for them, and re-layouts  4.45 us (4%)
    all_to_all x1, waiting for transfers between devices, shards(): lax.all_to_all(heads, ('c', 'y'), 0, 0, tiled=True).reshape(2, 8, 128, HD)  14.1 us
    ppermute x1, starting transfers between devices, shards(): units = [jnp.stack([unit, lax.ppermute(unit, ('k', 'z'), CORES[0])])]  9.01 us
    ppermute x2, starting transfers between devices, shards(): units.append(lax.ppermute(units[-1], ('k', 'z'), CORES[step]))  8.36 us
    all_to_all x1, waiting for transfers between devices, shards(): lax.all_to_all(jnp.broadcast_to(block, (8, 192, HD)), 'y', 0, 0, tiled=True)  7.68 us
    all_to_all x1, starting transfers between devices, shards(): lax.all_to_all(heads, ('c', 'y'), 0, 0, tiled=True).reshape(2, 8, 128, HD)  7.68 us
    ppermute x1, starting transfers between devices, shards(): other = lax.ppermute(there, 'c', SWAP)  7.02 us
    all_to_all x1, starting transfers between devices, shards(): lax.all_to_all(jnp.broadcast_to(block, (8, 192, HD)), 'y', 0, 0, tiled=True)  6.95 us
    ppermute x1, starting transfers between devices, shards(): block = lax.ppermute(out_weight.T, ('c', 'k', 'l'), spread_pairs())  3.94 us
  transfers between devices with their start and end apart: 11, of which 8 were waited for; matrix products, arithmetic and copies ran while one was open for 2% of the time, Pallas kernels for 6%

profile of v8, /device:TPU:1, one launch (start us, length us, event | category | flops | bytes accessed | tf_op | source)
XLA Modules:
  0.0 106.0 jit_solution(9007202611587971690)
XLA Ops:
  0.0 3.9 %collective-permute-start = (bf16[192,128]{1,0:T(8,128)(2,1)}, bf16[192,128]{1,0:T(8,128)(2,1)S(1)}, u32[]{:S(2)}, u32[]{:S(2)}) collective-permute-start(bf16[192,128]{1,0:T(8,128)(2,1)} %bitcast.35), channel_id=1, source_target_pairs={{0,0},{8,16},{16,24},{24,8},{256,280},{264,264},{272,256},{280,272... | collective-permute-start | bytes 147464 | tf_op jit(solution)/shard_map/ppermute | solution.py:279
  3.9 2.5 %collective-permute-done = bf16[192,128]{1,0:T(8,128)(2,1)S(1)} collective-permute-done((bf16[192,128]{1,0:T(8,128)(2,1)}, bf16[192,128]{1,0:T(8,128)(2,1)S(1)}, u32[]{:S(2)}, u32[]{:S(2)}) %collective-permute-start) | collective-permute-done | bytes 49184 | tf_op jit(solution)/shard_map/ppermute | solution.py:279
  7.3 7.0 %all-to-all-start = ((bf16[8,192,128]{2,1,0:T(8,128)(2,1)}), bf16[8,192,128]{2,1,0:T(8,128)(2,1)S(1)}, u32[]{:S(2)}, u32[]{:S(2)}) async-start(bf16[8,192,128]{2,1,0:T(8,128)(2,1)} %broadcast_in_dim.9), calls=%async_computation | async-start | bytes 786432 | tf_op jit(solution)/shard_map/all_to_all | solution.py:280
  14.9 2.3 %pack.1 = bf16[16,3,64,128]{3,2,1,0:T(8,128)(2,1)} custom-call(s32[5]{0:T(128)} %stack.32.where_ref, bf16[3,64,2048]{2,1,0:T(8,128)(2,1)} %bitcast.33), custom_call_target="tpu_custom_call" | custom-call | tf_op jit(solution)/shard_map/pack/pallas_call | solution.py:42
  17.9 1.1 %prepare.1 = (bf16[64,1536]{1,0:T(8,128)(2,1)S(1)}, bf16[80,1536]{1,0:T(8,128)(2,1)S(1)}, f32[3,1536]{1,0:T(4,128)S(1)}, bf16[64,1536]{1,0:T(8,128)(2,1)S(1)}, f32[64,128]{1,0:T(8,128)S(1)}) custom-call(s32[5]{0:T(128)S(1)} %copy-done.6, bf16[64,3072]{1,0:T(8,128)(2,1)S(1)} %bitcast.25, f32[3,3072]{1,0:T(4,128)S(1)} %bitcast.27, bf16[64,3072]{1,0:T(8,128)(2,1)S(1)} %bitcast.26), custom_call_target="tpu_custom_call" | custom-call | tf_op jit(solution)/shard_map/prepare/pallas_call | solution.py:171
  20.4 7.7 %all-to-all-done = bf16[8,192,128]{2,1,0:T(8,128)(2,1)S(1)} async-done(((bf16[8,192,128]{2,1,0:T(8,128)(2,1)}), bf16[8,192,128]{2,1,0:T(8,128)(2,1)S(1)}, u32[]{:S(2)}, u32[]{:S(2)}) %all-to-all-start) | async-done | bytes 393248 | tf_op jit(solution)/shard_map/all_to_all | solution.py:280
  28.1 9.0 %collective-permute-start.1 = (bf16[1536,128]{1,0:T(8,128)(2,1)S(1)}, bf16[1536,128]{1,0:T(8,128)(2,1)S(1)}, u32[]{:S(2)}, u32[]{:S(2)}) collective-permute-start(bf16[1536,128]{1,0:T(8,128)(2,1)S(1)} %bitcast.31), channel_id=1, source_target_pairs={{0,1},{1,0},{2,3},{3,2},{4,5},{5,4},{6,7},{7,6},{16,23},{17,18},{1... | collective-permute-start | bytes 1179656 | tf_op jit(solution)/shard_map/ppermute | solution.py:288
  37.1 3.5 %all-to-all-start.1 = ((bf16[16,3,64,128]{3,2,1,0:T(8,128)(2,1)}), bf16[16,3,64,128]{3,2,1,0:T(8,128)(2,1)S(1)}, u32[]{:S(2)}, u32[]{:S(2)}) async-start(bf16[16,3,64,128]{3,2,1,0:T(8,128)(2,1)} %pack.1), calls=%async_computation.1 | async-start | bytes 1572864 | tf_op jit(solution)/shard_map/all_to_all | solution.py:286
  40.6 1.6 %collective-permute-done.1 = bf16[1536,128]{1,0:T(8,128)(2,1)S(1)} collective-permute-done((bf16[1536,128]{1,0:T(8,128)(2,1)S(1)}, bf16[1536,128]{1,0:T(8,128)(2,1)S(1)}, u32[]{:S(2)}, u32[]{:S(2)}) %collective-permute-start.1) | collective-permute-done | bytes 393248 | tf_op jit(solution)/shard_map/ppermute | solution.py:288
  42.3 1.9 %collective-permute-start.2 = (bf16[2,1536,128]{2,1,0:T(8,128)(2,1)S(1)}, bf16[2,1536,128]{2,1,0:T(8,128)(2,1)S(1)}, u32[]{:S(2)}, u32[]{:S(2)}) collective-permute-start(bf16[2,1536,128]{2,1,0:T(8,128)(2,1)S(1)} %pad_maximum_fusion.refs_0_), channel_id=1, source_target_pairs={{0,7},{1,2},{2,1},{3,4},{4,3},{5,6},{6,5},{7,0},{16,17},{17,16},{1... | collective-permute-start | bytes 2359304 | tf_op jit(solution)/shard_map/ppermute | solution.py:291
  44.2 7.0 %collective-permute-start.3 = (bf16[80,1536]{1,0:T(8,128)(2,1)S(1)}, bf16[80,1536]{1,0:T(8,128)(2,1)S(1)}, u32[]{:S(2)}, u32[]{:S(2)}) collective-permute-start(bf16[80,1536]{1,0:T(8,128)(2,1)S(1)} %get-tuple-element.28), channel_id=1, source_target_pairs={{0,256},{256,0},{1,257},{257,1},{2,258},{258,2},{3,259},{259,3},{4... | collective-permute-start | bytes 737288 | tf_op jit(solution)/shard_map/ppermute | solution.py:290
  51.3 3.9 %collective-permute-done.3.other_ref = bf16[80,1536]{1,0:T(8,128)(2,1)S(1)} collective-permute-done((bf16[80,1536]{1,0:T(8,128)(2,1)S(1)}, bf16[80,1536]{1,0:T(8,128)(2,1)S(1)}, u32[]{:S(2)}, u32[]{:S(2)}) %collective-permute-start.3) | collective-permute-done | bytes 245792 | tf_op jit(solution)/shard_map/ppermute | solution.py:290
  55.3 6.4 %collective-permute-start.4 = (bf16[2,1536,128]{2,1,0:T(8,128)(2,1)S(1)}, bf16[2,1536,128]{2,1,0:T(8,128)(2,1)S(1)}, u32[]{:S(2)}, u32[]{:S(2)}) collective-permute-start(bf16[2,1536,128]{2,1,0:T(8,128)(2,1)S(1)} %collective-permute-done.2.refs_1_), channel_id=1, source_target_pairs={{0,1},{1,0},{2,3},{3,2},{4,5},{5,4},{6,7},{7,6},{16,23},{17,18},{1... | collective-permute-start | bytes 2359304 | tf_op jit(solution)/shard_map/ppermute | solution.py:294
  61.8 2.9 %attend.1 = bf16[8,128,128]{2,1,0:T(8,128)(2,1)S(1)} custom-call(s32[8]{0:T(128)S(1)} %bitcast.29, bf16[16,3,64,128]{3,2,1,0:T(8,128)(2,1)S(1)} %all-to-all-done.1.x_ref), custom_call_target="tpu_custom_call" | custom-call | flops 540000000 | bytes 2000000 | tf_op jit(solution)/shard_map/attend/pallas_call | solution.py:86
  65.6 7.7 %all-to-all-start.2 = ((bf16[16,128,128]{2,1,0:T(8,128)(2,1)}), bf16[16,128,128]{2,1,0:T(8,128)(2,1)S(1)}, u32[]{:S(2)}, u32[]{:S(2)}) async-start(bf16[16,128,128]{2,1,0:T(8,128)(2,1)} %bitcast.30), calls=%async_computation.2 | async-start | bytes 1048576 | tf_op jit(solution)/shard_map/all_to_all | solution.py:298
  73.3 1.9 %collective-permute-start.5 = (bf16[2,1536,128]{2,1,0:T(8,128)(2,1)S(1)}, bf16[2,1536,128]{2,1,0:T(8,128)(2,1)}, u32[]{:S(2)}, u32[]{:S(2)}) collective-permute-start(bf16[2,1536,128]{2,1,0:T(8,128)(2,1)S(1)} %collective-permute-done.4.refs_2_), channel_id=1, source_target_pairs={{0,7},{1,2},{2,1},{3,4},{4,3},{5,6},{6,5},{7,0},{16,17},{17,16},{1... | collective-permute-start | bytes 2359304 | tf_op jit(solution)/shard_map/ppermute | solution.py:294
  75.2 14.1 %all-to-all-done.2 = bf16[16,128,128]{2,1,0:T(8,128)(2,1)S(1)} async-done(((bf16[16,128,128]{2,1,0:T(8,128)(2,1)}), bf16[16,128,128]{2,1,0:T(8,128)(2,1)S(1)}, u32[]{:S(2)}, u32[]{:S(2)}) %all-to-all-start.2) | async-done | bytes 524320 | tf_op jit(solution)/shard_map/all_to_all | solution.py:298
  89.4 2.9 %project.1 = (f32[2,64,1536]{2,1,0:T(8,128)S(1)}, bf16[2,64,1536]{2,1,0:T(8,128)(2,1)S(1)}) custom-call(s32[5]{0:T(128)S(1)} %copy-done.6, bf16[2,8,128,128]{3,2,1,0:T(8,128)(2,1)S(1)} %bitcast.24, bf16[2,1536,128]{2,1,0:T(8,128)(2,1)S(1)} %pad_maximum_fusion.refs_0_, bf16[2,1536,128]{2,1,0:T(8,128)(2,1)S(1)} %collective-permute-done.2.refs_1_, ...), custom_call_target="tpu_custom_call" | custom-call | flops 810000000 | bytes 5000000 | tf_op jit(solution)/shard_map/project/pallas_call | solution.py:120
  92.3 3.6 %collective-permute-start.6 = (bf16[2,64,1536]{2,1,0:T(8,128)(2,1)S(1)}, bf16[2,64,1536]{2,1,0:T(8,128)(2,1)S(1)}, u32[]{:S(2)}, u32[]{:S(2)}) collective-permute-start(bf16[2,64,1536]{2,1,0:T(8,128)(2,1)S(1)} %get-tuple-element.31), channel_id=1, source_target_pairs={{0,16},{16,0},{1,17},{17,1},{2,18},{18,2},{3,19},{19,3},{4,20},{20... | collective-permute-start | bytes 1179656 | tf_op jit(solution)/shard_map/ppermute | solution.py:301
  95.9 1.3 %collective-permute-done.6.came_ref = bf16[2,64,1536]{2,1,0:T(8,128)(2,1)S(1)} collective-permute-done((bf16[2,64,1536]{2,1,0:T(8,128)(2,1)S(1)}, bf16[2,64,1536]{2,1,0:T(8,128)(2,1)S(1)}, u32[]{:S(2)}, u32[]{:S(2)}) %collective-permute-start.6) | collective-permute-done | bytes 393248 | tf_op jit(solution)/shard_map/ppermute | solution.py:301
  97.3 1.2 %norm.1 = (f32[72,128]{1,0:T(8,128)S(1)}, f32[72,128]{1,0:T(8,128)S(1)}) custom-call(s32[5]{0:T(128)S(1)} %copy-done.6, f32[2,64,1536]{2,1,0:T(8,128)S(1)} %get-tuple-element.30.keep_ref, bf16[2,64,1536]{2,1,0:T(8,128)(2,1)S(1)} %collective-permute-done.6.came_ref, bf16[64,1536]{1,0:T(8,128)(2,1)S(1)} %copy-done.3, ...), custom_call_target="tpu_custom_call" | custom-call | tf_op jit(solution)/shard_map/norm/pallas_call | solution.py:216
  98.4 2.7 %collective-permute-start.7 = (f32[72,128]{1,0:T(8,128)S(1)}, f32[72,128]{1,0:T(8,128)S(1)}, u32[]{:S(2)}, u32[]{:S(2)}) collective-permute-start(f32[72,128]{1,0:T(8,128)S(1)} %get-tuple-element.38), channel_id=1, source_target_pairs={{0,256},{256,0},{1,257},{257,1},{2,258},{258,2},{3,259},{259,3},{4... | collective-permute-start | bytes 110600 | tf_op jit(solution)/shard_map/ppermute | solution.py:303
  101.8 2.9 %collective-permute-done.7.came_ref = f32[72,128]{1,0:T(8,128)S(1)} collective-permute-done((f32[72,128]{1,0:T(8,128)S(1)}, f32[72,128]{1,0:T(8,128)S(1)}, u32[]{:S(2)}, u32[]{:S(2)}) %collective-permute-start.7) | collective-permute-done | bytes 36896 | tf_op jit(solution)/shard_map/ppermute | solution.py:303
  104.7 1.3 %finish.1 = f32[32,64]{1,0:T(8,128)} custom-call(s32[5]{0:T(128)S(1)} %copy-done.6, s32[1]{0:T(128)S(6)} %copy.12.time_ref, f32[72,128]{1,0:T(8,128)S(1)} %get-tuple-element.37.own_ref, f32[72,128]{1,0:T(8,128)S(1)} %collective-permute-done.7.came_ref, f32[32,64]{1,0:T(8,128)S(1)} %bitcast.28), custom_call_target="tpu_custom_call" | custom-call | tf_op jit(solution)/shard_map/finish/pallas_call | solution.py:243
  (29 shorter events, 4.7 us)
Async XLA Ops:
  0.0 6.5 %collective-permute-start = (bf16[192,128]{1,0:T(8,128)(2,1)}, bf16[192,128]{1,0:T(8,128)(2,1)S(1)}, u32[]{:S(2)}, u32[]{:S(2)}) collective-permute-start(bf16[192,128]{1,0:T(8,128)(2,1)} %bitcast.35), channel_id=1, source_target_pairs={{0,0},{8,16},{16,24},{24,8},{256,280},{264,264},{272,256},{280,272... | collective-permute-start | bytes 147464 | tf_op jit(solution)/shard_map/ppermute | solution.py:279
  7.3 7.0 %copy-start.9 = (f32[1,3,3072]{2,0,1:T(1,128)S(1)}, f32[1,3,3072]{2,0,1:T(1,128)}, u32[]{:S(2)}) copy-start(f32[1,3,3072]{2,0,1:T(1,128)} %param.12) | copy-start | bytes 110596
  7.3 20.8 %all-to-all-start = ((bf16[8,192,128]{2,1,0:T(8,128)(2,1)}), bf16[8,192,128]{2,1,0:T(8,128)(2,1)S(1)}, u32[]{:S(2)}, u32[]{:S(2)}) async-start(bf16[8,192,128]{2,1,0:T(8,128)(2,1)} %broadcast_in_dim.9), calls=%async_computation | async-start | bytes 786432 | tf_op jit(solution)/shard_map/all_to_all | solution.py:280
  14.9 2.3 %copy-start = (bf16[1,1,64,3072]{3,2,1,0:T(8,128)(2,1)S(1)}, bf16[1,1,64,3072]{3,2,1,0:T(8,128)(2,1)}, u32[]{:S(2)}) copy-start(bf16[1,1,64,3072]{3,2,1,0:T(8,128)(2,1)} %param.9) | copy-start | bytes 1179652
  14.9 2.3 %copy-start.1 = (bf16[3072,64]{0,1:T(8,128)(2,1)S(1)}, bf16[3072,64]{0,1:T(8,128)(2,1)}, u32[]{:S(2)}) copy-start(bf16[3072,64]{0,1:T(8,128)(2,1)} %param.11) | copy-start | bytes 1179652
  17.3 0.7 copy-start.6
  19.0 0.7 copy-start.2
  19.7 0.7 copy-start.4
  28.1 14.2 %collective-permute-start.1 = (bf16[1536,128]{1,0:T(8,128)(2,1)S(1)}, bf16[1536,128]{1,0:T(8,128)(2,1)S(1)}, u32[]{:S(2)}, u32[]{:S(2)}) collective-permute-start(bf16[1536,128]{1,0:T(8,128)(2,1)S(1)} %bitcast.31), channel_id=1, source_target_pairs={{0,1},{1,0},{2,3},{3,2},{4,5},{5,4},{6,7},{7,6},{16,23},{17,18},{1... | collective-permute-start | bytes 1179656 | tf_op jit(solution)/shard_map/ppermute | solution.py:288
  37.1 24.7 %all-to-all-start.1 = ((bf16[16,3,64,128]{3,2,1,0:T(8,128)(2,1)}), bf16[16,3,64,128]{3,2,1,0:T(8,128)(2,1)S(1)}, u32[]{:S(2)}, u32[]{:S(2)}) async-start(bf16[16,3,64,128]{3,2,1,0:T(8,128)(2,1)} %pack.1), calls=%async_computation.1 | async-start | bytes 1572864 | tf_op jit(solution)/shard_map/all_to_all | solution.py:286
  42.3 19.5 %copy-start.8 = (s32[1,8]{1,0:T(1,128)S(1)}, s32[1,8]{1,0:T(1,128)}, u32[]{:S(2)}) copy-start(s32[1,8]{1,0:T(1,128)} %param.13) | copy-start | bytes 100
  42.3 13.0 %collective-permute-start.2 = (bf16[2,1536,128]{2,1,0:T(8,128)(2,1)S(1)}, bf16[2,1536,128]{2,1,0:T(8,128)(2,1)S(1)}, u32[]{:S(2)}, u32[]{:S(2)}) collective-permute-start(bf16[2,1536,128]{2,1,0:T(8,128)(2,1)S(1)} %pad_maximum_fusion.refs_0_), channel_id=1, source_target_pairs={{0,7},{1,2},{2,1},{3,4},{4,3},{5,6},{6,5},{7,0},{16,17},{17,16},{1... | collective-permute-start | bytes 2359304 | tf_op jit(solution)/shard_map/ppermute | solution.py:291
  44.2 10.9 %collective-permute-start.3 = (bf16[80,1536]{1,0:T(8,128)(2,1)S(1)}, bf16[80,1536]{1,0:T(8,128)(2,1)S(1)}, u32[]{:S(2)}, u32[]{:S(2)}) collective-permute-start(bf16[80,1536]{1,0:T(8,128)(2,1)S(1)} %get-tuple-element.28), channel_id=1, source_target_pairs={{0,256},{256,0},{1,257},{257,1},{2,258},{258,2},{3,259},{259,3},{4... | collective-permute-start | bytes 737288 | tf_op jit(solution)/shard_map/ppermute | solution.py:290
  55.3 18.0 %collective-permute-start.4 = (bf16[2,1536,128]{2,1,0:T(8,128)(2,1)S(1)}, bf16[2,1536,128]{2,1,0:T(8,128)(2,1)S(1)}, u32[]{:S(2)}, u32[]{:S(2)}) collective-permute-start(bf16[2,1536,128]{2,1,0:T(8,128)(2,1)S(1)} %collective-permute-done.2.refs_1_), channel_id=1, source_target_pairs={{0,1},{1,0},{2,3},{3,2},{4,5},{5,4},{6,7},{7,6},{16,23},{17,18},{1... | collective-permute-start | bytes 2359304 | tf_op jit(solution)/shard_map/ppermute | solution.py:294
  65.6 23.8 %all-to-all-start.2 = ((bf16[16,128,128]{2,1,0:T(8,128)(2,1)}), bf16[16,128,128]{2,1,0:T(8,128)(2,1)S(1)}, u32[]{:S(2)}, u32[]{:S(2)}) async-start(bf16[16,128,128]{2,1,0:T(8,128)(2,1)} %bitcast.30), calls=%async_computation.2 | async-start | bytes 1048576 | tf_op jit(solution)/shard_map/all_to_all | solution.py:298
  73.3 16.1 %collective-permute-start.5 = (bf16[2,1536,128]{2,1,0:T(8,128)(2,1)S(1)}, bf16[2,1536,128]{2,1,0:T(8,128)(2,1)}, u32[]{:S(2)}, u32[]{:S(2)}) collective-permute-start(bf16[2,1536,128]{2,1,0:T(8,128)(2,1)S(1)} %collective-permute-done.4.refs_2_), channel_id=1, source_target_pairs={{0,7},{1,2},{2,1},{3,4},{4,3},{5,6},{6,5},{7,0},{16,17},{17,16},{1... | collective-permute-start | bytes 2359304 | tf_op jit(solution)/shard_map/ppermute | solution.py:294
  89.4 7.9 %copy-start.3 = (bf16[64,1536]{1,0:T(8,128)(2,1)S(1)}, bf16[64,1536]{1,0:T(8,128)(2,1)}, u32[]{:S(2)}) copy-start(bf16[64,1536]{1,0:T(8,128)(2,1)} %copy-done.2) | copy-start | bytes 589828
  89.4 7.9 %copy-start.5 = (bf16[64,1536]{1,0:T(8,128)(2,1)S(1)}, bf16[64,1536]{1,0:T(8,128)(2,1)}, u32[]{:S(2)}) copy-start(bf16[64,1536]{1,0:T(8,128)(2,1)} %copy-done.4) | copy-start | bytes 589828
  92.3 4.9 %collective-permute-start.6 = (bf16[2,64,1536]{2,1,0:T(8,128)(2,1)S(1)}, bf16[2,64,1536]{2,1,0:T(8,128)(2,1)S(1)}, u32[]{:S(2)}, u32[]{:S(2)}) collective-permute-start(bf16[2,64,1536]{2,1,0:T(8,128)(2,1)S(1)} %get-tuple-element.31), channel_id=1, source_target_pairs={{0,16},{16,0},{1,17},{17,1},{2,18},{18,2},{3,19},{19,3},{4,20},{20... | collective-permute-start | bytes 1179656 | tf_op jit(solution)/shard_map/ppermute | solution.py:301
  97.3 7.4 %copy-start.7 = (f32[1,64,32]{1,2,0:T(8,128)S(1)}, f32[1,64,32]{1,2,0:T(8,128)}, u32[]{:S(2)}) copy-start(f32[1,64,32]{1,2,0:T(8,128)} %param.15) | copy-start | bytes 24580
  98.4 6.2 %collective-permute-start.7 = (f32[72,128]{1,0:T(8,128)S(1)}, f32[72,128]{1,0:T(8,128)S(1)}, u32[]{:S(2)}, u32[]{:S(2)}) collective-permute-start(f32[72,128]{1,0:T(8,128)S(1)} %get-tuple-element.38), channel_id=1, source_target_pairs={{0,256},{256,0},{1,257},{257,1},{2,258},{258,2},{3,259},{259,3},{4... | collective-permute-start | bytes 110600 | tf_op jit(solution)/shard_map/ppermute | solution.py:303

commit v9 on v7

--- a/solution.py
+++ b/solution.py
@@ -104,12 +104,15 @@
     sign = (2 * lax.rem(z, 2) - 1) * (1 - 2 * core)
     heads = [lax.rem(z + offset * sign + 8, 8) for offset in (0, -1, 1, 2, -2, -3, 3, 4)]
     x = jnp.concatenate([x_ref[:, h].reshape(256, HD) for h in heads], axis=1)
-    copy.wait()
     tile = 384
     for t in range(HALF // tile):
         cols = slice(t * tile, (t + 1) * tile)
-        w = jnp.concatenate([buffers[i // 2][i % 2, cols] for i in range(8)], axis=1)
-        part = lax.dot_general(x, w, NT, preferred_element_type=jnp.float32)
+        w = jnp.concatenate([buffers[i // 2][i % 2, cols] for i in range(6)], axis=1)
+        part = lax.dot_general(x[:, : 6 * HD], w, NT, preferred_element_type=jnp.float32)
+        if t == 0:
+            copy.wait()
+        w = jnp.concatenate([buffer[i, cols] for i in range(2)], axis=1)
+        part = part + lax.dot_general(x[:, 6 * HD :], w, NT, preferred_element_type=jnp.float32)
         for b in range(2):
             low = part[b * 128 : b * 128 + 64]
             high = part[b * 128 + 64 : b * 128 + 128]

time: 107 us -> 107 us (level)
  no operation moved by 1% of the time
where the time goes in v9:
time: 107 us; the launch traced here: 106 us
  starting transfers between devices  54.7 us (51%)
  waiting for transfers between devices  34.4 us (32%)
  Pallas kernels  11.7 us (11%)
  local copies, waits for them, and re-layouts  4.14 us (4%)
    all_to_all x1, waiting for transfers between devices, shards(): lax.all_to_all(heads.reshape(16, 128, HD), ('c', 'y'), 0, 0, tiled=True)  14.2 us
    ppermute x1, starting transfers between devices, shards(): units = [jnp.stack([unit, lax.ppermute(unit, ('k', 'z'), CORES[0])])]  9.01 us
    ppermute x2, starting transfers between devices, shards(): units.append(lax.ppermute(units[-1], ('k', 'z'), CORES[step]))  8.36 us
    all_to_all x1, waiting for transfers between devices, shards(): lax.all_to_all(jnp.broadcast_to(block, (8, 192, HD)), 'y', 0, 0, tiled=True)  7.87 us
    all_to_all x1, starting transfers between devices, shards(): lax.all_to_all(heads.reshape(16, 128, HD), ('c', 'y'), 0, 0, tiled=True)  7.68 us
    ppermute x1, starting transfers between devices, shards(): other = lax.ppermute(there, 'c', SWAP)  7.02 us
    all_to_all x1, starting transfers between devices, shards(): lax.all_to_all(jnp.broadcast_to(block, (8, 192, HD)), 'y', 0, 0, tiled=True)  6.95 us
    ppermute x1, starting transfers between devices, shards(): block = lax.ppermute(out_weight.T, ('c', 'k', 'l'), spread_pairs())  3.94 us
  transfers between devices with their start and end apart: 11, of which 8 were waited for; matrix products, arithmetic and copies ran while one was open for 1% of the time, Pallas kernels for 6%

profile of v9, /device:TPU:1, one launch (start us, length us, event | category | flops | bytes accessed | tf_op | source)
XLA Modules:
  0.0 105.8 jit_solution(10173154357399439238)
XLA Ops:
  0.0 3.9 %collective-permute-start = (bf16[192,128]{1,0:T(8,128)(2,1)}, bf16[192,128]{1,0:T(8,128)(2,1)S(1)}, u32[]{:S(2)}, u32[]{:S(2)}) collective-permute-start(bf16[192,128]{1,0:T(8,128)(2,1)} %bitcast.35), channel_id=1, source_target_pairs={{0,0},{8,16},{16,24},{24,8},{256,280},{264,264},{272,256},{280,272... | collective-permute-start | bytes 147464 | tf_op jit(solution)/shard_map/ppermute | solution.py:283
  3.9 2.5 %collective-permute-done = bf16[192,128]{1,0:T(8,128)(2,1)S(1)} collective-permute-done((bf16[192,128]{1,0:T(8,128)(2,1)}, bf16[192,128]{1,0:T(8,128)(2,1)S(1)}, u32[]{:S(2)}, u32[]{:S(2)}) %collective-permute-start) | collective-permute-done | bytes 49184 | tf_op jit(solution)/shard_map/ppermute | solution.py:283
  7.3 7.0 %all-to-all-start = ((bf16[8,192,128]{2,1,0:T(8,128)(2,1)}), bf16[8,192,128]{2,1,0:T(8,128)(2,1)S(1)}, u32[]{:S(2)}, u32[]{:S(2)}) async-start(bf16[8,192,128]{2,1,0:T(8,128)(2,1)} %broadcast_in_dim.6), calls=%async_computation | async-start | bytes 786432 | tf_op jit(solution)/shard_map/all_to_all | solution.py:284
  14.9 2.3 %pack.1 = bf16[16,3,64,128]{3,2,1,0:T(8,128)(2,1)} custom-call(s32[5]{0:T(128)} %stack.32.where_ref, bf16[3,64,2048]{2,1,0:T(8,128)(2,1)} %bitcast.33), custom_call_target="tpu_custom_call" | custom-call | tf_op jit(solution)/shard_map/pack/pallas_call | solution.py:42
  17.7 1.1 %prepare.1 = (bf16[64,1536]{1,0:T(8,128)(2,1)S(1)}, bf16[80,1536]{1,0:T(8,128)(2,1)S(1)}, f32[3,1536]{1,0:T(4,128)S(1)}, bf16[64,1536]{1,0:T(8,128)(2,1)S(1)}, f32[64,128]{1,0:T(8,128)S(1)}) custom-call(s32[5]{0:T(128)S(1)} %copy-done.7, bf16[64,3072]{1,0:T(8,128)(2,1)S(1)} %bitcast.26, f32[3,3072]{1,0:T(4,128)S(1)} %bitcast.28, bf16[64,3072]{1,0:T(8,128)(2,1)S(1)} %bitcast.27), custom_call_target="tpu_custom_call" | custom-call | tf_op jit(solution)/shard_map/prepare/pallas_call | solution.py:175
  20.2 7.9 %all-to-all-done = bf16[8,192,128]{2,1,0:T(8,128)(2,1)S(1)} async-done(((bf16[8,192,128]{2,1,0:T(8,128)(2,1)}), bf16[8,192,128]{2,1,0:T(8,128)(2,1)S(1)}, u32[]{:S(2)}, u32[]{:S(2)}) %all-to-all-start) | async-done | bytes 393248 | tf_op jit(solution)/shard_map/all_to_all | solution.py:284
  28.1 9.0 %collective-permute-start.1 = (bf16[1536,128]{1,0:T(8,128)(2,1)S(1)}, bf16[1536,128]{1,0:T(8,128)(2,1)S(1)}, u32[]{:S(2)}, u32[]{:S(2)}) collective-permute-start(bf16[1536,128]{1,0:T(8,128)(2,1)S(1)} %bitcast.31), channel_id=1, source_target_pairs={{0,1},{1,0},{2,3},{3,2},{4,5},{5,4},{6,7},{7,6},{16,23},{17,18},{1... | collective-permute-start | bytes 1179656 | tf_op jit(solution)/shard_map/ppermute | solution.py:292
  37.1 3.5 %all-to-all-start.1 = ((bf16[16,3,64,128]{3,2,1,0:T(8,128)(2,1)}), bf16[16,3,64,128]{3,2,1,0:T(8,128)(2,1)S(1)}, u32[]{:S(2)}, u32[]{:S(2)}) async-start(bf16[16,3,64,128]{3,2,1,0:T(8,128)(2,1)} %pack.1), calls=%async_computation.1 | async-start | bytes 1572864 | tf_op jit(solution)/shard_map/all_to_all | solution.py:290
  40.6 1.6 %collective-permute-done.1 = bf16[1536,128]{1,0:T(8,128)(2,1)S(1)} collective-permute-done((bf16[1536,128]{1,0:T(8,128)(2,1)S(1)}, bf16[1536,128]{1,0:T(8,128)(2,1)S(1)}, u32[]{:S(2)}, u32[]{:S(2)}) %collective-permute-start.1) | collective-permute-done | bytes 393248 | tf_op jit(solution)/shard_map/ppermute | solution.py:292
  42.3 1.9 %collective-permute-start.2 = (bf16[2,1536,128]{2,1,0:T(8,128)(2,1)S(1)}, bf16[2,1536,128]{2,1,0:T(8,128)(2,1)S(1)}, u32[]{:S(2)}, u32[]{:S(2)}) collective-permute-start(bf16[2,1536,128]{2,1,0:T(8,128)(2,1)S(1)} %pad_maximum_fusion.refs_0_), channel_id=1, source_target_pairs={{0,7},{1,2},{2,1},{3,4},{4,3},{5,6},{6,5},{7,0},{16,17},{17,16},{1... | collective-permute-start | bytes 2359304 | tf_op jit(solution)/shard_map/ppermute | solution.py:295
  44.3 7.0 %collective-permute-start.3 = (bf16[80,1536]{1,0:T(8,128)(2,1)S(1)}, bf16[80,1536]{1,0:T(8,128)(2,1)S(1)}, u32[]{:S(2)}, u32[]{:S(2)}) collective-permute-start(bf16[80,1536]{1,0:T(8,128)(2,1)S(1)} %get-tuple-element.28), channel_id=1, source_target_pairs={{0,256},{256,0},{1,257},{257,1},{2,258},{258,2},{3,259},{259,3},{4... | collective-permute-start | bytes 737288 | tf_op jit(solution)/shard_map/ppermute | solution.py:294
  51.3 3.9 %collective-permute-done.3.other_ref = bf16[80,1536]{1,0:T(8,128)(2,1)S(1)} collective-permute-done((bf16[80,1536]{1,0:T(8,128)(2,1)S(1)}, bf16[80,1536]{1,0:T(8,128)(2,1)S(1)}, u32[]{:S(2)}, u32[]{:S(2)}) %collective-permute-start.3) | collective-permute-done | bytes 245792 | tf_op jit(solution)/shard_map/ppermute | solution.py:294
  55.4 6.4 %collective-permute-start.4 = (bf16[2,1536,128]{2,1,0:T(8,128)(2,1)S(1)}, bf16[2,1536,128]{2,1,0:T(8,128)(2,1)S(1)}, u32[]{:S(2)}, u32[]{:S(2)}) collective-permute-start(bf16[2,1536,128]{2,1,0:T(8,128)(2,1)S(1)} %collective-permute-done.2.refs_1_), channel_id=1, source_target_pairs={{0,1},{1,0},{2,3},{3,2},{4,5},{5,4},{6,7},{7,6},{16,23},{17,18},{1... | collective-permute-start | bytes 2359304 | tf_op jit(solution)/shard_map/ppermute | solution.py:298
  61.8 2.9 %attend.1 = bf16[2,8,128,128]{3,2,1,0:T(8,128)(2,1)S(1)} custom-call(s32[8]{0:T(128)S(1)} %bitcast.30, bf16[16,3,64,128]{3,2,1,0:T(8,128)(2,1)S(1)} %all-to-all-done.1.x_ref), custom_call_target="tpu_custom_call" | custom-call | flops 540000000 | bytes 2000000 | tf_op jit(solution)/shard_map/attend/pallas_call | solution.py:87
  65.5 7.7 %all-to-all-start.2 = ((bf16[16,128,128]{2,1,0:T(8,128)(2,1)}), bf16[16,128,128]{2,1,0:T(8,128)(2,1)S(1)}, u32[]{:S(2)}, u32[]{:S(2)}) async-start(bf16[16,128,128]{2,1,0:T(8,128)(2,1)} %bitcast.25), calls=%async_computation.2 | async-start | bytes 1048576 | tf_op jit(solution)/shard_map/all_to_all | solution.py:301
  73.2 1.9 %collective-permute-start.5 = (bf16[2,1536,128]{2,1,0:T(8,128)(2,1)S(1)}, bf16[2,1536,128]{2,1,0:T(8,128)(2,1)}, u32[]{:S(2)}, u32[]{:S(2)}) collective-permute-start(bf16[2,1536,128]{2,1,0:T(8,128)(2,1)S(1)} %collective-permute-done.4.refs_2_), channel_id=1, source_target_pairs={{0,7},{1,2},{2,1},{3,4},{4,3},{5,6},{6,5},{7,0},{16,17},{17,16},{1... | collective-permute-start | bytes 2359304 | tf_op jit(solution)/shard_map/ppermute | solution.py:298
  75.1 14.2 %all-to-all-done.2 = bf16[16,128,128]{2,1,0:T(8,128)(2,1)S(1)} async-done(((bf16[16,128,128]{2,1,0:T(8,128)(2,1)}), bf16[16,128,128]{2,1,0:T(8,128)(2,1)S(1)}, u32[]{:S(2)}, u32[]{:S(2)}) %all-to-all-start.2) | async-done | bytes 524320 | tf_op jit(solution)/shard_map/all_to_all | solution.py:301
  89.3 2.9 %project.1 = (f32[2,64,1536]{2,1,0:T(8,128)S(1)}, bf16[2,64,1536]{2,1,0:T(8,128)(2,1)S(1)}) custom-call(s32[5]{0:T(128)S(1)} %copy-done.7, bf16[2,8,128,128]{3,2,1,0:T(8,128)(2,1)S(1)} %bitcast.24, bf16[2,1536,128]{2,1,0:T(8,128)(2,1)S(1)} %pad_maximum_fusion.refs_0_, bf16[2,1536,128]{2,1,0:T(8,128)(2,1)S(1)} %collective-permute-done.2.refs_1_, ...), custom_call_target="tpu_custom_call" | custom-call | flops 810000000 | bytes 5000000 | tf_op jit(solution)/shard_map/project/pallas_call | solution.py:124
  92.2 3.6 %collective-permute-start.6 = (bf16[2,64,1536]{2,1,0:T(8,128)(2,1)S(1)}, bf16[2,64,1536]{2,1,0:T(8,128)(2,1)S(1)}, u32[]{:S(2)}, u32[]{:S(2)}) collective-permute-start(bf16[2,64,1536]{2,1,0:T(8,128)(2,1)S(1)} %get-tuple-element.31), channel_id=1, source_target_pairs={{0,16},{16,0},{1,17},{17,1},{2,18},{18,2},{3,19},{19,3},{4,20},{20... | collective-permute-start | bytes 1179656 | tf_op jit(solution)/shard_map/ppermute | solution.py:304
  95.8 1.3 %collective-permute-done.6.came_ref = bf16[2,64,1536]{2,1,0:T(8,128)(2,1)S(1)} collective-permute-done((bf16[2,64,1536]{2,1,0:T(8,128)(2,1)S(1)}, bf16[2,64,1536]{2,1,0:T(8,128)(2,1)S(1)}, u32[]{:S(2)}, u32[]{:S(2)}) %collective-permute-start.6) | collective-permute-done | bytes 393248 | tf_op jit(solution)/shard_map/ppermute | solution.py:304
  97.2 1.2 %norm.1 = (f32[72,128]{1,0:T(8,128)S(1)}, f32[72,128]{1,0:T(8,128)S(1)}) custom-call(s32[5]{0:T(128)S(1)} %copy-done.7, f32[2,64,1536]{2,1,0:T(8,128)S(1)} %get-tuple-element.30.keep_ref, bf16[2,64,1536]{2,1,0:T(8,128)(2,1)S(1)} %collective-permute-done.6.came_ref, bf16[64,1536]{1,0:T(8,128)(2,1)S(1)} %copy-done.4, ...), custom_call_target="tpu_custom_call" | custom-call | tf_op jit(solution)/shard_map/norm/pallas_call | solution.py:220
  98.3 2.7 %collective-permute-start.7 = (f32[72,128]{1,0:T(8,128)S(1)}, f32[72,128]{1,0:T(8,128)S(1)}, u32[]{:S(2)}, u32[]{:S(2)}) collective-permute-start(f32[72,128]{1,0:T(8,128)S(1)} %get-tuple-element.38), channel_id=1, source_target_pairs={{0,256},{256,0},{1,257},{257,1},{2,258},{258,2},{3,259},{259,3},{4... | collective-permute-start | bytes 110600 | tf_op jit(solution)/shard_map/ppermute | solution.py:306
  101.7 2.9 %collective-permute-done.7.came_ref = f32[72,128]{1,0:T(8,128)S(1)} collective-permute-done((f32[72,128]{1,0:T(8,128)S(1)}, f32[72,128]{1,0:T(8,128)S(1)}, u32[]{:S(2)}, u32[]{:S(2)}) %collective-permute-start.7) | collective-permute-done | bytes 36896 | tf_op jit(solution)/shard_map/ppermute | solution.py:306
  104.5 1.3 %finish.1 = f32[32,64]{1,0:T(8,128)} custom-call(s32[5]{0:T(128)S(1)} %copy-done.7, s32[1]{0:T(128)S(6)} %copy.12.time_ref, f32[72,128]{1,0:T(8,128)S(1)} %get-tuple-element.37.own_ref, f32[72,128]{1,0:T(8,128)S(1)} %collective-permute-done.7.came_ref, f32[32,64]{1,0:T(8,128)S(1)} %bitcast.29), custom_call_target="tpu_custom_call" | custom-call | tf_op jit(solution)/shard_map/finish/pallas_call | solution.py:247
  (30 shorter events, 4.4 us)
Async XLA Ops:
  0.0 6.5 %collective-permute-start = (bf16[192,128]{1,0:T(8,128)(2,1)}, bf16[192,128]{1,0:T(8,128)(2,1)S(1)}, u32[]{:S(2)}, u32[]{:S(2)}) collective-permute-start(bf16[192,128]{1,0:T(8,128)(2,1)} %bitcast.35), channel_id=1, source_target_pairs={{0,0},{8,16},{16,24},{24,8},{256,280},{264,264},{272,256},{280,272... | collective-permute-start | bytes 147464 | tf_op jit(solution)/shard_map/ppermute | solution.py:283
  7.3 7.0 %copy-start.10 = (f32[1,3,3072]{2,0,1:T(1,128)S(1)}, f32[1,3,3072]{2,0,1:T(1,128)}, u32[]{:S(2)}) copy-start(f32[1,3,3072]{2,0,1:T(1,128)} %param.12) | copy-start | bytes 110596
  7.3 20.8 %all-to-all-start = ((bf16[8,192,128]{2,1,0:T(8,128)(2,1)}), bf16[8,192,128]{2,1,0:T(8,128)(2,1)S(1)}, u32[]{:S(2)}, u32[]{:S(2)}) async-start(bf16[8,192,128]{2,1,0:T(8,128)(2,1)} %broadcast_in_dim.6), calls=%async_computation | async-start | bytes 786432 | tf_op jit(solution)/shard_map/all_to_all | solution.py:284
  14.9 2.3 %copy-start.1 = (bf16[1,1,64,3072]{3,2,1,0:T(8,128)(2,1)S(1)}, bf16[1,1,64,3072]{3,2,1,0:T(8,128)(2,1)}, u32[]{:S(2)}) copy-start(bf16[1,1,64,3072]{3,2,1,0:T(8,128)(2,1)} %param.9) | copy-start | bytes 1179652
  14.9 2.3 %copy-start.2 = (bf16[3072,64]{0,1:T(8,128)(2,1)S(1)}, bf16[3072,64]{0,1:T(8,128)(2,1)}, u32[]{:S(2)}) copy-start(bf16[3072,64]{0,1:T(8,128)(2,1)} %param.11) | copy-start | bytes 1179652
  17.2 0.6 copy-start.7
  18.9 0.7 copy-start.3
  19.5 0.7 copy-start.5
  28.1 14.2 %collective-permute-start.1 = (bf16[1536,128]{1,0:T(8,128)(2,1)S(1)}, bf16[1536,128]{1,0:T(8,128)(2,1)S(1)}, u32[]{:S(2)}, u32[]{:S(2)}) collective-permute-start(bf16[1536,128]{1,0:T(8,128)(2,1)S(1)} %bitcast.31), channel_id=1, source_target_pairs={{0,1},{1,0},{2,3},{3,2},{4,5},{5,4},{6,7},{7,6},{16,23},{17,18},{1... | collective-permute-start | bytes 1179656 | tf_op jit(solution)/shard_map/ppermute | solution.py:292
  37.1 24.7 %all-to-all-start.1 = ((bf16[16,3,64,128]{3,2,1,0:T(8,128)(2,1)}), bf16[16,3,64,128]{3,2,1,0:T(8,128)(2,1)S(1)}, u32[]{:S(2)}, u32[]{:S(2)}) async-start(bf16[16,3,64,128]{3,2,1,0:T(8,128)(2,1)} %pack.1), calls=%async_computation.1 | async-start | bytes 1572864 | tf_op jit(solution)/shard_map/all_to_all | solution.py:290
  42.3 19.5 %copy-start.9 = (s32[1,8]{1,0:T(1,128)S(1)}, s32[1,8]{1,0:T(1,128)}, u32[]{:S(2)}) copy-start(s32[1,8]{1,0:T(1,128)} %param.13) | copy-start | bytes 100
  42.3 13.0 %collective-permute-start.2 = (bf16[2,1536,128]{2,1,0:T(8,128)(2,1)S(1)}, bf16[2,1536,128]{2,1,0:T(8,128)(2,1)S(1)}, u32[]{:S(2)}, u32[]{:S(2)}) collective-permute-start(bf16[2,1536,128]{2,1,0:T(8,128)(2,1)S(1)} %pad_maximum_fusion.refs_0_), channel_id=1, source_target_pairs={{0,7},{1,2},{2,1},{3,4},{4,3},{5,6},{6,5},{7,0},{16,17},{17,16},{1... | collective-permute-start | bytes 2359304 | tf_op jit(solution)/shard_map/ppermute | solution.py:295
  44.3 10.9 %collective-permute-start.3 = (bf16[80,1536]{1,0:T(8,128)(2,1)S(1)}, bf16[80,1536]{1,0:T(8,128)(2,1)S(1)}, u32[]{:S(2)}, u32[]{:S(2)}) collective-permute-start(bf16[80,1536]{1,0:T(8,128)(2,1)S(1)} %get-tuple-element.28), channel_id=1, source_target_pairs={{0,256},{256,0},{1,257},{257,1},{2,258},{258,2},{3,259},{259,3},{4... | collective-permute-start | bytes 737288 | tf_op jit(solution)/shard_map/ppermute | solution.py:294
  55.4 17.8 %collective-permute-start.4 = (bf16[2,1536,128]{2,1,0:T(8,128)(2,1)S(1)}, bf16[2,1536,128]{2,1,0:T(8,128)(2,1)S(1)}, u32[]{:S(2)}, u32[]{:S(2)}) collective-permute-start(bf16[2,1536,128]{2,1,0:T(8,128)(2,1)S(1)} %collective-permute-done.2.refs_1_), channel_id=1, source_target_pairs={{0,1},{1,0},{2,3},{3,2},{4,5},{5,4},{6,7},{7,6},{16,23},{17,18},{1... | collective-permute-start | bytes 2359304 | tf_op jit(solution)/shard_map/ppermute | solution.py:298
  64.7 0.8 copy-start
  65.5 23.8 %all-to-all-start.2 = ((bf16[16,128,128]{2,1,0:T(8,128)(2,1)}), bf16[16,128,128]{2,1,0:T(8,128)(2,1)S(1)}, u32[]{:S(2)}, u32[]{:S(2)}) async-start(bf16[16,128,128]{2,1,0:T(8,128)(2,1)} %bitcast.25), calls=%async_computation.2 | async-start | bytes 1048576 | tf_op jit(solution)/shard_map/all_to_all | solution.py:301
  73.2 16.1 %collective-permute-start.5 = (bf16[2,1536,128]{2,1,0:T(8,128)(2,1)S(1)}, bf16[2,1536,128]{2,1,0:T(8,128)(2,1)}, u32[]{:S(2)}, u32[]{:S(2)}) collective-permute-start(bf16[2,1536,128]{2,1,0:T(8,128)(2,1)S(1)} %collective-permute-done.4.refs_2_), channel_id=1, source_target_pairs={{0,7},{1,2},{2,1},{3,4},{4,3},{5,6},{6,5},{7,0},{16,17},{17,16},{1... | collective-permute-start | bytes 2359304 | tf_op jit(solution)/shard_map/ppermute | solution.py:298
  89.3 7.9 %copy-start.4 = (bf16[64,1536]{1,0:T(8,128)(2,1)S(1)}, bf16[64,1536]{1,0:T(8,128)(2,1)}, u32[]{:S(2)}) copy-start(bf16[64,1536]{1,0:T(8,128)(2,1)} %copy-done.3) | copy-start | bytes 589828
  89.3 7.9 %copy-start.6 = (bf16[64,1536]{1,0:T(8,128)(2,1)S(1)}, bf16[64,1536]{1,0:T(8,128)(2,1)}, u32[]{:S(2)}) copy-start(bf16[64,1536]{1,0:T(8,128)(2,1)} %copy-done.5) | copy-start | bytes 589828
  92.2 4.9 %collective-permute-start.6 = (bf16[2,64,1536]{2,1,0:T(8,128)(2,1)S(1)}, bf16[2,64,1536]{2,1,0:T(8,128)(2,1)S(1)}, u32[]{:S(2)}, u32[]{:S(2)}) collective-permute-start(bf16[2,64,1536]{2,1,0:T(8,128)(2,1)S(1)} %get-tuple-element.31), channel_id=1, source_target_pairs={{0,16},{16,0},{1,17},{17,1},{2,18},{18,2},{3,19},{19,3},{4,20},{20... | collective-permute-start | bytes 1179656 | tf_op jit(solution)/shard_map/ppermute | solution.py:304
  97.2 7.4 %copy-start.8 = (f32[1,64,32]{1,2,0:T(8,128)S(1)}, f32[1,64,32]{1,2,0:T(8,128)}, u32[]{:S(2)}) copy-start(f32[1,64,32]{1,2,0:T(8,128)} %param.15) | copy-start | bytes 24580
  98.3 6.2 %collective-permute-start.7 = (f32[72,128]{1,0:T(8,128)S(1)}, f32[72,128]{1,0:T(8,128)S(1)}, u32[]{:S(2)}, u32[]{:S(2)}) collective-permute-start(f32[72,128]{1,0:T(8,128)S(1)} %get-tuple-element.38), channel_id=1, source_target_pairs={{0,256},{256,0},{1,257},{257,1},{2,258},{258,2},{3,259},{259,3},{4... | collective-permute-start | bytes 110600 | tf_op jit(solution)/shard_map/ppermute | solution.py:306
